TPU v7x, 32 devices: a whole 2x2x4 slice. The times are simulated.
32 devices in a mesh: emb: 16 (over z, y, core), seq: 2 (over x).
Axes of the slice: x: 2, y: 2, z: 4, core: 2. Of those that a mesh axis runs over, the one named last changes fastest.
Arguments:
- table: bfloat16 [8192, 256], P('emb'), may hold values from -6 to 6
- owner: int32 [64, 512, 1], P(('emb', 'seq')), may hold values from 0 to 15; in each aligned block of 512 rows (0 to 511, 512 to 1023, ..., all dimensions but the last counted through in order) at most 64 rows name the same one
- row: int32 [64, 512], P(('emb', 'seq')), may hold values from 0 to 511
- conv_weight: float32 [4, 768, 256], replicated, may hold values from -0.21875 to 0.21875
- gain: float32 [4, 256], replicated, may hold values from 0.1 to 1.9
- upstream: bfloat16 [64, 512, 256], P(('emb', 'seq')), may hold values from -6 to 6
Outputs:
- weight_grad: float32 [4, 768, 256], replicated
- gain_grad: float32 [4, 256], replicated
- table_grad: float32 [8192, 256], P('emb')
Inputs may be any that keep to these rules, and one draw needn't show every extreme that they name: Within the positions of one micro-batch on one device (aligned blocks of 512 positions, in sequence order), at most 64 have the same owner.
All inputs are finite; a program needn't handle non-finite values.
Results may differ from a plain program's by a relative error of at most 0.022.
Values may be sent and summed in bfloat16 or wider, within the bound.
No kernel may reach another device: no remote copies, remote signals or barrier semaphores. Data moves between devices by JAX's collectives and lax.ppermute only.
A program may use at most 64 MiB of HBM per device.

v0:
```python
import jax
import jax.numpy as jnp
from jax import lax
from jax.sharding import PartitionSpec as P

MB = 2


def shift_back(values, steps):
    return jnp.pad(values, ((0, 0), (steps, 0), (0, 0)))[:, : values.shape[1]]


def shift_ahead(values, steps):
    return jnp.pad(values, ((0, 0), (0, steps), (0, 0)))[:, steps:]


def gelu_tanh(values):
    return jax.nn.gelu(values, approximate=True)


def forward_block(state, weight, gain_row, dilation):
    width = state.shape[-1]
    statef = state.astype(jnp.float32)
    centred = statef - jnp.mean(statef, axis=-1, keepdims=True)
    inverse = lax.rsqrt(jnp.mean(centred * centred, axis=-1, keepdims=True) + 1e-05)
    normed = centred * inverse
    hidden = (normed * gain_row).astype(jnp.bfloat16)
    stacked = jnp.concatenate(
        [hidden, shift_back(hidden, dilation), shift_back(hidden, 2 * dilation)], axis=-1
    )
    flat = stacked.reshape(-1, 3 * width)
    conv = jnp.dot(flat, weight.astype(jnp.bfloat16), preferred_element_type=jnp.float32).reshape(
        state.shape
    )
    result = (statef + gelu_tanh(conv)).astype(jnp.bfloat16)
    return (result, (flat, normed, inverse, conv))


def backward_block(cotangent, saved, weight, gain_row, dilation):
    flat, normed, inverse, conv = saved
    width = cotangent.shape[-1]
    slope = jax.jvp(gelu_tanh, (conv,), (jnp.ones_like(conv),))[1]
    cotf = cotangent.astype(jnp.float32)
    dconv = (cotf * slope).astype(jnp.bfloat16).reshape(-1, width)
    dweight = lax.dot_general(
        flat, dconv, (((0,), (0,)), ((), ())), preferred_element_type=jnp.float32
    )
    dflat = jnp.dot(dconv, weight.astype(jnp.bfloat16).T, preferred_element_type=jnp.float32)
    dflat = dflat.reshape(cotangent.shape[:-1] + (3 * width,))
    dhidden = dflat[..., :width] + shift_ahead(dflat[..., width : 2 * width], dilation)
    dhidden = dhidden + shift_ahead(dflat[..., 2 * width :], 2 * dilation)
    dgain = jnp.sum(dhidden * normed, axis=(0, 1))
    dnorm = dhidden * gain_row
    dstate = inverse * (
        dnorm
        - jnp.mean(dnorm, axis=-1, keepdims=True)
        - normed * jnp.mean(dnorm * normed, axis=-1, keepdims=True)
    )
    return ((cotf + dstate).astype(jnp.bfloat16), dweight, dgain)


def run_stack(embed, weights, gains, cotangent):
    state = embed
    saves = []
    for layer in range(weights.shape[0]):
        state, saved = forward_block(state, weights[layer], gains[layer], 2**layer)
        saves.append(saved)
    weight_parts = []
    gain_parts = []
    for layer in reversed(range(weights.shape[0])):
        cotangent, dweight, dgain = backward_block(
            cotangent, saves[layer], weights[layer], gains[layer], 2**layer
        )
        weight_parts.insert(0, dweight)
        gain_parts.insert(0, dgain)
    return (cotangent, jnp.stack(weight_parts), jnp.stack(gain_parts))


def body(table, owner, row, conv_weight, gain, upstream):
    shards = lax.axis_size("emb")
    seqs_dev, length = row.shape
    slab, width = table.shape
    seq_mb = seqs_dev // MB
    count = seq_mb * length
    capacity = max(2, 2 * count // shards)
    owners = owner.reshape(MB, count)
    marks = (owners[:, :, None] == jnp.arange(shards, dtype=jnp.int32)[None, None, :]).astype(
        jnp.int32
    )
    slots = jnp.sum((jnp.cumsum(marks, axis=1) - 1) * marks, axis=2)
    batch_ids = jnp.broadcast_to(jnp.arange(MB, dtype=jnp.int32)[:, None], (MB, count))
    requests = jnp.zeros((shards, MB, capacity), jnp.int32).at[owners, batch_ids, slots].set(row)
    cotangents = upstream.reshape(MB, seq_mb, length, width)
    weight_total = jnp.zeros(conv_weight.shape, jnp.float32)
    gain_total = jnp.zeros(gain.shape, jnp.float32)
    table_part = jnp.zeros((slab, width), jnp.float32)
    for batch in range(MB):
        arrived_ids = lax.all_to_all(
            requests[:, batch], "emb", split_axis=0, concat_axis=0, tiled=True
        )
        served = table[arrived_ids]
        fetched = lax.all_to_all(served, "emb", split_axis=0, concat_axis=0, tiled=True)
        embed = fetched[owners[batch], slots[batch]].reshape(seq_mb, length, width)
        d_embed, dweight, dgain = run_stack(embed, conv_weight, gain, cotangents[batch])
        weight_total = weight_total + dweight
        gain_total = gain_total + dgain
        outgoing = (
            jnp.zeros((shards, capacity, width), jnp.bfloat16)
            .at[owners[batch], slots[batch]]
            .set(d_embed.reshape(count, width))
        )
        returned = lax.all_to_all(outgoing, "emb", split_axis=0, concat_axis=0, tiled=True)
        table_part = table_part.at[arrived_ids.reshape(-1)].add(
            returned.reshape(-1, width).astype(jnp.float32)
        )
    scale = float(seqs_dev * length * shards * lax.axis_size("seq")) ** (-0.5)
    table_grad = lax.psum(table_part.astype(jnp.bfloat16), "seq").astype(jnp.float32)
    weight_sum, gain_sum = lax.psum((weight_total, gain_total), ("emb", "seq"))
    return (weight_sum * scale, gain_sum * scale, table_grad)


def solution(mesh):
    in_specs = (
        P("emb", None),
        P(("emb", "seq"), None, None),
        P(("emb", "seq"), None),
        P(),
        P(),
        P(("emb", "seq"), None, None),
    )
    out_specs = (P(), P(), P("emb", None))
    return jax.shard_map(body, mesh=mesh, in_specs=in_specs, out_specs=out_specs, check_vma=False)
```

profile of v0, /device:TPU:0, one launch (start us, length us, event | category | flops | bytes accessed | tf_op | source)
XLA Modules:
  0.0 445.8 jit_solution(6143366590969808227)
XLA Ops:
  7.2 0.7 copy.19
  8.6 2.3 reduce-window.6
  11.3 0.7 compare_select_fusion.2
  12.0 0.8 and_reduce_fusion
  12.8 0.7 multiply_reduce_fusion.8
  14.3 4.3 scatter_custom_fusion.4
  19.3 13.6 %all_to_all.38 = s32[16,1,64]{2,1,0:T(1,128)S(1)} all-to-all(s32[16,1,64]{2,1,0:T(1,128)S(1)} %get-tuple-element.88), channel_id=1, replica_groups=mesh['emb'=16,'seq'=2] {'emb'}, dimensions={0} | all-to-all | bytes 8192 | tf_op jit(solution)/shard_map/all_to_all | solution.py:98
  32.9 3.5 all-to-all-start
  36.4 5.0 %gather_fusion.2 = bf16[1024,256]{1,0:T(8,128)(2,1)} fusion(bf16[512,256]{1,0:T(8,128)(2,1)S(1)} %copy-done, s32[1024]{0:T(1024)S(1)} %broadcast_clamp_fusion), kind=kCustom, calls=%fused_computation.2 | custom fusion | bytes 1052672 | tf_op jit(solution)/shard_map/gather | solution.py:101
  41.4 1.2 all-to-all-done
  42.6 4.7 %all-to-all-start.3 = ((bf16[16,64,256]{2,1,0:T(8,128)(2,1)}), bf16[16,64,256]{2,1,0:T(8,128)(2,1)S(1)}, u32[]{:S(2)}, u32[]{:S(2)}) async-start(bf16[16,64,256]{2,1,0:T(8,128)(2,1)} %bitcast.44), calls=%async_computation.3 | async-start | bytes 1048576 | tf_op jit(solution)/shard_map/all_to_all | solution.py:102
  47.4 2.1 convert.12
  49.6 5.0 %gather_fusion = bf16[1024,256]{1,0:T(8,128)(2,1)} fusion(bf16[512,256]{1,0:T(8,128)(2,1)S(1)} %copy-done, s32[1024]{0:T(1024)S(1)} %broadcast_clamp_fusion.1), kind=kCustom, calls=%fused_computation | custom fusion | bytes 1052672 | tf_op jit(solution)/shard_map/gather | solution.py:101
  55.9 6.0 %all-to-all-done.3 = bf16[16,64,256]{2,1,0:T(8,128)(2,1)S(1)} async-done(((bf16[16,64,256]{2,1,0:T(8,128)(2,1)}), bf16[16,64,256]{2,1,0:T(8,128)(2,1)S(1)}, u32[]{:S(2)}, u32[]{:S(2)}) %all-to-all-start.3) | async-done | bytes 524320 | tf_op jit(solution)/shard_map/all_to_all | solution.py:102
  61.9 4.3 all-to-all-start.1
  66.9 3.2 gather_fusion.3
  70.5 10.1 %all-to-all-done.1 = bf16[16,64,256]{2,1,0:T(8,128)(2,1)S(1)} async-done(((bf16[16,64,256]{2,1,0:T(8,128)(2,1)}), bf16[16,64,256]{2,1,0:T(8,128)(2,1)S(1)}, u32[]{:S(2)}, u32[]{:S(2)}) %all-to-all-start.1) | async-done | bytes 524320 | tf_op jit(solution)/shard_map/all_to_all | solution.py:102
  80.6 3.2 gather_fusion.1
  92.7 0.9 copy-done.43
  95.7 0.7 copy-done.54
  96.9 0.7 fusion.49
  97.6 1.1 fusion.113
  100.7 0.9 fusion.53
  104.0 0.9 fusion.51
  106.9 0.8 fusion.235
  107.8 0.8 fusion.267
  108.6 0.9 broadcast.920.clone
  109.4 57.3 %scatter_fusion = bf16[16,64,256]{2,1,0:T(8,128)(2,1)} fusion(bf16[16,64,256]{2,1,0:T(8,128)(2,1)} %broadcast.920.clone, s32[512]{0:T(512)S(1)} %bitcast.509, bf16[512,256]{1,0:T(8,128)(2,1)S(1)} %get-tuple-element.97), kind=kCustom, calls=%fused_computation.4 | custom fusion | bytes 790528 | tf_op jit(solution)/shard_map/scatter | solution.py:110
  166.7 4.3 all-to-all-start.4
  171.0 0.9 broadcast.920.clone.1
  171.9 57.1 %scatter_fusion.1 = bf16[16,64,256]{2,1,0:T(8,128)(2,1)} fusion(bf16[16,64,256]{2,1,0:T(8,128)(2,1)} %broadcast.920.clone.1, s32[512]{0:T(512)S(1)} %bitcast.508, bf16[512,256]{1,0:T(8,128)(2,1)S(1)} %get-tuple-element.96), kind=kCustom, calls=%fused_computation.6 | custom fusion | bytes 790528 | tf_op jit(solution)/shard_map/scatter | solution.py:110
  229.1 2.4 convolution_bitcast_fusion.12
  231.6 1.6 convolution_bitcast_fusion.13
  233.2 1.6 convolution_bitcast_fusion.14
  234.8 1.6 convolution_bitcast_fusion.15
  236.4 6.5 %all-to-all-start.5 = ((bf16[16,64,256]{2,1,0:T(8,128)(2,1)}), bf16[16,64,256]{2,1,0:T(8,128)(2,1)S(1)}, u32[]{:S(2)}, u32[]{:S(2)}) async-start(bf16[16,64,256]{2,1,0:T(8,128)(2,1)} %scatter_fusion.1), calls=%async_computation.5 | async-start | bytes 1048576 | tf_op jit(solution)/shard_map/all_to_all | solution.py:112
  243.0 2.4 convolution_bitcast_fusion.8
  245.5 1.6 convolution_bitcast_fusion.9
  247.1 1.6 convolution_bitcast_fusion.10
  248.7 1.6 convolution_bitcast_fusion.11
  250.2 7.1 %scatter_custom_fusion.1 = f32[512,256]{1,0:T(8,128)S(1)} fusion(s32[1024]{0:T(1024)S(1)} %bitcast.543, bf16[1024,256]{1,0:T(8,128)(2,1)S(1)} %bitcast.513, f32[]{:T(128)} %constant.79.clone.1), kind=kCustom, calls=%fused_computation.29 | custom fusion | flops 524288 | bytes 1048580 | tf_op jit(solution)/shard_map/scatter-add | solution.py:113
  257.4 7.2 %scatter_custom_fusion.3 = f32[512,256]{1,0:T(8,128)S(1)} fusion(f32[512,256]{1,0:T(8,128)S(1)} %scatter_custom_fusion.1, s32[1024]{0:T(1024)S(1)} %bitcast.542, bf16[1024,256]{1,0:T(8,128)(2,1)S(1)} %bitcast.514), kind=kCustom, calls=%fused_computation.27 | custom fusion | flops 524288 | bytes 1048576 | tf_op jit(solution)/shard_map/scatter-add | solution.py:113
  264.6 0.7 convert_element_type.428
  265.4 3.9 maximum_add_fusion
  269.4 40.1 %psum.22 = f32[4,256]{1,0:T(4,128)S(1)} all-reduce(f32[4,256]{1,0:T(4,128)S(1)} %maximum_add_fusion.1), channel_id=1, replica_groups=mesh['emb'=16,'seq'=2] {'emb','seq'}, use_global_device_ids=true, to_apply=%region_41.42 | all-reduce | flops 1024 | bytes 8192 | tf_op jit(solution)/shard_map/psum | solution.py:118
  310.1 1.8 convert_element_type.429
  311.8 122.8 %all-reduce.35.cloned.1.call-done = f32[4,768,256]{2,1,0:T(8,128)} async-done(((f32[4,768,256]{2,1,0:T(8,128)}), f32[4,768,256]{2,1,0:T(8,128)}) %all-reduce.35.cloned.1.call-update) | async-done | bytes 3145744 | tf_op jit(solution)/shard_map/psum | solution.py:118
  434.6 3.9 broadcast_multiply_fusion
  (253 shorter events, 23.2 us)
Async XLA Ops:
  7.2 29.3 %copy-start = (bf16[512,256]{1,0:T(8,128)(2,1)S(1)}, bf16[512,256]{1,0:T(8,128)(2,1)}, u32[]{:S(2)}) copy-start(bf16[512,256]{1,0:T(8,128)(2,1)} %param.6) | copy-start | bytes 786436
  32.9 9.8 %all-to-all-start = ((s32[16,1,64]{2,1,0:T(1,128)}), s32[16,1,64]{2,1,0:T(1,128)S(1)}, u32[]{:S(2)}, u32[]{:S(2)}) async-start(s32[16,1,64]{2,1,0:T(1,128)} %get-tuple-element.89), calls=%async_computation | async-start | bytes 16384 | tf_op jit(solution)/shard_map/all_to_all | solution.py:98
  42.6 19.2 %all-to-all-start.3 = ((bf16[16,64,256]{2,1,0:T(8,128)(2,1)}), bf16[16,64,256]{2,1,0:T(8,128)(2,1)S(1)}, u32[]{:S(2)}, u32[]{:S(2)}) async-start(bf16[16,64,256]{2,1,0:T(8,128)(2,1)} %bitcast.44), calls=%async_computation.3 | async-start | bytes 1048576 | tf_op jit(solution)/shard_map/all_to_all | solution.py:102
  47.4 2.1 copy-start.56
  47.4 2.1 copy-start.55
  61.9 18.7 %all-to-all-start.1 = ((bf16[16,64,256]{2,1,0:T(8,128)(2,1)}), bf16[16,64,256]{2,1,0:T(8,128)(2,1)S(1)}, u32[]{:S(2)}, u32[]{:S(2)}) async-start(bf16[16,64,256]{2,1,0:T(8,128)(2,1)} %bitcast.512), calls=%async_computation.1 | async-start | bytes 1048576 | tf_op jit(solution)/shard_map/all_to_all | solution.py:102
  85.4 20.7 %copy-start.57 = (f32[512,256]{1,0:T(8,128)}, f32[512,256]{1,0:T(8,128)S(1)}, u32[]{:S(2)}) copy-start(f32[512,256]{1,0:T(8,128)S(1)} %get-tuple-element.112) | copy-start | bytes 1572868
  86.6 18.8 %copy-start.61 = (f32[512,256]{1,0:T(8,128)}, f32[512,256]{1,0:T(8,128)S(1)}, u32[]{:S(2)}) copy-start(f32[512,256]{1,0:T(8,128)S(1)} %get-tuple-element.113) | copy-start | bytes 1572868
  88.1 14.7 %copy-start.59 = (f32[512,256]{1,0:T(8,128)}, f32[512,256]{1,0:T(8,128)S(1)}, u32[]{:S(2)}) copy-start(f32[512,256]{1,0:T(8,128)S(1)} %get-tuple-element.114) | copy-start | bytes 1572868
  89.3 12.8 %copy-start.65 = (f32[512,256]{1,0:T(8,128)}, f32[512,256]{1,0:T(8,128)S(1)}, u32[]{:S(2)}) copy-start(f32[512,256]{1,0:T(8,128)S(1)} %get-tuple-element.115) | copy-start | bytes 1572868
  90.9 8.6 %copy-start.63 = (f32[512,256]{1,0:T(8,128)}, f32[512,256]{1,0:T(8,128)S(1)}, u32[]{:S(2)}) copy-start(f32[512,256]{1,0:T(8,128)S(1)} %get-tuple-element.116) | copy-start | bytes 1572868
  92.0 6.8 %copy-start.67 = (f32[512,256]{1,0:T(8,128)}, f32[512,256]{1,0:T(8,128)S(1)}, u32[]{:S(2)}) copy-start(f32[512,256]{1,0:T(8,128)S(1)} %get-tuple-element.117) | copy-start | bytes 1572868
  92.0 1.7 copy-start.22
  92.6 1.7 copy-start.5
  92.6 2.5 copy-start.7
  92.7 2.4 copy-start.51
  92.7 2.4 copy-start.53
  98.7 1.9 copy-start.9
  98.7 2.9 copy-start.15
  101.6 2.4 copy-start.11
  102.0 2.9 copy-start.19
  104.9 2.8 copy-start.13
  105.4 2.3 copy-start.17
  166.7 69.7 %all-to-all-start.4 = ((bf16[16,64,256]{2,1,0:T(8,128)(2,1)}), bf16[16,64,256]{2,1,0:T(8,128)(2,1)S(1)}, u32[]{:S(2)}, u32[]{:S(2)}) async-start(bf16[16,64,256]{2,1,0:T(8,128)(2,1)} %scatter_fusion), calls=%async_computation.4 | async-start | bytes 1048576 | tf_op jit(solution)/shard_map/all_to_all | solution.py:112
  171.9 57.1 %copy-start.8 = (bf16[1,512,256]{2,1,0:T(8,128)(2,1)S(1)}, bf16[1,512,256]{2,1,0:T(8,128)(2,1)}, u32[]{:S(2)}) copy-start(bf16[1,512,256]{2,1,0:T(8,128)(2,1)} %copy-done.7) | copy-start | bytes 786436
  171.9 57.2 %copy-start.52 = (bf16[1,512,256]{2,1,0:T(8,128)(2,1)S(1)}, bf16[1,512,256]{2,1,0:T(8,128)(2,1)}, u32[]{:S(2)}) copy-start(bf16[1,512,256]{2,1,0:T(8,128)(2,1)} %copy-done.51) | copy-start | bytes 786436
  229.0 2.5 copy-start.4
  229.0 2.5 copy-start.16
  229.0 2.5 copy-start.48
  229.1 2.5 copy-start.50
  229.1 2.5 copy-start.68
  233.2 1.6 copy-start.18
  233.2 1.6 copy-start.32
  233.2 1.6 copy-start.34
  233.2 1.6 copy-start.62
  234.8 8.2 %copy-start.6 = (bf16[1,512,256]{2,1,0:T(8,128)(2,1)S(1)}, bf16[1,512,256]{2,1,0:T(8,128)(2,1)}, u32[]{:S(2)}) copy-start(bf16[1,512,256]{2,1,0:T(8,128)(2,1)} %copy-done.5) | copy-start | bytes 786436
  234.8 8.2 %copy-start.44 = (bf16[1,512,256]{2,1,0:T(8,128)(2,1)S(1)}, bf16[1,512,256]{2,1,0:T(8,128)(2,1)}, u32[]{:S(2)}) copy-start(bf16[1,512,256]{2,1,0:T(8,128)(2,1)} %copy-done.43) | copy-start | bytes 786436
  236.4 21.0 %all-to-all-start.5 = ((bf16[16,64,256]{2,1,0:T(8,128)(2,1)}), bf16[16,64,256]{2,1,0:T(8,128)(2,1)S(1)}, u32[]{:S(2)}, u32[]{:S(2)}) async-start(bf16[16,64,256]{2,1,0:T(8,128)(2,1)} %scatter_fusion.1), calls=%async_computation.5 | async-start | bytes 1048576 | tf_op jit(solution)/shard_map/all_to_all | solution.py:112
  242.9 2.6 copy-start.2
  242.9 2.6 copy-start.10
  242.9 2.5 copy-start.36
  242.9 2.5 copy-start.38
  242.9 67.2 %all-reduce.37.cloned.1.call-start = ((), (), s32[]{:S(2)}) async-start(), calls=%async_computation.7 | async-start | bytes 524288 | tf_op jit(solution)/shard_map/psum | solution.py:117
  243.0 2.5 copy-start.64
  245.4 1.6 copy-start.12
  247.1 1.6 copy-start.14
  250.2 15.1 %copy-start.21 = (f32[1,768,256]{2,1,0:T(8,128)S(1)}, f32[1,768,256]{2,1,0:T(8,128)}, u32[]{:S(2)}) copy-start(f32[1,768,256]{2,1,0:T(8,128)} %convolution_bitcast_fusion.12) | copy-start | bytes 2359300
  265.3 169.3 %all-reduce.35.cloned.1.call-start = ((), (), s32[]{:S(2)}) async-start(), calls=%async_computation.6 | async-start | bytes 6291456 | tf_op jit(solution)/shard_map/psum | solution.py:118
  (28 other events, 30.4 us)
Sparse Core Ops, SparseCore 0:
  265.4 24.3 all-reduce.36
  296.8 137.8 all-reduce.34
where the time goes:
time: 453 us; the launch traced here: 446 us
  local copies, waits for them, and re-layouts  145 us (32%)
  waiting for transfers between devices  140 us (31%)
  blocking collectives  53.7 us (12%)
  other arithmetic  44.7 us (10%)
  matrix products  23.4 us (5%)
  starting transfers between devices  23.3 us (5%)
  between operations  15.8 us (3%)
    psum x1, waiting for transfers between devices, body(): weight_sum, gain_sum = lax.psum((weight_total, gain_total), ('emb', 'seq'))  123 us
    scatter x2, local copies, waits for them, and re-layouts, body(): outgoing = jnp.zeros((shards, capacity, width), jnp.bfloat16).at[owners[b...  114 us
    psum x1, blocking collectives, body(): weight_sum, gain_sum = lax.psum((weight_total, gain_total), ('emb', 'seq'))  40.1 us
    all_to_all x2, waiting for transfers between devices, body(): lax.all_to_all(served, 'emb', split_axis=0, concat_axis=0, tiled=True)  16.1 us
    scatter-add x2, other arithmetic, body(): table_part.at[arrived_ids.reshape(-1)]  14.3 us
    dot_general x8, matrix products, backward_block(): lax.dot_general(flat, dconv, (((0,), (0,)), ((), ())), preferred_element_...  14.3 us
    all_to_all x1, blocking collectives, body(): lax.all_to_all(requests[:, batch], 'emb', split_axis=0, concat_axis=0, ti...  13.6 us
    all_to_all x2, starting transfers between devices, body(): lax.all_to_all(outgoing, 'emb', split_axis=0, concat_axis=0, tiled=True)  10.7 us
  transfers between devices with their start and end apart: 7, of which 4 were waited for; matrix products, arithmetic and copies ran while one was open for 23% of the time, Pallas kernels for 0%

commit v1 on v0

v1 whole, which is shorter than its diff:
```python
import functools
import math

import jax
import jax.numpy as jnp
from jax import lax
from jax.experimental import pallas as pl
from jax.experimental.pallas import tpu as pltpu
from jax.sharding import PartitionSpec as P

MB = 2
TILE = 128
CHUNK = 256
PAD = 16
GROUP = 16
F32 = jnp.float32
BF16 = jnp.bfloat16
VMEM = pl.BlockSpec(memory_space=pltpu.VMEM)
SMEM = pl.BlockSpec(memory_space=pltpu.SMEM)
ANY = pl.BlockSpec(memory_space=pl.ANY)


def iota(shape, axis):
    return lax.broadcasted_iota(jnp.int32, shape, axis)


def one_hot(mask):
    return jnp.where(mask, 1.0, 0.0).astype(BF16)


def dot(a, b, contract=(1, 0)):
    return lax.dot_general(
        a, b, (((contract[0],), (contract[1],)), ((), ())), preferred_element_type=F32
    )


def log2(number):
    return int(number).bit_length() - 1


def ordered(near):
    top = near // 2
    steps = sorted(range(1, near), key=lambda step: (step < 2, step & 1, step < top, step < top + 2))
    return [0] + steps


def returning(chips):
    return [0] + sorted(range(1, chips), key=lambda step: (step & 1, step))


def params(mib):
    return pltpu.CompilerParams(vmem_limit_bytes=mib * 2**20)


def request_kernel(
    slab, place_ref, ids_ref, table_hbm, request_ref, code_ref, table_ref, sem
):
    copy = pltpu.make_async_copy(table_hbm, table_ref, sem)
    copy.start()
    near = request_ref.shape[0]
    reach = request_ref.shape[1] // 2
    batches, count = ids_ref.shape
    capacity = reach // batches
    upper = one_hot(iota((count, count), 0) <= iota((count, count), 1))
    for batch in range(batches):
        ids = ids_ref[batch : batch + 1, :]
        owners, rows = ids >> log2(slab), ids & (slab - 1)
        peers = owners & (near - 1)
        sides = (owners >> log2(near)) ^ place_ref[3]
        marks = jnp.where(iota((2 * near, count), 0) == sides * near + peers, 1.0, 0.0)
        ranks = dot(marks.astype(BF16), upper)
        slots = (jnp.sum(marks * ranks, axis=0, keepdims=True) - 1.0).astype(jnp.int32)
        code_ref[batch : batch + 1, :] = ((peers ^ place_ref[5]) * 2 + sides) * capacity + slots
        spots = one_hot(iota((capacity, count), 0) == slots)
        high = (marks * (rows >> 8).astype(F32)).astype(BF16)
        low = (marks * (rows & 255).astype(F32)).astype(BF16)
        asked = dot(high, spots, (1, 1)) * 256.0 + dot(low, spots, (1, 1))
        for side in range(2):
            start = side * reach + batch * capacity
            request_ref[:, start : start + capacity] = asked[
                side * near : (side + 1) * near
            ].astype(jnp.int32)
    copy.wait()


def near_kernel(place_ref, asked_ref, table_ref, turned_ref, *served_refs):
    near, both = asked_ref.shape
    reach = both // 2
    slab = table_ref.shape[0]
    asked = jnp.concatenate(
        [asked_ref[pl.ds(place_ref[5] ^ step, 1), :] for step in range(near)], axis=0
    )
    turned_ref[...] = asked
    columns = jnp.transpose(asked.astype(F32)).astype(jnp.int32)
    for step, served_ref in enumerate(served_refs):
        picks = one_hot(columns[:reach, step : step + 1] == iota((reach, slab), 1))
        served_ref[...] = dot(picks, table_ref[...]).astype(BF16)


def far_kernel(asked_ref, table_ref, *refs):
    near, both = asked_ref.shape
    reach = both // 2
    slab = table_ref.shape[0]
    columns = jnp.transpose(asked_ref[...].astype(F32)).astype(jnp.int32)
    for step in range(near):
        picks = one_hot(columns[reach:, step : step + 1] == iota((reach, slab), 1))
        refs[near + step][:reach, :] = refs[step][...]
        refs[near + step][reach:, :] = dot(picks, table_ref[...]).astype(BF16)


def collect_kernel(place_ref, asked_ref, after_ref, *refs):
    del after_ref
    near, both = asked_ref.shape
    reach = both // 2
    order = returning(near // 2)
    returned, refs = [refs[order.index(chip)] for chip in range(near // 2)], refs[near // 2 :]
    keeps, messages, parts_s = refs[:2], refs[2:-1], refs[-1]
    slab = parts_s.shape[1]
    share = slab // (1 + len(messages))
    for side in range(2):
        span = slice(side * reach, (side + 1) * reach)
        picks = [
            one_hot(iota((slab, reach), 0) == asked_ref[peer : peer + 1, span])
            for peer in range(near)
        ]
        rows = [ref[core, span, :] for ref in returned for core in range(2)]
        total = None
        pair = 2 if reach % 128 == 0 else 1
        for spot in range(0, near, pair):
            term = dot(
                jnp.concatenate(picks[spot : spot + pair], axis=1),
                jnp.concatenate(rows[spot : spot + pair], axis=0),
            )
            total = term if total is None else total + term
        parts_s[side] = total
        for step in range(1 + len(messages)):
            spot = pl.multiple_of((place_ref[4] ^ step) * share, share)
            value = parts_s[side, pl.ds(spot, share), :]
            if step == 0:
                keeps[side][...] = value
            else:
                messages[step - 1][side * share : (side + 1) * share, :] = value.astype(BF16)


def gain_block(values):
    high = values.astype(BF16)
    low = (values - high.astype(F32)).astype(BF16)
    rest = GROUP - 2 * values.shape[0]
    return jnp.concatenate([high, low, jnp.zeros((rest, values.shape[1]), BF16)], axis=0)


def gain_values(block, layers):
    blockf = block.astype(F32)
    return blockf[:layers] + blockf[layers : 2 * layers]


def stack_kernel(
    place_ref, column_ref, weight_ref, gain_hbm, upstream_hbm, *refs,
):
    arrived_refs, refs = refs[:-18], refs[-18:]
    gain_ref, upstream_ref, sems = refs[15:]
    copies = [
        pltpu.make_async_copy(gain_hbm, gain_ref, sems.at[0]),
        pltpu.make_async_copy(upstream_hbm, upstream_ref, sems.at[1]),
    ]
    for copy in copies:
        copy.start()
    order = ordered(len(arrived_refs))
    fetched_refs = [arrived_refs[order.index(step)] for step in range(len(order))]
    g_ref, keep_ref, sent_ref, block_ref = refs[:4]
    x_s, h_s, hidden_s, normed_s, inverse_s, slope_s, dconv_s, spread_s, dw_s = refs[4:13]
    rounded_s, turned_s = refs[13:15]
    layers, taps, width = weight_ref.shape
    shards, reach = 2 * len(fetched_refs), fetched_refs[0].shape[0] // 2
    tokens = column_ref.shape[0]
    batches = MB
    length = tokens // batches
    capacity = reach // batches
    wide = shards * capacity
    per = length // CHUNK
    steps = taps // width

    def at(seq, j):
        return pl.ds(seq * length + j * CHUNK, CHUNK)

    def inside(seq, j, ahead, size=CHUNK):
        return pl.ds(seq * (length + PAD) + j * CHUNK + ahead, size)

    for batch in range(batches):
        start = batch * (length + PAD)
        for side in range(2):
            h_s[side, start : start + PAD, :] = jnp.zeros((PAD, width), F32)
            dconv_s[side, start + length : start + length + PAD, :] = jnp.zeros((PAD, width), F32)
    dw_s[...] = jnp.zeros(dw_s.shape, F32)
    for layer in range(layers):
        for start in range(0, taps, width):
            value = weight_ref[layer, start : start + width, :]
            rounded_s[layer, start : start + width, :] = value.astype(BF16)
            turned_s[layer, start : start + width, :] = jnp.transpose(value).astype(BF16)

    copies[0].wait()

    def normalise(seq, j, layer, value):
        centred = value - jnp.mean(value, axis=-1, keepdims=True)
        inverse = lax.rsqrt(jnp.mean(centred * centred, axis=-1, keepdims=True) + 1e-05)
        normed = centred * inverse
        normed_s[layer, at(seq, j), :] = normed
        inverse_s[layer, at(seq, j), :] = jnp.broadcast_to(inverse, (CHUNK, 128))
        hidden = normed * gain_ref[layer : layer + 1, :]
        h_s[layer % 2, inside(seq, j, PAD), :] = hidden
        hidden_s[layer, at(seq, j), :] = hidden.astype(BF16)

    for batch in range(batches):
        held = jnp.concatenate(
            [
                ref[side * reach + batch * capacity : side * reach + (batch + 1) * capacity, :]
                for ref in fetched_refs
                for side in range(2)
            ],
            axis=0,
        )
        for j in range(per):
            picks = one_hot(column_ref[at(batch, j), :] == iota((CHUNK, wide), 1))
            value = dot(picks, held)
            x_s[at(batch, j), :] = value
            normalise(batch, j, 0, value)

    root = math.sqrt(2.0 / math.pi)
    for layer in range(layers):
        dilation = 2**layer

        for seq in range(batches):
            for j in range(per):
                view = h_s[layer % 2, inside(seq, j, 0, CHUNK + PAD), :]
                stacked = jnp.concatenate(
                    [
                        view[PAD - tap * dilation : PAD - tap * dilation + CHUNK].astype(BF16)
                        for tap in range(steps)
                    ],
                    axis=1,
                )
                conv = dot(stacked, rounded_s[layer])
                square = conv * conv
                curve = jnp.tanh(conv * (root + (0.044715 * root) * square))
                half = 0.5 + 0.5 * curve
                gelu = conv * half
                slope_s[layer, at(seq, j), :] = half + gelu * (1.0 - curve) * (
                    root + (3.0 * 0.044715 * root) * square
                )
                if layer + 1 < layers:
                    value = (x_s[at(seq, j), :] + gelu).astype(BF16).astype(F32)
                    x_s[at(seq, j), :] = value
                    normalise(seq, j, layer + 1, value)

    def weigh(seq, layer):
        whole = pl.ds(seq * length, length)
        term = dot(hidden_s[layer, whole, :], spread_s[layer % 2, whole, :], (0, 0))
        for tap in range(steps):
            rows = pl.ds(layer * taps + tap * width, width)
            dw_s[rows, :] += term[:, tap * width : (tap + 1) * width]

    copies[1].wait()
    for seq in range(batches):
        for j in range(per):
            cotangent = upstream_ref[at(seq, j), :].astype(F32)
            dconv = (cotangent * slope_s[layers - 1, at(seq, j), :]).astype(BF16).astype(F32)
            dconv_s[(layers - 1) % 2, inside(seq, j, 0), :] = dconv

    gains = [None] * layers
    for layer in reversed(range(layers)):
        dilation = 2**layer

        total = jnp.zeros((8, width), F32)
        for seq in range(batches):
            if layer + 1 < layers:
                weigh(seq, layer + 1)
            for j in range(per):
                view = dconv_s[layer % 2, inside(seq, j, 0, CHUNK + PAD), :]
                spread = jnp.concatenate(
                    [
                        view[tap * dilation : tap * dilation + CHUNK].astype(BF16)
                        for tap in range(steps)
                    ],
                    axis=1,
                )
                spread_s[layer % 2, at(seq, j), :] = spread
                dhidden = dot(spread, turned_s[layer])
                normed = normed_s[layer, at(seq, j), :]
                product = dhidden * normed
                gain_row = gain_ref[layer : layer + 1, :]
                dnorm = dhidden * gain_row
                middle = jnp.mean(dnorm, axis=-1, keepdims=True)
                along = jnp.mean(product * gain_row, axis=-1, keepdims=True)
                inverse = inverse_s[layer, at(seq, j), :]
                inverse = jnp.concatenate([inverse] * (width // 128), axis=1)
                held = upstream_ref if layer == layers - 1 else g_ref
                cotangent = held[at(seq, j), :].astype(F32) + inverse * (
                    dnorm - middle - normed * along
                )
                cotangent = cotangent.astype(BF16)
                g_ref[at(seq, j), :] = cotangent
                if layer > 0:
                    dconv = cotangent.astype(F32) * slope_s[layer - 1, at(seq, j), :]
                    dconv_s[(layer - 1) % 2, inside(seq, j, 0), :] = dconv.astype(BF16).astype(F32)
                total = total + jnp.sum(product.reshape(CHUNK // 8, 8, width), axis=0)
        gains[layer] = jnp.sum(total, axis=0, keepdims=True)

    for batch in range(batches):
        weigh(batch, 0)
    half = keep_ref.shape[0]
    mine = place_ref[0]
    keep_ref[...] = dw_s[pl.ds(pl.multiple_of(mine * half, half), half), :].astype(BF16)
    sent_ref[:half, :] = dw_s[pl.ds(pl.multiple_of((1 - mine) * half, half), half), :].astype(BF16)
    block = gain_block(jnp.concatenate(gains, axis=0))
    sent_ref[half:, :] = block
    block_ref[...] = block


def place_kernel(code_ref, value_ref, *outgoing_refs):
    chips = outgoing_refs[0].shape[0]
    reach = outgoing_refs[0].shape[1] // 2
    batches, length = code_ref.shape
    capacity = reach // batches
    span = TILE // capacity
    for batch in range(batches):
        codes = code_ref[batch : batch + 1, :]
        whole = value_ref[batch * length : (batch + 1) * length, :]
        for j in range(4 * chips // span):
            picks = one_hot(iota((TILE, length), 0) + j * TILE == codes)
            rows = dot(picks, whole).astype(BF16)
            for spot in range(span):
                peer, side = divmod(j * span + spot, 2)
                start = side * reach + batch * capacity
                outgoing_refs[peer % 2][peer // 2, start : start + capacity, :] = rows[
                    spot * capacity : (spot + 1) * capacity
                ]


def pack_kernel(same_ref, other_ref, after_ref, *packed_refs):
    del after_ref
    for chip, ref in enumerate(packed_refs):
        ref[0] = same_ref[chip]
        ref[1] = other_ref[chip]


def tree(values):
    values = list(values)
    while len(values) > 1:
        values = [values[i] + values[i + 1] for i in range(0, len(values), 2)]
    return values[0]


def fold_kernel(layers, arrived, parts, spot, place_ref, keep_ref, block_ref, *refs):
    messages, outs = refs[:arrived], refs[-1 - parts :]
    size = keep_ref.shape[0]
    block = tree(
        [gain_values(block_ref[...], layers)]
        + [gain_values(message[size:, :], layers) for message in messages]
    )
    block = gain_block(block)
    piece = size // parts
    mine = place_ref[spot]
    for part in range(parts):
        rows = pl.ds(pl.multiple_of((mine ^ part) * piece, piece), piece)
        value = tree([keep_ref[rows, :].astype(F32)] + [m[rows, :].astype(F32) for m in messages])
        if part == 0:
            outs[0][...] = value
        else:
            outs[1 + part][:piece, :] = value.astype(BF16)
            outs[1 + part][piece:, :] = block
    outs[1][...] = block


def last_kernel(layers, scale, keep_ref, block_ref, *refs):
    messages, outs = refs[:-2], refs[-2:]
    size = keep_ref.shape[0]
    outs[0][...] = tree([keep_ref[...]] + [m[:size, :].astype(F32) for m in messages]).astype(BF16)
    block = tree(
        [gain_values(block_ref[...], layers)]
        + [gain_values(message[size:, :], layers) for message in messages]
    )
    outs[1][...] = block * scale


def finish_kernel(line, scale, side, place_ref, *refs):
    rows_s, sems = refs[-2:]
    out_ref = refs[-3 - side]
    square, block, _ = rows_s.shape
    piece = block // line
    copies = []
    for outer, ref in enumerate(refs[:square]):
        for inner in range(line):
            target = pl.multiple_of((place_ref[2] ^ inner) * piece, piece)
            rows_s[outer, pl.ds(target, piece), :] = (
                ref[inner * piece : (inner + 1) * piece, :].astype(F32) * scale
            )
        spot = (place_ref[0] ^ side) * square + (place_ref[1] ^ outer)
        rows = pl.ds(pl.multiple_of(spot * block, block), block)
        copies.append(pltpu.make_async_copy(rows_s.at[outer], out_ref.at[rows, :], sems.at[outer]))
        copies[-1].start()
    if side == 1:
        refs[-3][...] = jnp.zeros(refs[-3].shape, F32)
    for copy in copies:
        copy.wait()


def line_kernel(pieces, *refs):
    joined_ref, near_sum_ref, far_sum_ref = refs[-3:]
    size = refs[0].shape[0]
    for spot, ref in enumerate(refs[:pieces]):
        joined_ref[spot * size : (spot + 1) * size, :] = ref[...]
    near_ref, far_ref, *shares = refs[pieces:-3]
    share = near_ref.shape[0]
    near_sum_ref[...] = tree([near_ref[...]] + [m[:share, :].astype(F32) for m in shares])
    far_sum_ref[...] = tree([far_ref[...]] + [m[share:, :].astype(F32) for m in shares]).astype(BF16)


def share_kernel(near_ref, far_ref, *refs):
    refs[-1][...] = (near_ref[...] + far_ref[...].astype(F32)).astype(BF16)


def table_kernel(place_ref, after_ref, *refs):
    del after_ref
    share = refs[0].shape[0]
    for step, ref in enumerate(refs[:-1]):
        spot = pl.multiple_of((place_ref[4] ^ step) * share, share)
        refs[-1][pl.ds(spot, share), :] = ref[...].astype(F32)


def body(table, owner, row, conv_weight, gain, upstream):
    shards, seqs = lax.axis_size("emb"), lax.axis_size("seq")
    seqs_dev, length = row.shape
    slab, width = table.shape
    layers, taps, _ = conv_weight.shape
    count = seqs_dev // MB * length
    capacity = max(2, 2 * count // shards)
    reach = MB * capacity
    wide = shards * capacity
    rows = layers * taps
    devices = shards * seqs
    axes = ("emb", "seq")

    low = log2(seqs)
    stages = [[low], [0, low + 1], [low + 2, low + 3]]
    left = [bit for bit in range(log2(devices)) if bit not in sum(stages, [])]
    me = lax.axis_index("emb") * seqs + lax.axis_index("seq")
    across = [log2(devices) - 1]
    group = list(range(low))
    peers = list(range(low, log2(devices) - 1))
    place = jnp.stack(
        [
            sum(((me >> bit) & 1) << spot for spot, bit in enumerate(bits))
            for bits in stages + [across, group, peers]
        ]
    ).astype(jnp.int32)

    def swap(value, bits, step):
        mask = sum(((step >> spot) & 1) << bit for spot, bit in enumerate(bits))
        return lax.ppermute(value, axes, [(i, i ^ mask) for i in range(devices)])

    near = shards // 2

    def exchange(value):
        groups = [list(range(near)), list(range(near, shards))]
        return lax.all_to_all(
            value, "emb", split_axis=0, concat_axis=0, axis_index_groups=groups, tiled=True
        )

    shape = jax.ShapeDtypeStruct
    held = functools.partial(pltpu.with_memory_space_constraint, memory_space=pltpu.HBM)
    mirrored = swap(table, across, 1)
    requests, codes, table = pl.pallas_call(
        functools.partial(request_kernel, slab),
        out_shape=(
            shape((near, 2 * reach), jnp.int32),
            shape((MB, count), jnp.int32),
            shape(table.shape, BF16),
        ),
        in_specs=[SMEM, VMEM, ANY],
        out_specs=(VMEM,) * 3,
        scratch_shapes=[pltpu.SemaphoreType.DMA],
        compiler_params=params(16),
        name="request",
    )(place, (owner[:, :, 0] * slab + row).reshape(MB, count), held(table))
    asked = exchange(requests)
    asked, *served = pl.pallas_call(
        near_kernel,
        out_shape=(shape(asked.shape, jnp.int32),) + (shape((reach, width), BF16),) * near,
        in_specs=[SMEM, VMEM, VMEM],
        out_specs=(VMEM,) * (1 + near),
        compiler_params=params(16),
        name="near",
    )(place, asked, table)
    served = pl.pallas_call(
        far_kernel,
        out_shape=(shape((2 * reach, width), BF16),) * near,
        in_specs=[VMEM] * (2 + near),
        out_specs=(VMEM,) * near,
        compiler_params=params(16),
        name="far",
    )(asked, mirrored, *served)
    order = ordered(near)
    fetched = [swap(served[step], peers, step) if step else served[0] for step in order]

    tokens = MB * count
    half = rows // 2
    padded = tokens + MB * PAD
    moved, keep, sent, block = pl.pallas_call(
        stack_kernel,
        out_shape=(
            shape((tokens, width), BF16),
            shape((half, width), BF16),
            shape((half + GROUP, width), BF16),
            shape((GROUP, width), BF16),
        ),
        in_specs=[SMEM, VMEM, VMEM, ANY, ANY] + [VMEM] * near,
        out_specs=(VMEM,) * 4,
        scratch_shapes=[
            pltpu.VMEM((tokens, width), F32),
            pltpu.VMEM((2, padded, width), F32),
            pltpu.VMEM((layers, tokens, width), BF16),
            pltpu.VMEM((layers, tokens, width), F32),
            pltpu.VMEM((layers, tokens, 128), F32),
            pltpu.VMEM((layers, tokens, width), F32),
            pltpu.VMEM((2, padded, width), F32),
            pltpu.VMEM((2, tokens, taps), BF16),
            pltpu.VMEM((rows, width), F32),
            pltpu.VMEM((layers, taps, width), BF16),
            pltpu.VMEM((layers, taps, width), BF16),
            pltpu.VMEM((layers, width), F32),
            pltpu.VMEM((tokens, width), BF16),
            pltpu.SemaphoreType.DMA((2,)),
        ],
        compiler_params=params(50),
        name="stack",
    )(
        place, codes.reshape(tokens, 1), conv_weight, held(gain),
        held(upstream.reshape(tokens, width)),
        *fetched,
    )

    chips = near // 2
    same, other = pl.pallas_call(
        place_kernel,
        out_shape=(shape((chips, 2 * reach, width), BF16),) * 2,
        in_specs=[VMEM, VMEM],
        out_specs=(VMEM, VMEM),
        compiler_params=params(24),
        name="place",
    )(codes, moved)
    other = swap(other, peers, 1)

    messages = [sent]
    share = slab // seqs
    for spot, bits in enumerate(stages[:-1]):
        arrived = [swap(message, bits, step + 1) for step, message in enumerate(messages)]
        parts = 2 ** len(stages[spot + 1])
        piece = keep.shape[0] // parts
        outs = (shape((piece, width), F32), shape((GROUP, width), BF16)) + (
            shape((piece + GROUP, width), BF16),
        ) * (parts - 1)
        rest = returned[1 : 1 + chips // 4] if spot == 1 else []
        keep, block, *messages = pl.pallas_call(
            functools.partial(fold_kernel, layers, len(arrived), parts, spot + 1),
            out_shape=outs,
            in_specs=[SMEM] + [VMEM] * (2 + len(arrived)) + [ANY] * len(rest),
            out_specs=(VMEM,) * len(outs),
            compiler_params=params(16),
            name=f"fold{spot}",
        )(place, keep, block, *arrived, *rest)
        if spot == 0:
            packed = pl.pallas_call(
                pack_kernel,
                out_shape=(shape((2, 2 * reach, width), BF16),) * chips,
                in_specs=[VMEM, VMEM, ANY],
                out_specs=(VMEM,) * chips,
                compiler_params=params(16),
                name="pack",
            )(same, other, block)
            returned = [
                swap(packed[step], peers[1:], step) if step else packed[0]
                for step in returning(chips)
            ]

    scale = float(seqs_dev * length * devices) ** (-0.5)
    arrived = [swap(message, stages[2], step + 1) for step, message in enumerate(messages)]
    keep, gain_grad = pl.pallas_call(
        functools.partial(last_kernel, layers, scale),
        out_shape=(shape(keep.shape, BF16), shape((layers, width), F32)),
        in_specs=[VMEM] * (2 + len(arrived)),
        out_specs=(VMEM,) * 2,
        compiler_params=params(16),
        name="last",
    )(keep, block, *arrived)
    near_share, far_share, *shares = pl.pallas_call(
        collect_kernel,
        out_shape=(shape((share, width), F32),) * 2
        + (shape((2 * share, width), BF16),) * (seqs - 1),
        in_specs=[SMEM, VMEM, ANY] + [VMEM] * chips,
        out_specs=(VMEM,) * (1 + seqs),
        scratch_shapes=[pltpu.VMEM((2, slab, width), F32)],
        compiler_params=params(24),
        name="collect",
    )(place, asked, keep, *returned)
    shares = [swap(value, group, step + 1) for step, value in enumerate(shares)]
    for bit in left:
        keep = (keep.astype(F32) + swap(keep, [bit], 1).astype(F32)).astype(BF16)
        gain_grad = gain_grad + swap(gain_grad, [bit], 1)

    line = [keep] + [swap(keep, stages[2], step) for step in range(1, 2 ** len(stages[2]))]
    keep, near_share, far_share = pl.pallas_call(
        functools.partial(line_kernel, len(line)),
        out_shape=(
            shape((half // 4, width), BF16),
            shape((share, width), F32),
            shape((share, width), BF16),
        ),
        in_specs=[VMEM] * (len(line) + 2 + len(shares)),
        out_specs=(VMEM,) * 3,
        compiler_params=params(16),
        name="line",
    )(*line, near_share, far_share, *shares)
    far_share = swap(far_share, across, 1)
    square = [keep] + [swap(keep, stages[1], step) for step in range(1, 4)]
    other = [swap(value, stages[0], 1) for value in square]
    part = pl.pallas_call(
        share_kernel,
        out_shape=shape((share, width), BF16),
        in_specs=[VMEM, VMEM, ANY],
        out_specs=VMEM,
        compiler_params=params(16),
        name="share",
    )(near_share, far_share, square[3])
    weight_grad = pl.pallas_call(
        functools.partial(finish_kernel, 2 ** len(stages[2]), scale, 0),
        out_shape=shape((rows, width), F32),
        in_specs=[SMEM] + [VMEM] * 4,
        out_specs=ANY,
        scratch_shapes=[pltpu.VMEM((4, half // 4, width), F32), pltpu.SemaphoreType.DMA((4,))],
        compiler_params=params(16),
        name="finish0",
    )(place, *square)
    weight_grad, mark = pl.pallas_call(
        functools.partial(finish_kernel, 2 ** len(stages[2]), scale, 1),
        out_shape=(shape((rows, width), F32), shape((8, 128), F32)),
        in_specs=[SMEM] + [VMEM] * 4 + [ANY],
        out_specs=(ANY, VMEM),
        scratch_shapes=[pltpu.VMEM((4, half // 4, width), F32), pltpu.SemaphoreType.DMA((4,))],
        input_output_aliases={5: 0},
        compiler_params=params(16),
        name="finish1",
    )(place, *other, weight_grad)
    table_grad = pl.pallas_call(
        table_kernel,
        out_shape=shape((slab, width), F32),
        in_specs=[SMEM, ANY] + [VMEM] * seqs,
        out_specs=VMEM,
        compiler_params=params(16),
        name="table",
    )(place, mark, part, *[swap(part, group, step) for step in range(1, seqs)])
    return (weight_grad.reshape(conv_weight.shape), gain_grad, table_grad)


def solution(mesh):
    in_specs = (
        P("emb", None),
        P(("emb", "seq"), None, None),
        P(("emb", "seq"), None),
        P(),
        P(),
        P(("emb", "seq"), None, None),
    )
    out_specs = (P(), P(), P("emb", None))
    return jax.shard_map(body, mesh=mesh, in_specs=in_specs, out_specs=out_specs, check_vma=False)
```

time: 453 us -> 105 us (0.23); the launches traced: 446 us -> 104 us
  local copies, waits for them, and re-layouts: 145 us -> 0.32 us
  waiting for transfers between devices: 140 us -> 34.1 us
  blocking collectives: 53.7 us -> 8.43 us
  other arithmetic: 44.7 us -> 0.71 us
  Pallas kernels: 0 us -> 24.4 us
  matrix products: 23.4 us -> 0 us
  between operations: 15.8 us -> 0.8 us
  starting transfers between devices: 23.3 us -> 35.5 us
    psum x2 -> x0, waiting for transfers between devices: 123 us -> none  [the longest x1 123 us: body(): weight_sum, gain_sum = lax.psum((weight_total, gain_total), ('emb', 'seq'))]
    scatter x3 -> x0, local copies, waits for them, and re-layouts: 115 us -> none  [the longest x2 114 us: body(): outgoing = jnp.zeros((shards, capacity, width), jnp.bfloat16).at[owners[b...]
    psum x1 -> x0, blocking collectives: 40.1 us -> none  [body(): weight_sum, gain_sum = lax.psum((weight_total, gain_total), ('emb', 'seq'))]
    ppermute x0 -> x32, starting transfers between devices: none -> 35.5 us  [swap(): return lax.ppermute(value, axes, [(i, i ^ mask) for i in range(devices)])]
    ppermute x0 -> x32, waiting for transfers between devices: none -> 34.1 us  [swap(): return lax.ppermute(value, axes, [(i, i ^ mask) for i in range(devices)])]
    pallas_call x0 -> x15, Pallas kernels: none -> 24.4 us  [the longest x1 11.9 us: body(): pl.pallas_call(stack_kernel, out_shape=(shape((tokens, width), BF16), sha...]
    dot_general x24 -> x0, matrix products: 23.4 us -> none  [the longest x8 14.3 us: backward_block(): lax.dot_general(flat, dconv, (((0,), (0,)), ((), ())), preferred_element_...]
    all_to_all x5 -> x0, starting transfers between devices: 23.2 us -> none  [the longest x2 10.7 us: body(): lax.all_to_all(outgoing, 'emb', split_axis=0, concat_axis=0, tiled=True)]
  transfers between devices with their start and end apart: 7 -> 32, of which waited for: 4 -> 19; matrix products, arithmetic and copies ran while one was open for 23% -> 1% of each run, Pallas kernels for 0% -> 9%
where the time goes in v1:
time: 105 us; the launch traced here: 104 us
  starting transfers between devices  35.5 us (34%)
  waiting for transfers between devices  34.1 us (32%)
  Pallas kernels  24.4 us (23%)
  blocking collectives  8.43 us (8%)
    ppermute x32, starting transfers between devices, swap(): return lax.ppermute(value, axes, [(i, i ^ mask) for i in range(devices)])  35.5 us
    ppermute x32, waiting for transfers between devices, swap(): return lax.ppermute(value, axes, [(i, i ^ mask) for i in range(devices)])  34.1 us
    pallas_call x1, Pallas kernels, body(): pl.pallas_call(stack_kernel, out_shape=(shape((tokens, width), BF16), sha...  11.9 us
    all_to_all x1, blocking collectives, exchange(): lax.all_to_all(value, 'emb', split_axis=0, concat_axis=0, axis_index_grou...  8.43 us
    pallas_call x2, Pallas kernels, body(): pl.pallas_call(functools.partial(finish_kernel, 2 ** len(stages[2]), scal...  3.49 us
  transfers between devices with their start and end apart: 32, of which 19 were waited for; matrix products, arithmetic and copies ran while one was open for 1% of the time, Pallas kernels for 9%

profile of v1, /device:TPU:0, one launch (start us, length us, event | category | flops | bytes accessed | tf_op | source)
XLA Modules:
  0.0 104.3 jit_solution(14345833426870893357)
XLA Ops:
  0.6 4.1 %collective-permute-start = (bf16[512,256]{1,0:T(8,128)(2,1)}, bf16[512,256]{1,0:T(8,128)(2,1)S(1)}, u32[]{:S(2)}, u32[]{:S(2)}) collective-permute-start(bf16[512,256]{1,0:T(8,128)(2,1)} %table_hbm.1), channel_id=1, source_target_pairs={{0,16},{1,17},{2,18},{3,19},{4,20},{5,21},{6,22},{7,23},{8,24},{9,... | collective-permute-start | bytes 786440 | tf_op jit(solution)/shard_map/ppermute | solution.py:459
  4.8 0.7 bitcast_add_fusion.ids_ref
  5.5 1.5 %request.1 = (s32[8,256]{1,0:T(8,128)S(1)}, s32[2,512]{1,0:T(2,128)S(1)}, bf16[512,256]{1,0:T(8,128)(2,1)S(1)}) custom-call(s32[6]{0:T(128)S(1)} %stack.28.place_ref, s32[2,512]{1,0:T(2,128)S(1)} %bitcast_add_fusion.ids_ref, bf16[512,256]{1,0:T(8,128)(2,1)} %table_hbm.1), custom_call_target="tpu_custom_call" | custom-call | tf_op jit(solution)/shard_map/request/pallas_call | solution.py:472
  7.0 8.4 %all_to_all.11 = s32[8,1,256]{2,1,0:T(1,128)S(1)} all-to-all(s32[8,1,256]{2,1,0:T(1,128)S(1)} %copy.14), channel_id=1, replica_groups={{0,2,4,6,8,10,12,14},{16,18,20,22,24,26,28,30},{1,3,5,7,9,11,13,15},{17..., dimensions={0} | all-to-all | bytes 16384 | tf_op jit(solution)/shard_map/all_to_all | solution.py:465
  15.5 1.1 %near.1 = (s32[8,256]{1,0:T(8,128)S(1)}, bf16[128,256]{1,0:T(8,128)(2,1)S(1)}, bf16[128,256]{1,0:T(8,128)(2,1)S(1)}, bf16[128,256]{1,0:T(8,128)(2,1)S(1)}, bf16[...) custom-call(s32[6]{0:T(128)S(1)} %stack.28.place_ref, ...), custom_call_target="tpu_custom_call" | custom-call | tf_op jit(solution)/shard_map/near/pallas_call | solution.py:486
  17.6 1.8 %collective-permute-start.1 = (bf16[256,256]{1,0:T(8,128)(2,1)S(1)}, bf16[256,256]{1,0:T(8,128)(2,1)S(1)}, u32[]{:S(2)}, u32[]{:S(2)}) collective-permute-start(bf16[256,256]{1,0:T(8,128)(2,1)S(1)} %get-tuple-element.66), channel_id=1, source_target_pairs={{0,12},{1,13},{2,14},{3,15},{4,8},{5,9},{6,10},{7,11},{8,4},{9,5},... | collective-permute-start | bytes 393224 | tf_op jit(solution)/shard_map/ppermute | solution.py:459
  19.3 1.3 %collective-permute-start.2 = (bf16[256,256]{1,0:T(8,128)(2,1)S(1)}, bf16[256,256]{1,0:T(8,128)(2,1)S(1)}, u32[]{:S(2)}, u32[]{:S(2)}) collective-permute-start(bf16[256,256]{1,0:T(8,128)(2,1)S(1)} %get-tuple-element.67), channel_id=1, source_target_pairs={{0,8},{1,9},{2,10},{3,11},{4,12},{5,13},{6,14},{7,15},{8,0},{9,1},... | collective-permute-start | bytes 393224 | tf_op jit(solution)/shard_map/ppermute | solution.py:459
  21.6 2.3 %collective-permute-start.5 = (bf16[256,256]{1,0:T(8,128)(2,1)S(1)}, bf16[256,256]{1,0:T(8,128)(2,1)S(1)}, u32[]{:S(2)}, u32[]{:S(2)}) collective-permute-start(bf16[256,256]{1,0:T(8,128)(2,1)S(1)} %get-tuple-element.70), channel_id=1, source_target_pairs={{0,10},{1,11},{2,8},{3,9},{4,14},{5,15},{6,12},{7,13},{8,2},{9,3},... | collective-permute-start | bytes 393224 | tf_op jit(solution)/shard_map/ppermute | solution.py:459
  23.9 1.1 %collective-permute-done.1.refs_1_ = bf16[256,256]{1,0:T(8,128)(2,1)S(1)} collective-permute-done((bf16[256,256]{1,0:T(8,128)(2,1)S(1)}, bf16[256,256]{1,0:T(8,128)(2,1)S(1)}, u32[]{:S(2)}, u32[]{:S(2)}) %collective-permute-start.1) | collective-permute-done | bytes 131104 | tf_op jit(solution)/shard_map/ppermute | solution.py:459
  24.9 1.6 %collective-permute-done.2.refs_2_ = bf16[256,256]{1,0:T(8,128)(2,1)S(1)} collective-permute-done((bf16[256,256]{1,0:T(8,128)(2,1)S(1)}, bf16[256,256]{1,0:T(8,128)(2,1)S(1)}, u32[]{:S(2)}, u32[]{:S(2)}) %collective-permute-start.2) | collective-permute-done | bytes 131104 | tf_op jit(solution)/shard_map/ppermute | solution.py:459
  26.8 0.9 collective-permute-done.3.refs_3_
  27.7 1.1 %collective-permute-done.4.refs_4_ = bf16[256,256]{1,0:T(8,128)(2,1)S(1)} collective-permute-done((bf16[256,256]{1,0:T(8,128)(2,1)S(1)}, bf16[256,256]{1,0:T(8,128)(2,1)S(1)}, u32[]{:S(2)}, u32[]{:S(2)}) %collective-permute-start.4) | collective-permute-done | bytes 131104 | tf_op jit(solution)/shard_map/ppermute | solution.py:459
  28.8 2.0 %collective-permute-done.5.refs_5_ = bf16[256,256]{1,0:T(8,128)(2,1)S(1)} collective-permute-done((bf16[256,256]{1,0:T(8,128)(2,1)S(1)}, bf16[256,256]{1,0:T(8,128)(2,1)S(1)}, u32[]{:S(2)}, u32[]{:S(2)}) %collective-permute-start.5) | collective-permute-done | bytes 131104 | tf_op jit(solution)/shard_map/ppermute | solution.py:459
  30.8 1.3 %collective-permute-done.6.refs_6_ = bf16[256,256]{1,0:T(8,128)(2,1)S(1)} collective-permute-done((bf16[256,256]{1,0:T(8,128)(2,1)S(1)}, bf16[256,256]{1,0:T(8,128)(2,1)S(1)}, u32[]{:S(2)}, u32[]{:S(2)}) %collective-permute-start.6) | collective-permute-done | bytes 131104 | tf_op jit(solution)/shard_map/ppermute | solution.py:459
  32.1 11.9 %stack.29 = (bf16[1024,256]{1,0:T(8,128)(2,1)S(1)}, bf16[1536,256]{1,0:T(8,128)(2,1)S(1)}, bf16[1552,256]{1,0:T(8,128)(2,1)S(1)}, bf16[16,256]{1,0:T(8,128)(2,1)S(1)}) custom-call(s32[6]{0:T(128)S(1)} %stack.28.place_ref, s32[1024,1]{1,0:T(8,128)S(1)} %bitcast.18, f32[4,768,256]{2,1,0:T(8,128)} %weight_ref.1, f32[4,256]{1,0:T(4,128)} %gain_hbm.1, ...), custom_call_target="tpu_custom_call" | custom-call | tf_op jit(solution)/shard_map/stack/pallas_call | solution.py:508
  44.1 0.9 place.1
  45.6 0.8 collective-permute-done.8.refs_0_
  46.4 0.7 fold0.1
  47.1 1.6 %collective-permute-start.9 = (bf16[400,256]{1,0:T(8,128)(2,1)S(1)}, bf16[400,256]{1,0:T(8,128)(2,1)S(1)}, u32[]{:S(2)}, u32[]{:S(2)}) collective-permute-start(bf16[400,256]{1,0:T(8,128)(2,1)S(1)} %get-tuple-element.78), channel_id=1, source_target_pairs={{0,1},{1,0},{2,3},{3,2},{4,5},{5,4},{6,7},{7,6},{8,9},{9,8},{10,11... | collective-permute-start | bytes 614408 | tf_op jit(solution)/shard_map/ppermute | solution.py:459
  48.7 1.1 %collective-permute-start.13 = (bf16[2,256,256]{2,1,0:T(8,128)(2,1)S(1)}, bf16[2,256,256]{2,1,0:T(8,128)(2,1)S(1)}, u32[]{:S(2)}, u32[]{:S(2)}) collective-permute-start(bf16[2,256,256]{2,1,0:T(8,128)(2,1)S(1)} %get-tuple-element.84), channel_id=1, source_target_pairs={{0,8},{1,9},{2,10},{3,11},{4,12},{5,13},{6,14},{7,15},{8,0},{9,1},... | collective-permute-start | bytes 786440 | tf_op jit(solution)/shard_map/ppermute | solution.py:459
  49.8 1.5 %collective-permute-start.10 = (bf16[400,256]{1,0:T(8,128)(2,1)S(1)}, bf16[400,256]{1,0:T(8,128)(2,1)S(1)}, u32[]{:S(2)}, u32[]{:S(2)}) collective-permute-start(bf16[400,256]{1,0:T(8,128)(2,1)S(1)} %get-tuple-element.79), channel_id=1, source_target_pairs={{0,4},{1,5},{2,6},{3,7},{4,0},{5,1},{6,2},{7,3},{8,12},{9,13},{10,... | collective-permute-start | bytes 614408 | tf_op jit(solution)/shard_map/ppermute | solution.py:459
  51.8 1.5 %collective-permute-start.20 = (bf16[2,256,256]{2,1,0:T(8,128)(2,1)S(1)}, bf16[2,256,256]{2,1,0:T(8,128)(2,1)S(1)}, u32[]{:S(2)}, u32[]{:S(2)}) collective-permute-start(bf16[2,256,256]{2,1,0:T(8,128)(2,1)S(1)} %get-tuple-element.92), channel_id=1, source_target_pairs={{0,4},{1,5},{2,6},{3,7},{4,0},{5,1},{6,2},{7,3},{8,12},{9,13},{10,... | collective-permute-start | bytes 786440 | tf_op jit(solution)/shard_map/ppermute | solution.py:459
  53.4 1.7 %collective-permute-done.9.refs_0_ = bf16[400,256]{1,0:T(8,128)(2,1)S(1)} collective-permute-done((bf16[400,256]{1,0:T(8,128)(2,1)S(1)}, bf16[400,256]{1,0:T(8,128)(2,1)S(1)}, u32[]{:S(2)}, u32[]{:S(2)}) %collective-permute-start.9) | collective-permute-done | bytes 204832 | tf_op jit(solution)/shard_map/ppermute | solution.py:459
  55.1 2.0 %collective-permute-start.21 = (bf16[2,256,256]{2,1,0:T(8,128)(2,1)S(1)}, bf16[2,256,256]{2,1,0:T(8,128)(2,1)S(1)}, u32[]{:S(2)}, u32[]{:S(2)}) collective-permute-start(bf16[2,256,256]{2,1,0:T(8,128)(2,1)S(1)} %get-tuple-element.93), channel_id=1, source_target_pairs={{0,12},{1,13},{2,14},{3,15},{4,8},{5,9},{6,10},{7,11},{8,4},{9,5},... | collective-permute-start | bytes 786440 | tf_op jit(solution)/shard_map/ppermute | solution.py:459
  57.1 10.8 %collective-permute-done.10.refs_1_ = bf16[400,256]{1,0:T(8,128)(2,1)S(1)} collective-permute-done((bf16[400,256]{1,0:T(8,128)(2,1)S(1)}, bf16[400,256]{1,0:T(8,128)(2,1)S(1)}, u32[]{:S(2)}, u32[]{:S(2)}) %collective-permute-start.10) | collective-permute-done | bytes 204832 | tf_op jit(solution)/shard_map/ppermute | solution.py:459
  67.9 0.6 fold1.1
  68.5 1.1 %collective-permute-start.14 = (bf16[112,256]{1,0:T(8,128)(2,1)S(1)}, bf16[112,256]{1,0:T(8,128)(2,1)S(1)}, u32[]{:S(2)}, u32[]{:S(2)}) collective-permute-start(bf16[112,256]{1,0:T(8,128)(2,1)S(1)} %get-tuple-element.87), channel_id=1, source_target_pairs={{0,8},{1,9},{2,10},{3,11},{4,12},{5,13},{6,14},{7,15},{8,0},{9,1},... | collective-permute-start | bytes 172040 | tf_op jit(solution)/shard_map/ppermute | solution.py:459
  69.6 2.6 %collective-permute-start.15 = (bf16[112,256]{1,0:T(8,128)(2,1)S(1)}, bf16[112,256]{1,0:T(8,128)(2,1)S(1)}, u32[]{:S(2)}, u32[]{:S(2)}) collective-permute-start(bf16[112,256]{1,0:T(8,128)(2,1)S(1)} %get-tuple-element.88), channel_id=1, source_target_pairs={{0,16},{1,17},{2,18},{3,19},{4,20},{5,21},{6,22},{7,23},{8,24},{9,... | collective-permute-start | bytes 172040 | tf_op jit(solution)/shard_map/ppermute | solution.py:459
  72.2 1.1 %collective-permute-start.16 = (bf16[112,256]{1,0:T(8,128)(2,1)S(1)}, bf16[112,256]{1,0:T(8,128)(2,1)S(1)}, u32[]{:S(2)}, u32[]{:S(2)}) collective-permute-start(bf16[112,256]{1,0:T(8,128)(2,1)S(1)} %get-tuple-element.89), channel_id=1, source_target_pairs={{0,24},{1,25},{2,26},{3,27},{4,28},{5,29},{6,30},{7,31},{8,16},{9,... | collective-permute-start | bytes 172040 | tf_op jit(solution)/shard_map/ppermute | solution.py:459
  73.3 1.3 %collective-permute-done.15.refs_1_ = bf16[112,256]{1,0:T(8,128)(2,1)S(1)} collective-permute-done((bf16[112,256]{1,0:T(8,128)(2,1)S(1)}, bf16[112,256]{1,0:T(8,128)(2,1)S(1)}, u32[]{:S(2)}, u32[]{:S(2)}) %collective-permute-start.15) | collective-permute-done | bytes 57376 | tf_op jit(solution)/shard_map/ppermute | solution.py:459
  74.6 3.5 %collective-permute-done.16.refs_2_ = bf16[112,256]{1,0:T(8,128)(2,1)S(1)} collective-permute-done((bf16[112,256]{1,0:T(8,128)(2,1)S(1)}, bf16[112,256]{1,0:T(8,128)(2,1)S(1)}, u32[]{:S(2)}, u32[]{:S(2)}) %collective-permute-start.16) | collective-permute-done | bytes 57376 | tf_op jit(solution)/shard_map/ppermute | solution.py:459
  78.2 0.6 last.1
  78.8 1.3 %collect.1 = (f32[256,256]{1,0:T(8,128)S(1)}, f32[256,256]{1,0:T(8,128)S(1)}, bf16[512,256]{1,0:T(8,128)(2,1)S(1)}) custom-call(s32[6]{0:T(128)S(1)} %stack.28.place_ref, s32[8,256]{1,0:T(8,128)S(1)} %get-tuple-element.56.asked_ref, bf16[96,256]{1,0:T(8,128)(2,1)S(1)} %get-tuple-element.90.after_ref.refs_0_, ...), custom_call_target="tpu_custom_call" | custom-call | tf_op jit(solution)/shard_map/collect/pallas_call | solution.py:595
  80.1 0.6 collective-permute-start.22
  80.7 1.2 %collective-permute-start.19 = (bf16[96,256]{1,0:T(8,128)(2,1)S(1)}, bf16[96,256]{1,0:T(8,128)(2,1)S(1)}, u32[]{:S(2)}, u32[]{:S(2)}) collective-permute-start(bf16[96,256]{1,0:T(8,128)(2,1)S(1)} %get-tuple-element.90.after_ref.refs_0_), channel_id=1, source_target_pairs={{0,24},{1,25},{2,26},{3,27},{4,28},{5,29},{6,30},{7,31},{8,16},{9,... | collective-permute-start | bytes 147464 | tf_op jit(solution)/shard_map/ppermute | solution.py:459
  82.1 3.0 %collective-permute-start.17 = (bf16[96,256]{1,0:T(8,128)(2,1)S(1)}, bf16[96,256]{1,0:T(8,128)(2,1)S(1)}, u32[]{:S(2)}, u32[]{:S(2)}) collective-permute-start(bf16[96,256]{1,0:T(8,128)(2,1)S(1)} %get-tuple-element.90.after_ref.refs_0_), channel_id=1, source_target_pairs={{0,8},{1,9},{2,10},{3,11},{4,12},{5,13},{6,14},{7,15},{8,0},{9,1},... | collective-permute-start | bytes 147464 | tf_op jit(solution)/shard_map/ppermute | solution.py:459
  85.1 1.5 %collective-permute-done.19.refs_3_ = bf16[96,256]{1,0:T(8,128)(2,1)S(1)} collective-permute-done((bf16[96,256]{1,0:T(8,128)(2,1)S(1)}, bf16[96,256]{1,0:T(8,128)(2,1)S(1)}, u32[]{:S(2)}, u32[]{:S(2)}) %collective-permute-start.19) | collective-permute-done | bytes 49184 | tf_op jit(solution)/shard_map/ppermute | solution.py:459
  86.6 1.1 %collective-permute-done.18.refs_2_ = bf16[96,256]{1,0:T(8,128)(2,1)S(1)} collective-permute-done((bf16[96,256]{1,0:T(8,128)(2,1)S(1)}, bf16[96,256]{1,0:T(8,128)(2,1)S(1)}, u32[]{:S(2)}, u32[]{:S(2)}) %collective-permute-start.18) | collective-permute-done | bytes 49184 | tf_op jit(solution)/shard_map/ppermute | solution.py:459
  87.8 2.3 %collective-permute-start.28 = (bf16[384,256]{1,0:T(8,128)(2,1)S(1)}, bf16[384,256]{1,0:T(8,128)(2,1)S(1)}, u32[]{:S(2)}, u32[]{:S(2)}) collective-permute-start(bf16[384,256]{1,0:T(8,128)(2,1)S(1)} %get-tuple-element.97.refs_0_), channel_id=1, source_target_pairs={{0,5},{1,4},{2,7},{3,6},{4,1},{5,0},{6,3},{7,2},{8,13},{9,12},{10,... | collective-permute-start | bytes 589832 | tf_op jit(solution)/shard_map/ppermute | solution.py:459
  90.1 0.7 collective-permute-start.26
  91.3 1.3 %collective-permute-start.30 = (bf16[256,256]{1,0:T(8,128)(2,1)S(1)}, bf16[256,256]{1,0:T(8,128)(2,1)S(1)}, u32[]{:S(2)}, u32[]{:S(2)}) collective-permute-start(bf16[256,256]{1,0:T(8,128)(2,1)S(1)} %get-tuple-element.102), channel_id=1, source_target_pairs={{0,16},{1,17},{2,18},{3,19},{4,20},{5,21},{6,22},{7,23},{8,24},{9,... | collective-permute-start | bytes 393224 | tf_op jit(solution)/shard_map/ppermute | solution.py:459
  92.6 1.9 %collective-permute-done.28.refs_3_.refs_0_ = bf16[384,256]{1,0:T(8,128)(2,1)S(1)} collective-permute-done((bf16[384,256]{1,0:T(8,128)(2,1)S(1)}, bf16[384,256]{1,0:T(8,128)(2,1)S(1)}, u32[]{:S(2)}, u32[]{:S(2)}) %collective-permute-start.28) | collective-permute-done | bytes 196640 | tf_op jit(solution)/shard_map/ppermute | solution.py:459
  94.5 2.0 %collective-permute-done.26.refs_2_ = bf16[384,256]{1,0:T(8,128)(2,1)S(1)} collective-permute-done((bf16[384,256]{1,0:T(8,128)(2,1)S(1)}, bf16[384,256]{1,0:T(8,128)(2,1)S(1)}, u32[]{:S(2)}, u32[]{:S(2)}) %collective-permute-start.26) | collective-permute-done | bytes 196640 | tf_op jit(solution)/shard_map/ppermute | solution.py:459
  97.2 1.6 %collective-permute-start.31 = (bf16[256,256]{1,0:T(8,128)(2,1)S(1)}, bf16[256,256]{1,0:T(8,128)(2,1)S(1)}, u32[]{:S(2)}, u32[]{:S(2)}) collective-permute-start(bf16[256,256]{1,0:T(8,128)(2,1)S(1)} %share.1.refs_0_), channel_id=1, source_target_pairs={{0,1},{1,0},{2,3},{3,2},{4,5},{5,4},{6,7},{7,6},{8,9},{9,8},{10,11... | collective-permute-start | bytes 393224 | tf_op jit(solution)/shard_map/ppermute | solution.py:459
  98.8 1.7 %finish0.1.refs_4_ = f32[3072,256]{1,0:T(8,128)} custom-call(s32[6]{0:T(128)S(1)} %stack.28.place_ref, bf16[384,256]{1,0:T(8,128)(2,1)S(1)} %get-tuple-element.97.refs_0_, bf16[384,256]{1,0:T(8,128)(2,1)S(1)} %collective-permute-done.24.refs_1_, bf16[384,256]{1,0:T(8,128)(2,1)S(1)} %collective-permute-done.26.refs_2_, ...), custom_call_target="tpu_custom_call" | custom-call | tf_op jit(solution)/shard_map/finish0/pallas_call | solution.py:634
  100.6 1.7 %finish1.1 = (f32[3072,256]{1,0:T(8,128)}, f32[8,128]{1,0:T(8,128)S(1)}) custom-call(s32[6]{0:T(128)S(1)} %stack.28.place_ref, bf16[384,256]{1,0:T(8,128)(2,1)S(1)} %collective-permute-done.23.refs_0_, bf16[384,256]{1,0:T(8,128)(2,1)S(1)} %collective-permute-done.25.refs_1_, ...), custom_call_target="tpu_custom_call", output_to_operand_aliasing={{0}: (5, {})} | custom-call | tf_op jit(solution)/shard_map/finish1/pallas_call | solution.py:643
  102.3 0.6 collective-permute-done.31.refs_1_
  103.0 1.4 %table.1 = f32[512,256]{1,0:T(8,128)} custom-call(s32[6]{0:T(128)S(1)} %stack.28.place_ref, f32[8,128]{1,0:T(8,128)S(1)} %get-tuple-element.100.after_ref, bf16[256,256]{1,0:T(8,128)(2,1)S(1)} %share.1.refs_0_, bf16[256,256]{1,0:T(8,128)(2,1)S(1)} %collective-permute-done.31.refs_1_), custom_call_target="tpu_custom_call" | custom-call | tf_op jit(solution)/shard_map/table/pallas_call | solution.py:653
  (38 shorter events, 4.8 us)
Async XLA Ops:
  0.6 16.3 %collective-permute-start = (bf16[512,256]{1,0:T(8,128)(2,1)}, bf16[512,256]{1,0:T(8,128)(2,1)S(1)}, u32[]{:S(2)}, u32[]{:S(2)}) collective-permute-start(bf16[512,256]{1,0:T(8,128)(2,1)} %table_hbm.1), channel_id=1, source_target_pairs={{0,16},{1,17},{2,18},{3,19},{4,20},{5,21},{6,22},{7,23},{8,24},{9,... | collective-permute-start | bytes 786440 | tf_op jit(solution)/shard_map/ppermute | solution.py:459
  17.6 7.4 %collective-permute-start.1 = (bf16[256,256]{1,0:T(8,128)(2,1)S(1)}, bf16[256,256]{1,0:T(8,128)(2,1)S(1)}, u32[]{:S(2)}, u32[]{:S(2)}) collective-permute-start(bf16[256,256]{1,0:T(8,128)(2,1)S(1)} %get-tuple-element.66), channel_id=1, source_target_pairs={{0,12},{1,13},{2,14},{3,15},{4,8},{5,9},{6,10},{7,11},{8,4},{9,5},... | collective-permute-start | bytes 393224 | tf_op jit(solution)/shard_map/ppermute | solution.py:459
  19.3 7.2 %collective-permute-start.2 = (bf16[256,256]{1,0:T(8,128)(2,1)S(1)}, bf16[256,256]{1,0:T(8,128)(2,1)S(1)}, u32[]{:S(2)}, u32[]{:S(2)}) collective-permute-start(bf16[256,256]{1,0:T(8,128)(2,1)S(1)} %get-tuple-element.67), channel_id=1, source_target_pairs={{0,8},{1,9},{2,10},{3,11},{4,12},{5,13},{6,14},{7,15},{8,0},{9,1},... | collective-permute-start | bytes 393224 | tf_op jit(solution)/shard_map/ppermute | solution.py:459
  20.7 7.1 %collective-permute-start.3 = (bf16[256,256]{1,0:T(8,128)(2,1)S(1)}, bf16[256,256]{1,0:T(8,128)(2,1)S(1)}, u32[]{:S(2)}, u32[]{:S(2)}) collective-permute-start(bf16[256,256]{1,0:T(8,128)(2,1)S(1)} %get-tuple-element.68), channel_id=1, source_target_pairs={{0,4},{1,5},{2,6},{3,7},{4,0},{5,1},{6,2},{7,3},{8,12},{9,13},{10,... | collective-permute-start | bytes 393224 | tf_op jit(solution)/shard_map/ppermute | solution.py:459
  21.1 7.7 %collective-permute-start.4 = (bf16[256,256]{1,0:T(8,128)(2,1)S(1)}, bf16[256,256]{1,0:T(8,128)(2,1)S(1)}, u32[]{:S(2)}, u32[]{:S(2)}) collective-permute-start(bf16[256,256]{1,0:T(8,128)(2,1)S(1)} %get-tuple-element.69), channel_id=1, source_target_pairs={{0,14},{1,15},{2,12},{3,13},{4,10},{5,11},{6,8},{7,9},{8,6},{9,7},... | collective-permute-start | bytes 393224 | tf_op jit(solution)/shard_map/ppermute | solution.py:459
  21.6 9.2 %collective-permute-start.5 = (bf16[256,256]{1,0:T(8,128)(2,1)S(1)}, bf16[256,256]{1,0:T(8,128)(2,1)S(1)}, u32[]{:S(2)}, u32[]{:S(2)}) collective-permute-start(bf16[256,256]{1,0:T(8,128)(2,1)S(1)} %get-tuple-element.70), channel_id=1, source_target_pairs={{0,10},{1,11},{2,8},{3,9},{4,14},{5,15},{6,12},{7,13},{8,2},{9,3},... | collective-permute-start | bytes 393224 | tf_op jit(solution)/shard_map/ppermute | solution.py:459
  24.9 7.1 %collective-permute-start.6 = (bf16[256,256]{1,0:T(8,128)(2,1)S(1)}, bf16[256,256]{1,0:T(8,128)(2,1)S(1)}, u32[]{:S(2)}, u32[]{:S(2)}) collective-permute-start(bf16[256,256]{1,0:T(8,128)(2,1)S(1)} %get-tuple-element.71), channel_id=1, source_target_pairs={{0,6},{1,7},{2,4},{3,5},{4,2},{5,3},{6,0},{7,1},{8,14},{9,15},{10,... | collective-permute-start | bytes 393224 | tf_op jit(solution)/shard_map/ppermute | solution.py:459
  26.5 5.5 %collective-permute-start.7 = (bf16[256,256]{1,0:T(8,128)(2,1)S(1)}, bf16[256,256]{1,0:T(8,128)(2,1)S(1)}, u32[]{:S(2)}, u32[]{:S(2)}) collective-permute-start(bf16[256,256]{1,0:T(8,128)(2,1)S(1)} %get-tuple-element.72), channel_id=1, source_target_pairs={{0,2},{1,3},{2,0},{3,1},{4,6},{5,7},{6,4},{7,5},{8,10},{9,11},{10,... | collective-permute-start | bytes 393224 | tf_op jit(solution)/shard_map/ppermute | solution.py:459
  44.0 2.4 %collective-permute-start.8 = (bf16[1552,256]{1,0:T(8,128)(2,1)S(1)}, bf16[1552,256]{1,0:T(8,128)(2,1)S(1)}, u32[]{:S(2)}, u32[]{:S(2)}) collective-permute-start(bf16[1552,256]{1,0:T(8,128)(2,1)S(1)} %get-tuple-element.75), channel_id=1, source_target_pairs={{0,2},{1,3},{2,0},{3,1},{4,6},{5,7},{6,4},{7,5},{8,10},{9,11},{10,... | collective-permute-start | bytes 2383880 | tf_op jit(solution)/shard_map/ppermute | solution.py:459
  45.0 3.6 %collective-permute-start.12 = (bf16[4,256,256]{2,1,0:T(8,128)(2,1)S(1)}, bf16[4,256,256]{2,1,0:T(8,128)(2,1)S(1)}, u32[]{:S(2)}, u32[]{:S(2)}) collective-permute-start(bf16[4,256,256]{2,1,0:T(8,128)(2,1)S(1)} %get-tuple-element.83), channel_id=1, source_target_pairs={{0,2},{1,3},{2,0},{3,1},{4,6},{5,7},{6,4},{7,5},{8,10},{9,11},{10,... | collective-permute-start | bytes 1572872 | tf_op jit(solution)/shard_map/ppermute | solution.py:459
  47.1 8.0 %collective-permute-start.9 = (bf16[400,256]{1,0:T(8,128)(2,1)S(1)}, bf16[400,256]{1,0:T(8,128)(2,1)S(1)}, u32[]{:S(2)}, u32[]{:S(2)}) collective-permute-start(bf16[400,256]{1,0:T(8,128)(2,1)S(1)} %get-tuple-element.78), channel_id=1, source_target_pairs={{0,1},{1,0},{2,3},{3,2},{4,5},{5,4},{6,7},{7,6},{8,9},{9,8},{10,11... | collective-permute-start | bytes 614408 | tf_op jit(solution)/shard_map/ppermute | solution.py:459
  48.7 19.1 %collective-permute-start.13 = (bf16[2,256,256]{2,1,0:T(8,128)(2,1)S(1)}, bf16[2,256,256]{2,1,0:T(8,128)(2,1)S(1)}, u32[]{:S(2)}, u32[]{:S(2)}) collective-permute-start(bf16[2,256,256]{2,1,0:T(8,128)(2,1)S(1)} %get-tuple-element.84), channel_id=1, source_target_pairs={{0,8},{1,9},{2,10},{3,11},{4,12},{5,13},{6,14},{7,15},{8,0},{9,1},... | collective-permute-start | bytes 786440 | tf_op jit(solution)/shard_map/ppermute | solution.py:459
  49.8 18.0 %collective-permute-start.10 = (bf16[400,256]{1,0:T(8,128)(2,1)S(1)}, bf16[400,256]{1,0:T(8,128)(2,1)S(1)}, u32[]{:S(2)}, u32[]{:S(2)}) collective-permute-start(bf16[400,256]{1,0:T(8,128)(2,1)S(1)} %get-tuple-element.79), channel_id=1, source_target_pairs={{0,4},{1,5},{2,6},{3,7},{4,0},{5,1},{6,2},{7,3},{8,12},{9,13},{10,... | collective-permute-start | bytes 614408 | tf_op jit(solution)/shard_map/ppermute | solution.py:459
  51.4 16.5 %collective-permute-start.11 = (bf16[400,256]{1,0:T(8,128)(2,1)S(1)}, bf16[400,256]{1,0:T(8,128)(2,1)S(1)}, u32[]{:S(2)}, u32[]{:S(2)}) collective-permute-start(bf16[400,256]{1,0:T(8,128)(2,1)S(1)} %get-tuple-element.80), channel_id=1, source_target_pairs={{0,5},{1,4},{2,7},{3,6},{4,1},{5,0},{6,3},{7,2},{8,13},{9,12},{10,... | collective-permute-start | bytes 614408 | tf_op jit(solution)/shard_map/ppermute | solution.py:459
  51.8 26.9 %collective-permute-start.20 = (bf16[2,256,256]{2,1,0:T(8,128)(2,1)S(1)}, bf16[2,256,256]{2,1,0:T(8,128)(2,1)S(1)}, u32[]{:S(2)}, u32[]{:S(2)}) collective-permute-start(bf16[2,256,256]{2,1,0:T(8,128)(2,1)S(1)} %get-tuple-element.92), channel_id=1, source_target_pairs={{0,4},{1,5},{2,6},{3,7},{4,0},{5,1},{6,2},{7,3},{8,12},{9,13},{10,... | collective-permute-start | bytes 786440 | tf_op jit(solution)/shard_map/ppermute | solution.py:459
  55.1 23.7 %collective-permute-start.21 = (bf16[2,256,256]{2,1,0:T(8,128)(2,1)S(1)}, bf16[2,256,256]{2,1,0:T(8,128)(2,1)S(1)}, u32[]{:S(2)}, u32[]{:S(2)}) collective-permute-start(bf16[2,256,256]{2,1,0:T(8,128)(2,1)S(1)} %get-tuple-element.93), channel_id=1, source_target_pairs={{0,12},{1,13},{2,14},{3,15},{4,8},{5,9},{6,10},{7,11},{8,4},{9,5},... | collective-permute-start | bytes 786440 | tf_op jit(solution)/shard_map/ppermute | solution.py:459
  68.5 4.8 %collective-permute-start.14 = (bf16[112,256]{1,0:T(8,128)(2,1)S(1)}, bf16[112,256]{1,0:T(8,128)(2,1)S(1)}, u32[]{:S(2)}, u32[]{:S(2)}) collective-permute-start(bf16[112,256]{1,0:T(8,128)(2,1)S(1)} %get-tuple-element.87), channel_id=1, source_target_pairs={{0,8},{1,9},{2,10},{3,11},{4,12},{5,13},{6,14},{7,15},{8,0},{9,1},... | collective-permute-start | bytes 172040 | tf_op jit(solution)/shard_map/ppermute | solution.py:459
  69.6 5.1 %collective-permute-start.15 = (bf16[112,256]{1,0:T(8,128)(2,1)S(1)}, bf16[112,256]{1,0:T(8,128)(2,1)S(1)}, u32[]{:S(2)}, u32[]{:S(2)}) collective-permute-start(bf16[112,256]{1,0:T(8,128)(2,1)S(1)} %get-tuple-element.88), channel_id=1, source_target_pairs={{0,16},{1,17},{2,18},{3,19},{4,20},{5,21},{6,22},{7,23},{8,24},{9,... | collective-permute-start | bytes 172040 | tf_op jit(solution)/shard_map/ppermute | solution.py:459
  72.2 6.0 %collective-permute-start.16 = (bf16[112,256]{1,0:T(8,128)(2,1)S(1)}, bf16[112,256]{1,0:T(8,128)(2,1)S(1)}, u32[]{:S(2)}, u32[]{:S(2)}) collective-permute-start(bf16[112,256]{1,0:T(8,128)(2,1)S(1)} %get-tuple-element.89), channel_id=1, source_target_pairs={{0,24},{1,25},{2,26},{3,27},{4,28},{5,29},{6,30},{7,31},{8,16},{9,... | collective-permute-start | bytes 172040 | tf_op jit(solution)/shard_map/ppermute | solution.py:459
  80.1 7.6 %collective-permute-start.22 = (bf16[512,256]{1,0:T(8,128)(2,1)S(1)}, bf16[512,256]{1,0:T(8,128)(2,1)S(1)}, u32[]{:S(2)}, u32[]{:S(2)}) collective-permute-start(bf16[512,256]{1,0:T(8,128)(2,1)S(1)} %get-tuple-element.96), channel_id=1, source_target_pairs={{0,1},{1,0},{2,3},{3,2},{4,5},{5,4},{6,7},{7,6},{8,9},{9,8},{10,11... | collective-permute-start | bytes 786440 | tf_op jit(solution)/shard_map/ppermute | solution.py:459
  80.7 5.9 %collective-permute-start.19 = (bf16[96,256]{1,0:T(8,128)(2,1)S(1)}, bf16[96,256]{1,0:T(8,128)(2,1)S(1)}, u32[]{:S(2)}, u32[]{:S(2)}) collective-permute-start(bf16[96,256]{1,0:T(8,128)(2,1)S(1)} %get-tuple-element.90.after_ref.refs_0_), channel_id=1, source_target_pairs={{0,24},{1,25},{2,26},{3,27},{4,28},{5,29},{6,30},{7,31},{8,16},{9,... | collective-permute-start | bytes 147464 | tf_op jit(solution)/shard_map/ppermute | solution.py:459
  82.0 5.7 %collective-permute-start.18 = (bf16[96,256]{1,0:T(8,128)(2,1)S(1)}, bf16[96,256]{1,0:T(8,128)(2,1)S(1)}, u32[]{:S(2)}, u32[]{:S(2)}) collective-permute-start(bf16[96,256]{1,0:T(8,128)(2,1)S(1)} %get-tuple-element.90.after_ref.refs_0_), channel_id=1, source_target_pairs={{0,16},{1,17},{2,18},{3,19},{4,20},{5,21},{6,22},{7,23},{8,24},{9,... | collective-permute-start | bytes 147464 | tf_op jit(solution)/shard_map/ppermute | solution.py:459
  82.1 5.6 %collective-permute-start.17 = (bf16[96,256]{1,0:T(8,128)(2,1)S(1)}, bf16[96,256]{1,0:T(8,128)(2,1)S(1)}, u32[]{:S(2)}, u32[]{:S(2)}) collective-permute-start(bf16[96,256]{1,0:T(8,128)(2,1)S(1)} %get-tuple-element.90.after_ref.refs_0_), channel_id=1, source_target_pairs={{0,8},{1,9},{2,10},{3,11},{4,12},{5,13},{6,14},{7,15},{8,0},{9,1},... | collective-permute-start | bytes 147464 | tf_op jit(solution)/shard_map/ppermute | solution.py:459
  87.8 6.7 %collective-permute-start.28 = (bf16[384,256]{1,0:T(8,128)(2,1)S(1)}, bf16[384,256]{1,0:T(8,128)(2,1)S(1)}, u32[]{:S(2)}, u32[]{:S(2)}) collective-permute-start(bf16[384,256]{1,0:T(8,128)(2,1)S(1)} %get-tuple-element.97.refs_0_), channel_id=1, source_target_pairs={{0,5},{1,4},{2,7},{3,6},{4,1},{5,0},{6,3},{7,2},{8,13},{9,12},{10,... | collective-permute-start | bytes 589832 | tf_op jit(solution)/shard_map/ppermute | solution.py:459
  90.1 6.4 %collective-permute-start.26 = (bf16[384,256]{1,0:T(8,128)(2,1)S(1)}, bf16[384,256]{1,0:T(8,128)(2,1)S(1)}, u32[]{:S(2)}, u32[]{:S(2)}) collective-permute-start(bf16[384,256]{1,0:T(8,128)(2,1)S(1)} %get-tuple-element.97.refs_0_), channel_id=1, source_target_pairs={{0,4},{1,5},{2,6},{3,7},{4,0},{5,1},{6,2},{7,3},{8,12},{9,13},{10,... | collective-permute-start | bytes 589832 | tf_op jit(solution)/shard_map/ppermute | solution.py:459
  90.8 6.2 %collective-permute-start.24 = (bf16[384,256]{1,0:T(8,128)(2,1)S(1)}, bf16[384,256]{1,0:T(8,128)(2,1)S(1)}, u32[]{:S(2)}, u32[]{:S(2)}) collective-permute-start(bf16[384,256]{1,0:T(8,128)(2,1)S(1)} %get-tuple-element.97.refs_0_), channel_id=1, source_target_pairs={{0,1},{1,0},{2,3},{3,2},{4,5},{5,4},{6,7},{7,6},{8,9},{9,8},{10,11... | collective-permute-start | bytes 589832 | tf_op jit(solution)/shard_map/ppermute | solution.py:459
  91.3 5.9 %collective-permute-start.30 = (bf16[256,256]{1,0:T(8,128)(2,1)S(1)}, bf16[256,256]{1,0:T(8,128)(2,1)S(1)}, u32[]{:S(2)}, u32[]{:S(2)}) collective-permute-start(bf16[256,256]{1,0:T(8,128)(2,1)S(1)} %get-tuple-element.102), channel_id=1, source_target_pairs={{0,16},{1,17},{2,18},{3,19},{4,20},{5,21},{6,22},{7,23},{8,24},{9,... | collective-permute-start | bytes 393224 | tf_op jit(solution)/shard_map/ppermute | solution.py:459
  92.6 7.9 %collective-permute-start.23 = (bf16[384,256]{1,0:T(8,128)(2,1)S(1)}, bf16[384,256]{1,0:T(8,128)(2,1)S(1)}, u32[]{:S(2)}, u32[]{:S(2)}) collective-permute-start(bf16[384,256]{1,0:T(8,128)(2,1)S(1)} %get-tuple-element.97.refs_0_), channel_id=1, source_target_pairs={{0,2},{1,3},{2,0},{3,1},{4,6},{5,7},{6,4},{7,5},{8,10},{9,11},{10,... | collective-permute-start | bytes 589832 | tf_op jit(solution)/shard_map/ppermute | solution.py:459
  94.5 6.1 %collective-permute-start.29 = (bf16[384,256]{1,0:T(8,128)(2,1)S(1)}, bf16[384,256]{1,0:T(8,128)(2,1)S(1)}, u32[]{:S(2)}, u32[]{:S(2)}) collective-permute-start(bf16[384,256]{1,0:T(8,128)(2,1)S(1)} %collective-permute-done.28.refs_3_.refs_0_), channel_id=1, source_target_pairs={{0,2},{1,3},{2,0},{3,1},{4,6},{5,7},{6,4},{7,5},{8,10},{9,11},{10,... | collective-permute-start | bytes 589832 | tf_op jit(solution)/shard_map/ppermute | solution.py:459
  96.5 4.0 %collective-permute-start.27 = (bf16[384,256]{1,0:T(8,128)(2,1)S(1)}, bf16[384,256]{1,0:T(8,128)(2,1)S(1)}, u32[]{:S(2)}, u32[]{:S(2)}) collective-permute-start(bf16[384,256]{1,0:T(8,128)(2,1)S(1)} %collective-permute-done.26.refs_2_), channel_id=1, source_target_pairs={{0,2},{1,3},{2,0},{3,1},{4,6},{5,7},{6,4},{7,5},{8,10},{9,11},{10,... | collective-permute-start | bytes 589832 | tf_op jit(solution)/shard_map/ppermute | solution.py:459
  97.0 3.6 %collective-permute-start.25 = (bf16[384,256]{1,0:T(8,128)(2,1)S(1)}, bf16[384,256]{1,0:T(8,128)(2,1)S(1)}, u32[]{:S(2)}, u32[]{:S(2)}) collective-permute-start(bf16[384,256]{1,0:T(8,128)(2,1)S(1)} %collective-permute-done.24.refs_1_), channel_id=1, source_target_pairs={{0,2},{1,3},{2,0},{3,1},{4,6},{5,7},{6,4},{7,5},{8,10},{9,11},{10,... | collective-permute-start | bytes 589832 | tf_op jit(solution)/shard_map/ppermute | solution.py:459
  97.2 5.7 %collective-permute-start.31 = (bf16[256,256]{1,0:T(8,128)(2,1)S(1)}, bf16[256,256]{1,0:T(8,128)(2,1)S(1)}, u32[]{:S(2)}, u32[]{:S(2)}) collective-permute-start(bf16[256,256]{1,0:T(8,128)(2,1)S(1)} %share.1.refs_0_), channel_id=1, source_target_pairs={{0,1},{1,0},{2,3},{3,2},{4,5},{5,4},{6,7},{7,6},{8,9},{9,8},{10,11... | collective-permute-start | bytes 393224 | tf_op jit(solution)/shard_map/ppermute | solution.py:459

commit v2 on v1

--- a/solution.py
+++ b/solution.py
@@ -10,7 +10,7 @@
 
 MB = 2
 TILE = 128
-CHUNK = 256
+CHUNK = 128
 PAD = 16
 GROUP = 16
 F32 = jnp.float32
@@ -39,9 +39,10 @@
 
 
 def ordered(near):
-    top = near // 2
-    steps = sorted(range(1, near), key=lambda step: (step < 2, step & 1, step < top, step < top + 2))
-    return [0] + steps
+    return [0] + sorted(
+        range(1, near),
+        key=lambda step: (bin(step).count("1") != 1, not step & 2 or step < 4, step),
+    )
 
 
 def returning(chips):
@@ -155,13 +156,16 @@
 
 
 def stack_kernel(
-    place_ref, column_ref, weight_ref, gain_hbm, upstream_hbm, *refs,
+    place_ref, column_ref, weight_hbm, gain_hbm, upstream_hbm, *refs,
 ):
-    arrived_refs, refs = refs[:-18], refs[-18:]
-    gain_ref, upstream_ref, sems = refs[15:]
+    arrived_refs, refs = refs[:-19], refs[-19:]
+    gain_ref, upstream_ref, weight_ref, sems = refs[15:]
     copies = [
         pltpu.make_async_copy(gain_hbm, gain_ref, sems.at[0]),
         pltpu.make_async_copy(upstream_hbm, upstream_ref, sems.at[1]),
+    ] + [
+        pltpu.make_async_copy(weight_hbm.at[layer], weight_ref.at[layer], sems.at[2 + layer])
+        for layer in range(weight_ref.shape[0])
     ]
     for copy in copies:
         copy.start()
@@ -192,11 +196,6 @@
             h_s[side, start : start + PAD, :] = jnp.zeros((PAD, width), F32)
             dconv_s[side, start + length : start + length + PAD, :] = jnp.zeros((PAD, width), F32)
     dw_s[...] = jnp.zeros(dw_s.shape, F32)
-    for layer in range(layers):
-        for start in range(0, taps, width):
-            value = weight_ref[layer, start : start + width, :]
-            rounded_s[layer, start : start + width, :] = value.astype(BF16)
-            turned_s[layer, start : start + width, :] = jnp.transpose(value).astype(BF16)
 
     copies[0].wait()
 
@@ -228,6 +227,11 @@
     root = math.sqrt(2.0 / math.pi)
     for layer in range(layers):
         dilation = 2**layer
+        copies[2 + layer].wait()
+        for start in range(0, taps, width):
+            value = weight_ref[layer, start : start + width, :]
+            rounded_s[layer, start : start + width, :] = value.astype(BF16)
+            turned_s[layer, start : start + width, :] = jnp.transpose(value).astype(BF16)
 
         for seq in range(batches):
             for j in range(per):
@@ -404,12 +408,15 @@
         copy.wait()
 
 
-def line_kernel(pieces, *refs):
-    joined_ref, near_sum_ref, far_sum_ref = refs[-3:]
+def line_kernel(*refs):
     size = refs[0].shape[0]
-    for spot, ref in enumerate(refs[:pieces]):
-        joined_ref[spot * size : (spot + 1) * size, :] = ref[...]
-    near_ref, far_ref, *shares = refs[pieces:-3]
+    for spot, ref in enumerate(refs[:-1]):
+        refs[-1][spot * size : (spot + 1) * size, :] = ref[...]
+
+
+def shares_kernel(after_ref, near_ref, far_ref, *refs):
+    del after_ref
+    shares, (near_sum_ref, far_sum_ref) = refs[:-2], refs[-2:]
     share = near_ref.shape[0]
     near_sum_ref[...] = tree([near_ref[...]] + [m[:share, :].astype(F32) for m in shares])
     far_sum_ref[...] = tree([far_ref[...]] + [m[share:, :].astype(F32) for m in shares]).astype(BF16)
@@ -513,7 +520,7 @@
             shape((half + GROUP, width), BF16),
             shape((GROUP, width), BF16),
         ),
-        in_specs=[SMEM, VMEM, VMEM, ANY, ANY] + [VMEM] * near,
+        in_specs=[SMEM, VMEM, ANY, ANY, ANY] + [VMEM] * near,
         out_specs=(VMEM,) * 4,
         scratch_shapes=[
             pltpu.VMEM((tokens, width), F32),
@@ -529,12 +536,13 @@
             pltpu.VMEM((layers, taps, width), BF16),
             pltpu.VMEM((layers, width), F32),
             pltpu.VMEM((tokens, width), BF16),
-            pltpu.SemaphoreType.DMA((2,)),
+            pltpu.VMEM((layers, taps, width), F32),
+            pltpu.SemaphoreType.DMA((2 + layers,)),
         ],
-        compiler_params=params(50),
+        compiler_params=params(40),
         name="stack",
     )(
-        place, codes.reshape(tokens, 1), conv_weight, held(gain),
+        place, codes.reshape(tokens, 1), held(conv_weight), held(gain),
         held(upstream.reshape(tokens, width)),
         *fetched,
     )
@@ -608,18 +616,22 @@
         gain_grad = gain_grad + swap(gain_grad, [bit], 1)
 
     line = [keep] + [swap(keep, stages[2], step) for step in range(1, 2 ** len(stages[2]))]
-    keep, near_share, far_share = pl.pallas_call(
-        functools.partial(line_kernel, len(line)),
-        out_shape=(
-            shape((half // 4, width), BF16),
-            shape((share, width), F32),
-            shape((share, width), BF16),
-        ),
-        in_specs=[VMEM] * (len(line) + 2 + len(shares)),
-        out_specs=(VMEM,) * 3,
+    keep = pl.pallas_call(
+        line_kernel,
+        out_shape=shape((half // 4, width), BF16),
+        in_specs=[VMEM] * len(line),
+        out_specs=VMEM,
         compiler_params=params(16),
         name="line",
-    )(*line, near_share, far_share, *shares)
+    )(*line)
+    near_share, far_share = pl.pallas_call(
+        shares_kernel,
+        out_shape=(shape((share, width), F32), shape((share, width), BF16)),
+        in_specs=[ANY] + [VMEM] * (2 + len(shares)),
+        out_specs=(VMEM,) * 2,
+        compiler_params=params(16),
+        name="shares",
+    )(keep, near_share, far_share, *shares)
     far_share = swap(far_share, across, 1)
     square = [keep] + [swap(keep, stages[1], step) for step in range(1, 4)]
     other = [swap(value, stages[0], 1) for value in square]

time: 105 us -> 104 us (level)
  waiting for transfers between devices: 34.1 us -> 35.9 us
  starting transfers between devices: 35.5 us -> 34.1 us
    ppermute x32, waiting for transfers between devices: 34.1 us -> 35.9 us  [swap(): return lax.ppermute(value, axes, [(i, i ^ mask) for i in range(devices)])]
    ppermute x32, starting transfers between devices: 35.5 us -> 34.1 us  [swap(): return lax.ppermute(value, axes, [(i, i ^ mask) for i in range(devices)])]
  transfers between devices with their start and end apart: 32 -> 32, of which waited for: 19 -> 18; matrix products, arithmetic and copies ran while one was open for 1% -> 1% of each run, Pallas kernels for 9% -> 9%
where the time goes in v2:
time: 104 us
  waiting for transfers between devices  35.9 us (35%)
  starting transfers between devices  34.1 us (33%)
  Pallas kernels  23.9 us (23%)
  blocking collectives  8.43 us (8%)
    ppermute x32, waiting for transfers between devices, swap(): return lax.ppermute(value, axes, [(i, i ^ mask) for i in range(devices)])  35.9 us
    ppermute x32, starting transfers between devices, swap(): return lax.ppermute(value, axes, [(i, i ^ mask) for i in range(devices)])  34.1 us
    pallas_call x1, Pallas kernels, body(): pl.pallas_call(stack_kernel, out_shape=(shape((tokens, width), BF16), sha...  11.4 us
    all_to_all x1, blocking collectives, exchange(): lax.all_to_all(value, 'emb', split_axis=0, concat_axis=0, axis_index_grou...  8.43 us
    pallas_call x2, Pallas kernels, body(): pl.pallas_call(functools.partial(finish_kernel, 2 ** len(stages[2]), scal...  3.49 us
  transfers between devices with their start and end apart: 32, of which 18 were waited for; matrix products, arithmetic and copies ran while one was open for 1% of the time, Pallas kernels for 9%

profile of v2, /device:TPU:0, one launch (start us, length us, event | category | flops | bytes accessed | tf_op | source)
XLA Modules:
  0.0 104.2 jit_solution(7668507824115943425)
XLA Ops:
  0.6 4.1 %collective-permute-start = (bf16[512,256]{1,0:T(8,128)(2,1)}, bf16[512,256]{1,0:T(8,128)(2,1)S(1)}, u32[]{:S(2)}, u32[]{:S(2)}) collective-permute-start(bf16[512,256]{1,0:T(8,128)(2,1)} %table_hbm.1), channel_id=1, source_target_pairs={{0,16},{1,17},{2,18},{3,19},{4,20},{5,21},{6,22},{7,23},{8,24},{9,... | collective-permute-start | bytes 786440 | tf_op jit(solution)/shard_map/ppermute | solution.py:466
  4.8 0.7 bitcast_add_fusion.ids_ref
  5.5 1.5 %request.1 = (s32[8,256]{1,0:T(8,128)S(1)}, s32[2,512]{1,0:T(2,128)S(1)}, bf16[512,256]{1,0:T(8,128)(2,1)S(1)}) custom-call(s32[6]{0:T(128)S(1)} %stack.28.place_ref, s32[2,512]{1,0:T(2,128)S(1)} %bitcast_add_fusion.ids_ref, bf16[512,256]{1,0:T(8,128)(2,1)} %table_hbm.1), custom_call_target="tpu_custom_call" | custom-call | tf_op jit(solution)/shard_map/request/pallas_call | solution.py:479
  7.0 8.4 %all_to_all.11 = s32[8,1,256]{2,1,0:T(1,128)S(1)} all-to-all(s32[8,1,256]{2,1,0:T(1,128)S(1)} %copy.14), channel_id=1, replica_groups={{0,2,4,6,8,10,12,14},{16,18,20,22,24,26,28,30},{1,3,5,7,9,11,13,15},{17..., dimensions={0} | all-to-all | bytes 16384 | tf_op jit(solution)/shard_map/all_to_all | solution.py:472
  15.5 1.1 %near.1 = (s32[8,256]{1,0:T(8,128)S(1)}, bf16[128,256]{1,0:T(8,128)(2,1)S(1)}, bf16[128,256]{1,0:T(8,128)(2,1)S(1)}, bf16[128,256]{1,0:T(8,128)(2,1)S(1)}, bf16[...) custom-call(s32[6]{0:T(128)S(1)} %stack.28.place_ref, ...), custom_call_target="tpu_custom_call" | custom-call | tf_op jit(solution)/shard_map/near/pallas_call | solution.py:493
  17.0 0.6 far.1
  17.6 1.6 %collective-permute-start.2 = (bf16[256,256]{1,0:T(8,128)(2,1)S(1)}, bf16[256,256]{1,0:T(8,128)(2,1)S(1)}, u32[]{:S(2)}, u32[]{:S(2)}) collective-permute-start(bf16[256,256]{1,0:T(8,128)(2,1)S(1)} %get-tuple-element.66), channel_id=1, source_target_pairs={{0,4},{1,5},{2,6},{3,7},{4,0},{5,1},{6,2},{7,3},{8,12},{9,13},{10,... | collective-permute-start | bytes 393224 | tf_op jit(solution)/shard_map/ppermute | solution.py:466
  19.3 0.7 collective-permute-start.3
  20.0 1.2 %collective-permute-start.4 = (bf16[256,256]{1,0:T(8,128)(2,1)S(1)}, bf16[256,256]{1,0:T(8,128)(2,1)S(1)}, u32[]{:S(2)}, u32[]{:S(2)}) collective-permute-start(bf16[256,256]{1,0:T(8,128)(2,1)S(1)} %get-tuple-element.68), channel_id=1, source_target_pairs={{0,12},{1,13},{2,14},{3,15},{4,8},{5,9},{6,10},{7,11},{8,4},{9,5},... | collective-permute-start | bytes 393224 | tf_op jit(solution)/shard_map/ppermute | solution.py:466
  21.2 0.9 collective-permute-start.5
  22.1 1.0 collective-permute-start.6
  24.3 1.4 %collective-permute-done.3.refs_3_ = bf16[256,256]{1,0:T(8,128)(2,1)S(1)} collective-permute-done((bf16[256,256]{1,0:T(8,128)(2,1)S(1)}, bf16[256,256]{1,0:T(8,128)(2,1)S(1)}, u32[]{:S(2)}, u32[]{:S(2)}) %collective-permute-start.3) | collective-permute-done | bytes 131104 | tf_op jit(solution)/shard_map/ppermute | solution.py:466
  25.6 2.8 %collective-permute-done.4.refs_4_ = bf16[256,256]{1,0:T(8,128)(2,1)S(1)} collective-permute-done((bf16[256,256]{1,0:T(8,128)(2,1)S(1)}, bf16[256,256]{1,0:T(8,128)(2,1)S(1)}, u32[]{:S(2)}, u32[]{:S(2)}) %collective-permute-start.4) | collective-permute-done | bytes 131104 | tf_op jit(solution)/shard_map/ppermute | solution.py:466
  28.4 1.3 %collective-permute-done.5.refs_5_ = bf16[256,256]{1,0:T(8,128)(2,1)S(1)} collective-permute-done((bf16[256,256]{1,0:T(8,128)(2,1)S(1)}, bf16[256,256]{1,0:T(8,128)(2,1)S(1)}, u32[]{:S(2)}, u32[]{:S(2)}) %collective-permute-start.5) | collective-permute-done | bytes 131104 | tf_op jit(solution)/shard_map/ppermute | solution.py:466
  29.7 3.0 %collective-permute-done.6.refs_6_ = bf16[256,256]{1,0:T(8,128)(2,1)S(1)} collective-permute-done((bf16[256,256]{1,0:T(8,128)(2,1)S(1)}, bf16[256,256]{1,0:T(8,128)(2,1)S(1)}, u32[]{:S(2)}, u32[]{:S(2)}) %collective-permute-start.6) | collective-permute-done | bytes 131104 | tf_op jit(solution)/shard_map/ppermute | solution.py:466
  32.6 11.4 %stack.29 = (bf16[1024,256]{1,0:T(8,128)(2,1)S(1)}, bf16[1536,256]{1,0:T(8,128)(2,1)S(1)}, bf16[1552,256]{1,0:T(8,128)(2,1)S(1)}, bf16[16,256]{1,0:T(8,128)(2,1)S(1)}) custom-call(s32[6]{0:T(128)S(1)} %stack.28.place_ref, s32[1024,1]{1,0:T(8,128)S(1)} %bitcast.18, f32[4,768,256]{2,1,0:T(8,128)} %weight_hbm.1, f32[4,256]{1,0:T(4,128)} %gain_hbm.1, ...), custom_call_target="tpu_custom_call" | custom-call | tf_op jit(solution)/shard_map/stack/pallas_call | solution.py:515
  44.6 0.9 place.1
  45.7 0.9 collective-permute-done.8.refs_0_
  46.6 0.7 fold0.1
  47.3 1.6 %collective-permute-start.9 = (bf16[400,256]{1,0:T(8,128)(2,1)S(1)}, bf16[400,256]{1,0:T(8,128)(2,1)S(1)}, u32[]{:S(2)}, u32[]{:S(2)}) collective-permute-start(bf16[400,256]{1,0:T(8,128)(2,1)S(1)} %get-tuple-element.77), channel_id=1, source_target_pairs={{0,1},{1,0},{2,3},{3,2},{4,5},{5,4},{6,7},{7,6},{8,9},{9,8},{10,11... | collective-permute-start | bytes 614408 | tf_op jit(solution)/shard_map/ppermute | solution.py:466
  48.9 1.1 %collective-permute-start.13 = (bf16[2,256,256]{2,1,0:T(8,128)(2,1)S(1)}, bf16[2,256,256]{2,1,0:T(8,128)(2,1)S(1)}, u32[]{:S(2)}, u32[]{:S(2)}) collective-permute-start(bf16[2,256,256]{2,1,0:T(8,128)(2,1)S(1)} %get-tuple-element.83), channel_id=1, source_target_pairs={{0,8},{1,9},{2,10},{3,11},{4,12},{5,13},{6,14},{7,15},{8,0},{9,1},... | collective-permute-start | bytes 786440 | tf_op jit(solution)/shard_map/ppermute | solution.py:466
  50.0 1.0 collective-permute-start.10
  51.0 1.0 collective-permute-start.11
  52.0 1.0 collective-permute-start.27
  53.1 2.2 %collective-permute-done.9.refs_0_ = bf16[400,256]{1,0:T(8,128)(2,1)S(1)} collective-permute-done((bf16[400,256]{1,0:T(8,128)(2,1)S(1)}, bf16[400,256]{1,0:T(8,128)(2,1)S(1)}, u32[]{:S(2)}, u32[]{:S(2)}) %collective-permute-start.9) | collective-permute-done | bytes 204832 | tf_op jit(solution)/shard_map/ppermute | solution.py:466
  55.3 1.5 %collective-permute-start.28 = (bf16[2,256,256]{2,1,0:T(8,128)(2,1)S(1)}, bf16[2,256,256]{2,1,0:T(8,128)(2,1)S(1)}, u32[]{:S(2)}, u32[]{:S(2)}) collective-permute-start(bf16[2,256,256]{2,1,0:T(8,128)(2,1)S(1)} %get-tuple-element.95), channel_id=1, source_target_pairs={{0,12},{1,13},{2,14},{3,15},{4,8},{5,9},{6,10},{7,11},{8,4},{9,5},... | collective-permute-start | bytes 786440 | tf_op jit(solution)/shard_map/ppermute | solution.py:466
  56.8 11.3 %collective-permute-done.10.refs_1_ = bf16[400,256]{1,0:T(8,128)(2,1)S(1)} collective-permute-done((bf16[400,256]{1,0:T(8,128)(2,1)S(1)}, bf16[400,256]{1,0:T(8,128)(2,1)S(1)}, u32[]{:S(2)}, u32[]{:S(2)}) %collective-permute-start.10) | collective-permute-done | bytes 204832 | tf_op jit(solution)/shard_map/ppermute | solution.py:466
  68.1 0.6 fold1.1
  68.7 1.0 collective-permute-start.14
  69.7 2.6 %collective-permute-start.15 = (bf16[112,256]{1,0:T(8,128)(2,1)S(1)}, bf16[112,256]{1,0:T(8,128)(2,1)S(1)}, u32[]{:S(2)}, u32[]{:S(2)}) collective-permute-start(bf16[112,256]{1,0:T(8,128)(2,1)S(1)} %get-tuple-element.87), channel_id=1, source_target_pairs={{0,16},{1,17},{2,18},{3,19},{4,20},{5,21},{6,22},{7,23},{8,24},{9,... | collective-permute-start | bytes 172040 | tf_op jit(solution)/shard_map/ppermute | solution.py:466
  72.3 0.8 collective-permute-start.16
  73.2 1.7 %collective-permute-done.15.refs_1_ = bf16[112,256]{1,0:T(8,128)(2,1)S(1)} collective-permute-done((bf16[112,256]{1,0:T(8,128)(2,1)S(1)}, bf16[112,256]{1,0:T(8,128)(2,1)S(1)}, u32[]{:S(2)}, u32[]{:S(2)}) %collective-permute-start.15) | collective-permute-done | bytes 57376 | tf_op jit(solution)/shard_map/ppermute | solution.py:466
  74.8 3.5 %collective-permute-done.16.refs_2_ = bf16[112,256]{1,0:T(8,128)(2,1)S(1)} collective-permute-done((bf16[112,256]{1,0:T(8,128)(2,1)S(1)}, bf16[112,256]{1,0:T(8,128)(2,1)S(1)}, u32[]{:S(2)}, u32[]{:S(2)}) %collective-permute-start.16) | collective-permute-done | bytes 57376 | tf_op jit(solution)/shard_map/ppermute | solution.py:466
  78.3 0.6 last.1
  78.9 1.3 %collect.1 = (f32[256,256]{1,0:T(8,128)S(1)}, f32[256,256]{1,0:T(8,128)S(1)}, bf16[512,256]{1,0:T(8,128)(2,1)S(1)}) custom-call(s32[6]{0:T(128)S(1)} %stack.28.place_ref, s32[8,256]{1,0:T(8,128)S(1)} %get-tuple-element.55.asked_ref, bf16[96,256]{1,0:T(8,128)(2,1)S(1)} %get-tuple-element.89.refs_0_.after_ref, ...), custom_call_target="tpu_custom_call" | custom-call | tf_op jit(solution)/shard_map/collect/pallas_call | solution.py:603
  80.9 1.2 %collective-permute-start.19 = (bf16[96,256]{1,0:T(8,128)(2,1)S(1)}, bf16[96,256]{1,0:T(8,128)(2,1)S(1)}, u32[]{:S(2)}, u32[]{:S(2)}) collective-permute-start(bf16[96,256]{1,0:T(8,128)(2,1)S(1)} %get-tuple-element.89.refs_0_.after_ref), channel_id=1, source_target_pairs={{0,24},{1,25},{2,26},{3,27},{4,28},{5,29},{6,30},{7,31},{8,16},{9,... | collective-permute-start | bytes 147464 | tf_op jit(solution)/shard_map/ppermute | solution.py:466
  82.0 3.2 %collective-permute-start.17 = (bf16[96,256]{1,0:T(8,128)(2,1)S(1)}, bf16[96,256]{1,0:T(8,128)(2,1)S(1)}, u32[]{:S(2)}, u32[]{:S(2)}) collective-permute-start(bf16[96,256]{1,0:T(8,128)(2,1)S(1)} %get-tuple-element.89.refs_0_.after_ref), channel_id=1, source_target_pairs={{0,8},{1,9},{2,10},{3,11},{4,12},{5,13},{6,14},{7,15},{8,0},{9,1},... | collective-permute-start | bytes 147464 | tf_op jit(solution)/shard_map/ppermute | solution.py:466
  85.2 1.5 %collective-permute-done.19.refs_3_ = bf16[96,256]{1,0:T(8,128)(2,1)S(1)} collective-permute-done((bf16[96,256]{1,0:T(8,128)(2,1)S(1)}, bf16[96,256]{1,0:T(8,128)(2,1)S(1)}, u32[]{:S(2)}, u32[]{:S(2)}) %collective-permute-start.19) | collective-permute-done | bytes 49184 | tf_op jit(solution)/shard_map/ppermute | solution.py:466
  86.8 1.0 collective-permute-done.18.refs_2_
  87.8 2.4 %collective-permute-start.25 = (bf16[384,256]{1,0:T(8,128)(2,1)S(1)}, bf16[384,256]{1,0:T(8,128)(2,1)S(1)}, u32[]{:S(2)}, u32[]{:S(2)}) collective-permute-start(bf16[384,256]{1,0:T(8,128)(2,1)S(1)} %line.1.refs_0_.after_ref), channel_id=1, source_target_pairs={{0,5},{1,4},{2,7},{3,6},{4,1},{5,0},{6,3},{7,2},{8,13},{9,12},{10,... | collective-permute-start | bytes 589832 | tf_op jit(solution)/shard_map/ppermute | solution.py:466
  90.3 0.6 collective-permute-start.23
  91.5 1.3 %collective-permute-start.30 = (bf16[256,256]{1,0:T(8,128)(2,1)S(1)}, bf16[256,256]{1,0:T(8,128)(2,1)S(1)}, u32[]{:S(2)}, u32[]{:S(2)}) collective-permute-start(bf16[256,256]{1,0:T(8,128)(2,1)S(1)} %get-tuple-element.100), channel_id=1, source_target_pairs={{0,16},{1,17},{2,18},{3,19},{4,20},{5,21},{6,22},{7,23},{8,24},{9,... | collective-permute-start | bytes 393224 | tf_op jit(solution)/shard_map/ppermute | solution.py:466
  92.7 1.8 %collective-permute-done.25.refs_3_.refs_0_ = bf16[384,256]{1,0:T(8,128)(2,1)S(1)} collective-permute-done((bf16[384,256]{1,0:T(8,128)(2,1)S(1)}, bf16[384,256]{1,0:T(8,128)(2,1)S(1)}, u32[]{:S(2)}, u32[]{:S(2)}) %collective-permute-start.25) | collective-permute-done | bytes 196640 | tf_op jit(solution)/shard_map/ppermute | solution.py:466
  94.5 2.0 %collective-permute-done.23.refs_2_ = bf16[384,256]{1,0:T(8,128)(2,1)S(1)} collective-permute-done((bf16[384,256]{1,0:T(8,128)(2,1)S(1)}, bf16[384,256]{1,0:T(8,128)(2,1)S(1)}, u32[]{:S(2)}, u32[]{:S(2)}) %collective-permute-start.23) | collective-permute-done | bytes 196640 | tf_op jit(solution)/shard_map/ppermute | solution.py:466
  97.4 1.6 %collective-permute-start.31 = (bf16[256,256]{1,0:T(8,128)(2,1)S(1)}, bf16[256,256]{1,0:T(8,128)(2,1)S(1)}, u32[]{:S(2)}, u32[]{:S(2)}) collective-permute-start(bf16[256,256]{1,0:T(8,128)(2,1)S(1)} %share.1.refs_0_), channel_id=1, source_target_pairs={{0,1},{1,0},{2,3},{3,2},{4,5},{5,4},{6,7},{7,6},{8,9},{9,8},{10,11... | collective-permute-start | bytes 393224 | tf_op jit(solution)/shard_map/ppermute | solution.py:466
  99.0 1.7 %finish0.1.refs_4_ = f32[3072,256]{1,0:T(8,128)} custom-call(s32[6]{0:T(128)S(1)} %stack.28.place_ref, bf16[384,256]{1,0:T(8,128)(2,1)S(1)} %line.1.refs_0_.after_ref, bf16[384,256]{1,0:T(8,128)(2,1)S(1)} %collective-permute-done.21.refs_1_, bf16[384,256]{1,0:T(8,128)(2,1)S(1)} %collective-permute-done.23.refs_2_, ...), custom_call_target="tpu_custom_call" | custom-call | tf_op jit(solution)/shard_map/finish0/pallas_call | solution.py:646
  100.8 1.7 %finish1.1 = (f32[3072,256]{1,0:T(8,128)}, f32[8,128]{1,0:T(8,128)S(1)}) custom-call(s32[6]{0:T(128)S(1)} %stack.28.place_ref, bf16[384,256]{1,0:T(8,128)(2,1)S(1)} %collective-permute-done.20.refs_0_, bf16[384,256]{1,0:T(8,128)(2,1)S(1)} %collective-permute-done.22.refs_1_, ...), custom_call_target="tpu_custom_call", output_to_operand_aliasing={{0}: (5, {})} | custom-call | tf_op jit(solution)/shard_map/finish1/pallas_call | solution.py:655
  102.8 1.4 %table.1 = f32[512,256]{1,0:T(8,128)} custom-call(s32[6]{0:T(128)S(1)} %stack.28.place_ref, f32[8,128]{1,0:T(8,128)S(1)} %get-tuple-element.92.after_ref, bf16[256,256]{1,0:T(8,128)(2,1)S(1)} %share.1.refs_0_, bf16[256,256]{1,0:T(8,128)(2,1)S(1)} %collective-permute-done.31.refs_1_), custom_call_target="tpu_custom_call" | custom-call | tf_op jit(solution)/shard_map/table/pallas_call | solution.py:665
  (39 shorter events, 4.7 us)
Async XLA Ops:
  0.6 16.3 %collective-permute-start = (bf16[512,256]{1,0:T(8,128)(2,1)}, bf16[512,256]{1,0:T(8,128)(2,1)S(1)}, u32[]{:S(2)}, u32[]{:S(2)}) collective-permute-start(bf16[512,256]{1,0:T(8,128)(2,1)} %table_hbm.1), channel_id=1, source_target_pairs={{0,16},{1,17},{2,18},{3,19},{4,20},{5,21},{6,22},{7,23},{8,24},{9,... | collective-permute-start | bytes 786440 | tf_op jit(solution)/shard_map/ppermute | solution.py:466
  17.6 4.5 %collective-permute-start.1 = (bf16[256,256]{1,0:T(8,128)(2,1)S(1)}, bf16[256,256]{1,0:T(8,128)(2,1)S(1)}, u32[]{:S(2)}, u32[]{:S(2)}) collective-permute-start(bf16[256,256]{1,0:T(8,128)(2,1)S(1)} %get-tuple-element.65), channel_id=1, source_target_pairs={{0,2},{1,3},{2,0},{3,1},{4,6},{5,7},{6,4},{7,5},{8,10},{9,11},{10,... | collective-permute-start | bytes 393224 | tf_op jit(solution)/shard_map/ppermute | solution.py:466
  17.6 5.9 %collective-permute-start.2 = (bf16[256,256]{1,0:T(8,128)(2,1)S(1)}, bf16[256,256]{1,0:T(8,128)(2,1)S(1)}, u32[]{:S(2)}, u32[]{:S(2)}) collective-permute-start(bf16[256,256]{1,0:T(8,128)(2,1)S(1)} %get-tuple-element.66), channel_id=1, source_target_pairs={{0,4},{1,5},{2,6},{3,7},{4,0},{5,1},{6,2},{7,3},{8,12},{9,13},{10,... | collective-permute-start | bytes 393224 | tf_op jit(solution)/shard_map/ppermute | solution.py:466
  19.3 6.3 %collective-permute-start.3 = (bf16[256,256]{1,0:T(8,128)(2,1)S(1)}, bf16[256,256]{1,0:T(8,128)(2,1)S(1)}, u32[]{:S(2)}, u32[]{:S(2)}) collective-permute-start(bf16[256,256]{1,0:T(8,128)(2,1)S(1)} %get-tuple-element.67), channel_id=1, source_target_pairs={{0,8},{1,9},{2,10},{3,11},{4,12},{5,13},{6,14},{7,15},{8,0},{9,1},... | collective-permute-start | bytes 393224 | tf_op jit(solution)/shard_map/ppermute | solution.py:466
  20.0 8.5 %collective-permute-start.4 = (bf16[256,256]{1,0:T(8,128)(2,1)S(1)}, bf16[256,256]{1,0:T(8,128)(2,1)S(1)}, u32[]{:S(2)}, u32[]{:S(2)}) collective-permute-start(bf16[256,256]{1,0:T(8,128)(2,1)S(1)} %get-tuple-element.68), channel_id=1, source_target_pairs={{0,12},{1,13},{2,14},{3,15},{4,8},{5,9},{6,10},{7,11},{8,4},{9,5},... | collective-permute-start | bytes 393224 | tf_op jit(solution)/shard_map/ppermute | solution.py:466
  21.2 8.5 %collective-permute-start.5 = (bf16[256,256]{1,0:T(8,128)(2,1)S(1)}, bf16[256,256]{1,0:T(8,128)(2,1)S(1)}, u32[]{:S(2)}, u32[]{:S(2)}) collective-permute-start(bf16[256,256]{1,0:T(8,128)(2,1)S(1)} %get-tuple-element.69), channel_id=1, source_target_pairs={{0,14},{1,15},{2,12},{3,13},{4,10},{5,11},{6,8},{7,9},{8,6},{9,7},... | collective-permute-start | bytes 393224 | tf_op jit(solution)/shard_map/ppermute | solution.py:466
  22.1 10.5 %collective-permute-start.6 = (bf16[256,256]{1,0:T(8,128)(2,1)S(1)}, bf16[256,256]{1,0:T(8,128)(2,1)S(1)}, u32[]{:S(2)}, u32[]{:S(2)}) collective-permute-start(bf16[256,256]{1,0:T(8,128)(2,1)S(1)} %get-tuple-element.70), channel_id=1, source_target_pairs={{0,6},{1,7},{2,4},{3,5},{4,2},{5,3},{6,0},{7,1},{8,14},{9,15},{10,... | collective-permute-start | bytes 393224 | tf_op jit(solution)/shard_map/ppermute | solution.py:466
  23.6 9.1 %collective-permute-start.7 = (bf16[256,256]{1,0:T(8,128)(2,1)S(1)}, bf16[256,256]{1,0:T(8,128)(2,1)S(1)}, u32[]{:S(2)}, u32[]{:S(2)}) collective-permute-start(bf16[256,256]{1,0:T(8,128)(2,1)S(1)} %get-tuple-element.71), channel_id=1, source_target_pairs={{0,10},{1,11},{2,8},{3,9},{4,14},{5,15},{6,12},{7,13},{8,2},{9,3},... | collective-permute-start | bytes 393224 | tf_op jit(solution)/shard_map/ppermute | solution.py:466
  44.1 2.5 %collective-permute-start.8 = (bf16[1552,256]{1,0:T(8,128)(2,1)S(1)}, bf16[1552,256]{1,0:T(8,128)(2,1)S(1)}, u32[]{:S(2)}, u32[]{:S(2)}) collective-permute-start(bf16[1552,256]{1,0:T(8,128)(2,1)S(1)} %get-tuple-element.74), channel_id=1, source_target_pairs={{0,2},{1,3},{2,0},{3,1},{4,6},{5,7},{6,4},{7,5},{8,10},{9,11},{10,... | collective-permute-start | bytes 2383880 | tf_op jit(solution)/shard_map/ppermute | solution.py:466
  45.6 3.3 %collective-permute-start.12 = (bf16[4,256,256]{2,1,0:T(8,128)(2,1)S(1)}, bf16[4,256,256]{2,1,0:T(8,128)(2,1)S(1)}, u32[]{:S(2)}, u32[]{:S(2)}) collective-permute-start(bf16[4,256,256]{2,1,0:T(8,128)(2,1)S(1)} %get-tuple-element.82), channel_id=1, source_target_pairs={{0,2},{1,3},{2,0},{3,1},{4,6},{5,7},{6,4},{7,5},{8,10},{9,11},{10,... | collective-permute-start | bytes 1572872 | tf_op jit(solution)/shard_map/ppermute | solution.py:466
  47.3 8.0 %collective-permute-start.9 = (bf16[400,256]{1,0:T(8,128)(2,1)S(1)}, bf16[400,256]{1,0:T(8,128)(2,1)S(1)}, u32[]{:S(2)}, u32[]{:S(2)}) collective-permute-start(bf16[400,256]{1,0:T(8,128)(2,1)S(1)} %get-tuple-element.77), channel_id=1, source_target_pairs={{0,1},{1,0},{2,3},{3,2},{4,5},{5,4},{6,7},{7,6},{8,9},{9,8},{10,11... | collective-permute-start | bytes 614408 | tf_op jit(solution)/shard_map/ppermute | solution.py:466
  48.9 19.1 %collective-permute-start.13 = (bf16[2,256,256]{2,1,0:T(8,128)(2,1)S(1)}, bf16[2,256,256]{2,1,0:T(8,128)(2,1)S(1)}, u32[]{:S(2)}, u32[]{:S(2)}) collective-permute-start(bf16[2,256,256]{2,1,0:T(8,128)(2,1)S(1)} %get-tuple-element.83), channel_id=1, source_target_pairs={{0,8},{1,9},{2,10},{3,11},{4,12},{5,13},{6,14},{7,15},{8,0},{9,1},... | collective-permute-start | bytes 786440 | tf_op jit(solution)/shard_map/ppermute | solution.py:466
  50.0 18.0 %collective-permute-start.10 = (bf16[400,256]{1,0:T(8,128)(2,1)S(1)}, bf16[400,256]{1,0:T(8,128)(2,1)S(1)}, u32[]{:S(2)}, u32[]{:S(2)}) collective-permute-start(bf16[400,256]{1,0:T(8,128)(2,1)S(1)} %get-tuple-element.78), channel_id=1, source_target_pairs={{0,4},{1,5},{2,6},{3,7},{4,0},{5,1},{6,2},{7,3},{8,12},{9,13},{10,... | collective-permute-start | bytes 614408 | tf_op jit(solution)/shard_map/ppermute | solution.py:466
  51.0 17.0 %collective-permute-start.11 = (bf16[400,256]{1,0:T(8,128)(2,1)S(1)}, bf16[400,256]{1,0:T(8,128)(2,1)S(1)}, u32[]{:S(2)}, u32[]{:S(2)}) collective-permute-start(bf16[400,256]{1,0:T(8,128)(2,1)S(1)} %get-tuple-element.79), channel_id=1, source_target_pairs={{0,5},{1,4},{2,7},{3,6},{4,1},{5,0},{6,3},{7,2},{8,13},{9,12},{10,... | collective-permute-start | bytes 614408 | tf_op jit(solution)/shard_map/ppermute | solution.py:466
  52.0 26.9 %collective-permute-start.27 = (bf16[2,256,256]{2,1,0:T(8,128)(2,1)S(1)}, bf16[2,256,256]{2,1,0:T(8,128)(2,1)S(1)}, u32[]{:S(2)}, u32[]{:S(2)}) collective-permute-start(bf16[2,256,256]{2,1,0:T(8,128)(2,1)S(1)} %get-tuple-element.94), channel_id=1, source_target_pairs={{0,4},{1,5},{2,6},{3,7},{4,0},{5,1},{6,2},{7,3},{8,12},{9,13},{10,... | collective-permute-start | bytes 786440 | tf_op jit(solution)/shard_map/ppermute | solution.py:466
  55.3 23.7 %collective-permute-start.28 = (bf16[2,256,256]{2,1,0:T(8,128)(2,1)S(1)}, bf16[2,256,256]{2,1,0:T(8,128)(2,1)S(1)}, u32[]{:S(2)}, u32[]{:S(2)}) collective-permute-start(bf16[2,256,256]{2,1,0:T(8,128)(2,1)S(1)} %get-tuple-element.95), channel_id=1, source_target_pairs={{0,12},{1,13},{2,14},{3,15},{4,8},{5,9},{6,10},{7,11},{8,4},{9,5},... | collective-permute-start | bytes 786440 | tf_op jit(solution)/shard_map/ppermute | solution.py:466
  68.7 4.5 %collective-permute-start.14 = (bf16[112,256]{1,0:T(8,128)(2,1)S(1)}, bf16[112,256]{1,0:T(8,128)(2,1)S(1)}, u32[]{:S(2)}, u32[]{:S(2)}) collective-permute-start(bf16[112,256]{1,0:T(8,128)(2,1)S(1)} %get-tuple-element.86), channel_id=1, source_target_pairs={{0,8},{1,9},{2,10},{3,11},{4,12},{5,13},{6,14},{7,15},{8,0},{9,1},... | collective-permute-start | bytes 172040 | tf_op jit(solution)/shard_map/ppermute | solution.py:466
  69.7 5.1 %collective-permute-start.15 = (bf16[112,256]{1,0:T(8,128)(2,1)S(1)}, bf16[112,256]{1,0:T(8,128)(2,1)S(1)}, u32[]{:S(2)}, u32[]{:S(2)}) collective-permute-start(bf16[112,256]{1,0:T(8,128)(2,1)S(1)} %get-tuple-element.87), channel_id=1, source_target_pairs={{0,16},{1,17},{2,18},{3,19},{4,20},{5,21},{6,22},{7,23},{8,24},{9,... | collective-permute-start | bytes 172040 | tf_op jit(solution)/shard_map/ppermute | solution.py:466
  72.3 6.0 %collective-permute-start.16 = (bf16[112,256]{1,0:T(8,128)(2,1)S(1)}, bf16[112,256]{1,0:T(8,128)(2,1)S(1)}, u32[]{:S(2)}, u32[]{:S(2)}) collective-permute-start(bf16[112,256]{1,0:T(8,128)(2,1)S(1)} %get-tuple-element.88), channel_id=1, source_target_pairs={{0,24},{1,25},{2,26},{3,27},{4,28},{5,29},{6,30},{7,31},{8,16},{9,... | collective-permute-start | bytes 172040 | tf_op jit(solution)/shard_map/ppermute | solution.py:466
  80.3 11.1 %collective-permute-start.29 = (bf16[512,256]{1,0:T(8,128)(2,1)S(1)}, bf16[512,256]{1,0:T(8,128)(2,1)S(1)}, u32[]{:S(2)}, u32[]{:S(2)}) collective-permute-start(bf16[512,256]{1,0:T(8,128)(2,1)S(1)} %get-tuple-element.98), channel_id=1, source_target_pairs={{0,1},{1,0},{2,3},{3,2},{4,5},{5,4},{6,7},{7,6},{8,9},{9,8},{10,11... | collective-permute-start | bytes 786440 | tf_op jit(solution)/shard_map/ppermute | solution.py:466
  80.9 5.9 %collective-permute-start.19 = (bf16[96,256]{1,0:T(8,128)(2,1)S(1)}, bf16[96,256]{1,0:T(8,128)(2,1)S(1)}, u32[]{:S(2)}, u32[]{:S(2)}) collective-permute-start(bf16[96,256]{1,0:T(8,128)(2,1)S(1)} %get-tuple-element.89.refs_0_.after_ref), channel_id=1, source_target_pairs={{0,24},{1,25},{2,26},{3,27},{4,28},{5,29},{6,30},{7,31},{8,16},{9,... | collective-permute-start | bytes 147464 | tf_op jit(solution)/shard_map/ppermute | solution.py:466
  82.0 5.8 %collective-permute-start.18 = (bf16[96,256]{1,0:T(8,128)(2,1)S(1)}, bf16[96,256]{1,0:T(8,128)(2,1)S(1)}, u32[]{:S(2)}, u32[]{:S(2)}) collective-permute-start(bf16[96,256]{1,0:T(8,128)(2,1)S(1)} %get-tuple-element.89.refs_0_.after_ref), channel_id=1, source_target_pairs={{0,16},{1,17},{2,18},{3,19},{4,20},{5,21},{6,22},{7,23},{8,24},{9,... | collective-permute-start | bytes 147464 | tf_op jit(solution)/shard_map/ppermute | solution.py:466
  82.0 5.8 %collective-permute-start.17 = (bf16[96,256]{1,0:T(8,128)(2,1)S(1)}, bf16[96,256]{1,0:T(8,128)(2,1)S(1)}, u32[]{:S(2)}, u32[]{:S(2)}) collective-permute-start(bf16[96,256]{1,0:T(8,128)(2,1)S(1)} %get-tuple-element.89.refs_0_.after_ref), channel_id=1, source_target_pairs={{0,8},{1,9},{2,10},{3,11},{4,12},{5,13},{6,14},{7,15},{8,0},{9,1},... | collective-permute-start | bytes 147464 | tf_op jit(solution)/shard_map/ppermute | solution.py:466
  87.8 6.7 %collective-permute-start.25 = (bf16[384,256]{1,0:T(8,128)(2,1)S(1)}, bf16[384,256]{1,0:T(8,128)(2,1)S(1)}, u32[]{:S(2)}, u32[]{:S(2)}) collective-permute-start(bf16[384,256]{1,0:T(8,128)(2,1)S(1)} %line.1.refs_0_.after_ref), channel_id=1, source_target_pairs={{0,5},{1,4},{2,7},{3,6},{4,1},{5,0},{6,3},{7,2},{8,13},{9,12},{10,... | collective-permute-start | bytes 589832 | tf_op jit(solution)/shard_map/ppermute | solution.py:466
  90.3 6.3 %collective-permute-start.23 = (bf16[384,256]{1,0:T(8,128)(2,1)S(1)}, bf16[384,256]{1,0:T(8,128)(2,1)S(1)}, u32[]{:S(2)}, u32[]{:S(2)}) collective-permute-start(bf16[384,256]{1,0:T(8,128)(2,1)S(1)} %line.1.refs_0_.after_ref), channel_id=1, source_target_pairs={{0,4},{1,5},{2,6},{3,7},{4,0},{5,1},{6,2},{7,3},{8,12},{9,13},{10,... | collective-permute-start | bytes 589832 | tf_op jit(solution)/shard_map/ppermute | solution.py:466
  90.9 6.0 %collective-permute-start.21 = (bf16[384,256]{1,0:T(8,128)(2,1)S(1)}, bf16[384,256]{1,0:T(8,128)(2,1)S(1)}, u32[]{:S(2)}, u32[]{:S(2)}) collective-permute-start(bf16[384,256]{1,0:T(8,128)(2,1)S(1)} %line.1.refs_0_.after_ref), channel_id=1, source_target_pairs={{0,1},{1,0},{2,3},{3,2},{4,5},{5,4},{6,7},{7,6},{8,9},{9,8},{10,11... | collective-permute-start | bytes 589832 | tf_op jit(solution)/shard_map/ppermute | solution.py:466
  91.5 5.9 %collective-permute-start.30 = (bf16[256,256]{1,0:T(8,128)(2,1)S(1)}, bf16[256,256]{1,0:T(8,128)(2,1)S(1)}, u32[]{:S(2)}, u32[]{:S(2)}) collective-permute-start(bf16[256,256]{1,0:T(8,128)(2,1)S(1)} %get-tuple-element.100), channel_id=1, source_target_pairs={{0,16},{1,17},{2,18},{3,19},{4,20},{5,21},{6,22},{7,23},{8,24},{9,... | collective-permute-start | bytes 393224 | tf_op jit(solution)/shard_map/ppermute | solution.py:466
  92.7 8.0 %collective-permute-start.20 = (bf16[384,256]{1,0:T(8,128)(2,1)S(1)}, bf16[384,256]{1,0:T(8,128)(2,1)S(1)}, u32[]{:S(2)}, u32[]{:S(2)}) collective-permute-start(bf16[384,256]{1,0:T(8,128)(2,1)S(1)} %line.1.refs_0_.after_ref), channel_id=1, source_target_pairs={{0,2},{1,3},{2,0},{3,1},{4,6},{5,7},{6,4},{7,5},{8,10},{9,11},{10,... | collective-permute-start | bytes 589832 | tf_op jit(solution)/shard_map/ppermute | solution.py:466
  94.5 6.2 %collective-permute-start.26 = (bf16[384,256]{1,0:T(8,128)(2,1)S(1)}, bf16[384,256]{1,0:T(8,128)(2,1)S(1)}, u32[]{:S(2)}, u32[]{:S(2)}) collective-permute-start(bf16[384,256]{1,0:T(8,128)(2,1)S(1)} %collective-permute-done.25.refs_3_.refs_0_), channel_id=1, source_target_pairs={{0,2},{1,3},{2,0},{3,1},{4,6},{5,7},{6,4},{7,5},{8,10},{9,11},{10,... | collective-permute-start | bytes 589832 | tf_op jit(solution)/shard_map/ppermute | solution.py:466
  96.6 4.2 %collective-permute-start.24 = (bf16[384,256]{1,0:T(8,128)(2,1)S(1)}, bf16[384,256]{1,0:T(8,128)(2,1)S(1)}, u32[]{:S(2)}, u32[]{:S(2)}) collective-permute-start(bf16[384,256]{1,0:T(8,128)(2,1)S(1)} %collective-permute-done.23.refs_2_), channel_id=1, source_target_pairs={{0,2},{1,3},{2,0},{3,1},{4,6},{5,7},{6,4},{7,5},{8,10},{9,11},{10,... | collective-permute-start | bytes 589832 | tf_op jit(solution)/shard_map/ppermute | solution.py:466
  96.8 4.0 %collective-permute-start.22 = (bf16[384,256]{1,0:T(8,128)(2,1)S(1)}, bf16[384,256]{1,0:T(8,128)(2,1)S(1)}, u32[]{:S(2)}, u32[]{:S(2)}) collective-permute-start(bf16[384,256]{1,0:T(8,128)(2,1)S(1)} %collective-permute-done.21.refs_1_), channel_id=1, source_target_pairs={{0,2},{1,3},{2,0},{3,1},{4,6},{5,7},{6,4},{7,5},{8,10},{9,11},{10,... | collective-permute-start | bytes 589832 | tf_op jit(solution)/shard_map/ppermute | solution.py:466
  97.4 5.4 %collective-permute-start.31 = (bf16[256,256]{1,0:T(8,128)(2,1)S(1)}, bf16[256,256]{1,0:T(8,128)(2,1)S(1)}, u32[]{:S(2)}, u32[]{:S(2)}) collective-permute-start(bf16[256,256]{1,0:T(8,128)(2,1)S(1)} %share.1.refs_0_), channel_id=1, source_target_pairs={{0,1},{1,0},{2,3},{3,2},{4,5},{5,4},{6,7},{7,6},{8,9},{9,8},{10,11... | collective-permute-start | bytes 393224 | tf_op jit(solution)/shard_map/ppermute | solution.py:466

commit v3 on v2

--- a/solution.py
+++ b/solution.py
@@ -39,10 +39,9 @@
 
 
 def ordered(near):
-    return [0] + sorted(
-        range(1, near),
-        key=lambda step: (bin(step).count("1") != 1, not step & 2 or step < 4, step),
-    )
+    top = near // 2
+    steps = sorted(range(1, near), key=lambda step: (step < 2, step & 1, step < top, step < top + 2))
+    return [0] + steps
 
 
 def returning(chips):
@@ -162,10 +161,11 @@
     gain_ref, upstream_ref, weight_ref, sems = refs[15:]
     copies = [
         pltpu.make_async_copy(gain_hbm, gain_ref, sems.at[0]),
+        *(
+            pltpu.make_async_copy(weight_hbm.at[layer], weight_ref.at[layer], sems.at[2 + layer])
+            for layer in range(weight_ref.shape[0])
+        ),
         pltpu.make_async_copy(upstream_hbm, upstream_ref, sems.at[1]),
-    ] + [
-        pltpu.make_async_copy(weight_hbm.at[layer], weight_ref.at[layer], sems.at[2 + layer])
-        for layer in range(weight_ref.shape[0])
     ]
     for copy in copies:
         copy.start()
@@ -227,7 +227,7 @@
     root = math.sqrt(2.0 / math.pi)
     for layer in range(layers):
         dilation = 2**layer
-        copies[2 + layer].wait()
+        copies[1 + layer].wait()
         for start in range(0, taps, width):
             value = weight_ref[layer, start : start + width, :]
             rounded_s[layer, start : start + width, :] = value.astype(BF16)
@@ -263,7 +263,7 @@
             rows = pl.ds(layer * taps + tap * width, width)
             dw_s[rows, :] += term[:, tap * width : (tap + 1) * width]
 
-    copies[1].wait()
+    copies[-1].wait()
     for seq in range(batches):
         for j in range(per):
             cotangent = upstream_ref[at(seq, j), :].astype(F32)
@@ -386,23 +386,26 @@
     outs[1][...] = block * scale
 
 
-def finish_kernel(line, scale, side, place_ref, *refs):
+def finish_kernel(line, scale, spots, place_ref, *refs):
     rows_s, sems = refs[-2:]
-    out_ref = refs[-3 - side]
-    square, block, _ = rows_s.shape
+    first = len(refs) == len(spots) + 3
+    out_ref = refs[-3 if first else -4]
+    block = rows_s.shape[1]
     piece = block // line
     copies = []
-    for outer, ref in enumerate(refs[:square]):
+    for number, (side, outer) in enumerate(spots):
         for inner in range(line):
             target = pl.multiple_of((place_ref[2] ^ inner) * piece, piece)
-            rows_s[outer, pl.ds(target, piece), :] = (
-                ref[inner * piece : (inner + 1) * piece, :].astype(F32) * scale
+            rows_s[number, pl.ds(target, piece), :] = (
+                refs[number][inner * piece : (inner + 1) * piece, :].astype(F32) * scale
             )
-        spot = (place_ref[0] ^ side) * square + (place_ref[1] ^ outer)
+        spot = (place_ref[0] ^ side) * 4 + (place_ref[1] ^ outer)
         rows = pl.ds(pl.multiple_of(spot * block, block), block)
-        copies.append(pltpu.make_async_copy(rows_s.at[outer], out_ref.at[rows, :], sems.at[outer]))
+        copies.append(
+            pltpu.make_async_copy(rows_s.at[number], out_ref.at[rows, :], sems.at[number])
+        )
         copies[-1].start()
-    if side == 1:
+    if not first:
         refs[-3][...] = jnp.zeros(refs[-3].shape, F32)
     for copy in copies:
         copy.wait()
@@ -422,8 +425,9 @@
     far_sum_ref[...] = tree([far_ref[...]] + [m[share:, :].astype(F32) for m in shares]).astype(BF16)
 
 
-def share_kernel(near_ref, far_ref, *refs):
-    refs[-1][...] = (near_ref[...] + far_ref[...].astype(F32)).astype(BF16)
+def share_kernel(near_ref, far_ref, after_ref, part_ref):
+    del after_ref
+    part_ref[...] = (near_ref[...] + far_ref[...].astype(F32)).astype(BF16)
 
 
 def table_kernel(place_ref, after_ref, *refs):
@@ -643,25 +647,23 @@
         compiler_params=params(16),
         name="share",
     )(near_share, far_share, square[3])
-    weight_grad = pl.pallas_call(
-        functools.partial(finish_kernel, 2 ** len(stages[2]), scale, 0),
-        out_shape=shape((rows, width), F32),
-        in_specs=[SMEM] + [VMEM] * 4,
-        out_specs=ANY,
-        scratch_shapes=[pltpu.VMEM((4, half // 4, width), F32), pltpu.SemaphoreType.DMA((4,))],
-        compiler_params=params(16),
-        name="finish0",
-    )(place, *square)
-    weight_grad, mark = pl.pallas_call(
-        functools.partial(finish_kernel, 2 ** len(stages[2]), scale, 1),
-        out_shape=(shape((rows, width), F32), shape((8, 128), F32)),
-        in_specs=[SMEM] + [VMEM] * 4 + [ANY],
-        out_specs=(ANY, VMEM),
-        scratch_shapes=[pltpu.VMEM((4, half // 4, width), F32), pltpu.SemaphoreType.DMA((4,))],
-        input_output_aliases={5: 0},
-        compiler_params=params(16),
-        name="finish1",
-    )(place, *other, weight_grad)
+    pieces = [(side, outer) for side in range(2) for outer in range(4)]
+    written = []
+    for number, spots in enumerate((pieces[:5], pieces[5:])):
+        written = pl.pallas_call(
+            functools.partial(finish_kernel, 2 ** len(stages[2]), scale, spots),
+            out_shape=(shape((rows, width), F32), shape((8, 128), F32))[: 1 + number],
+            in_specs=[SMEM] + [VMEM] * len(spots) + [ANY] * number,
+            out_specs=(ANY, VMEM)[: 1 + number],
+            scratch_shapes=[
+                pltpu.VMEM((len(spots), half // 4, width), F32),
+                pltpu.SemaphoreType.DMA((len(spots),)),
+            ],
+            input_output_aliases={1 + len(spots): 0} if number else {},
+            compiler_params=params(16),
+            name=f"finish{number}",
+        )(place, *[(square, other)[side][outer] for side, outer in spots], *written)
+    weight_grad, mark = written
     table_grad = pl.pallas_call(
         table_kernel,
         out_shape=shape((slab, width), F32),

time: 104 us -> 104 us (level)
  waiting for transfers between devices: 35.9 us -> 33.1 us
  starting transfers between devices: 34.1 us -> 36 us
    ppermute x32, waiting for transfers between devices: 35.9 us -> 33.1 us  [swap(): return lax.ppermute(value, axes, [(i, i ^ mask) for i in range(devices)])]
    ppermute x32, starting transfers between devices: 34.1 us -> 36 us  [swap(): return lax.ppermute(value, axes, [(i, i ^ mask) for i in range(devices)])]
where the time goes in v3:
time: 104 us; the launch traced here: 103 us
  starting transfers between devices  36 us (35%)
  waiting for transfers between devices  33.1 us (32%)
  Pallas kernels  23.9 us (23%)
  blocking collectives  8.43 us (8%)
    ppermute x32, starting transfers between devices, swap(): return lax.ppermute(value, axes, [(i, i ^ mask) for i in range(devices)])  36 us
    ppermute x32, waiting for transfers between devices, swap(): return lax.ppermute(value, axes, [(i, i ^ mask) for i in range(devices)])  33.1 us
    pallas_call x1, Pallas kernels, body(): pl.pallas_call(stack_kernel, out_shape=(shape((tokens, width), BF16), sha...  11.4 us
    all_to_all x1, blocking collectives, exchange(): lax.all_to_all(value, 'emb', split_axis=0, concat_axis=0, axis_index_grou...  8.43 us
    pallas_call x2, Pallas kernels, body(): pl.pallas_call(functools.partial(finish_kernel, 2 ** len(stages[2]), scal...  3.49 us
  transfers between devices with their start and end apart: 32, of which 18 were waited for; matrix products, arithmetic and copies ran while one was open for 1% of the time, Pallas kernels for 9%

profile of v3, /device:TPU:0, one launch (start us, length us, event | category | flops | bytes accessed | tf_op | source)
XLA Modules:
  0.0 103.3 jit_solution(4920960528261539331)
XLA Ops:
  0.6 4.1 %collective-permute-start = (bf16[512,256]{1,0:T(8,128)(2,1)}, bf16[512,256]{1,0:T(8,128)(2,1)S(1)}, u32[]{:S(2)}, u32[]{:S(2)}) collective-permute-start(bf16[512,256]{1,0:T(8,128)(2,1)} %table_hbm.1), channel_id=1, source_target_pairs={{0,16},{1,17},{2,18},{3,19},{4,20},{5,21},{6,22},{7,23},{8,24},{9,... | collective-permute-start | bytes 786440 | tf_op jit(solution)/shard_map/ppermute | solution.py:470
  4.8 0.7 bitcast_add_fusion.ids_ref
  5.5 1.5 %request.1 = (s32[8,256]{1,0:T(8,128)S(1)}, s32[2,512]{1,0:T(2,128)S(1)}, bf16[512,256]{1,0:T(8,128)(2,1)S(1)}) custom-call(s32[6]{0:T(128)S(1)} %stack.28.place_ref, s32[2,512]{1,0:T(2,128)S(1)} %bitcast_add_fusion.ids_ref, bf16[512,256]{1,0:T(8,128)(2,1)} %table_hbm.1), custom_call_target="tpu_custom_call" | custom-call | tf_op jit(solution)/shard_map/request/pallas_call | solution.py:483
  7.0 8.4 %all_to_all.11 = s32[8,1,256]{2,1,0:T(1,128)S(1)} all-to-all(s32[8,1,256]{2,1,0:T(1,128)S(1)} %copy.14), channel_id=1, replica_groups={{0,2,4,6,8,10,12,14},{16,18,20,22,24,26,28,30},{1,3,5,7,9,11,13,15},{17..., dimensions={0} | all-to-all | bytes 16384 | tf_op jit(solution)/shard_map/all_to_all | solution.py:476
  15.5 1.1 %near.1 = (s32[8,256]{1,0:T(8,128)S(1)}, bf16[128,256]{1,0:T(8,128)(2,1)S(1)}, bf16[128,256]{1,0:T(8,128)(2,1)S(1)}, bf16[128,256]{1,0:T(8,128)(2,1)S(1)}, bf16[...) custom-call(s32[6]{0:T(128)S(1)} %stack.28.place_ref, ...), custom_call_target="tpu_custom_call" | custom-call | tf_op jit(solution)/shard_map/near/pallas_call | solution.py:497
  17.0 0.6 far.1
  17.6 1.8 %collective-permute-start.1 = (bf16[256,256]{1,0:T(8,128)(2,1)S(1)}, bf16[256,256]{1,0:T(8,128)(2,1)S(1)}, u32[]{:S(2)}, u32[]{:S(2)}) collective-permute-start(bf16[256,256]{1,0:T(8,128)(2,1)S(1)} %get-tuple-element.65), channel_id=1, source_target_pairs={{0,12},{1,13},{2,14},{3,15},{4,8},{5,9},{6,10},{7,11},{8,4},{9,5},... | collective-permute-start | bytes 393224 | tf_op jit(solution)/shard_map/ppermute | solution.py:470
  19.3 1.3 %collective-permute-start.2 = (bf16[256,256]{1,0:T(8,128)(2,1)S(1)}, bf16[256,256]{1,0:T(8,128)(2,1)S(1)}, u32[]{:S(2)}, u32[]{:S(2)}) collective-permute-start(bf16[256,256]{1,0:T(8,128)(2,1)S(1)} %get-tuple-element.66), channel_id=1, source_target_pairs={{0,8},{1,9},{2,10},{3,11},{4,12},{5,13},{6,14},{7,15},{8,0},{9,1},... | collective-permute-start | bytes 393224 | tf_op jit(solution)/shard_map/ppermute | solution.py:470
  21.6 2.3 %collective-permute-start.5 = (bf16[256,256]{1,0:T(8,128)(2,1)S(1)}, bf16[256,256]{1,0:T(8,128)(2,1)S(1)}, u32[]{:S(2)}, u32[]{:S(2)}) collective-permute-start(bf16[256,256]{1,0:T(8,128)(2,1)S(1)} %get-tuple-element.69), channel_id=1, source_target_pairs={{0,10},{1,11},{2,8},{3,9},{4,14},{5,15},{6,12},{7,13},{8,2},{9,3},... | collective-permute-start | bytes 393224 | tf_op jit(solution)/shard_map/ppermute | solution.py:470
  23.9 1.1 %collective-permute-done.1.refs_1_ = bf16[256,256]{1,0:T(8,128)(2,1)S(1)} collective-permute-done((bf16[256,256]{1,0:T(8,128)(2,1)S(1)}, bf16[256,256]{1,0:T(8,128)(2,1)S(1)}, u32[]{:S(2)}, u32[]{:S(2)}) %collective-permute-start.1) | collective-permute-done | bytes 131104 | tf_op jit(solution)/shard_map/ppermute | solution.py:470
  24.9 1.6 %collective-permute-done.2.refs_2_ = bf16[256,256]{1,0:T(8,128)(2,1)S(1)} collective-permute-done((bf16[256,256]{1,0:T(8,128)(2,1)S(1)}, bf16[256,256]{1,0:T(8,128)(2,1)S(1)}, u32[]{:S(2)}, u32[]{:S(2)}) %collective-permute-start.2) | collective-permute-done | bytes 131104 | tf_op jit(solution)/shard_map/ppermute | solution.py:470
  26.8 0.9 collective-permute-done.3.refs_3_
  27.7 1.1 %collective-permute-done.4.refs_4_ = bf16[256,256]{1,0:T(8,128)(2,1)S(1)} collective-permute-done((bf16[256,256]{1,0:T(8,128)(2,1)S(1)}, bf16[256,256]{1,0:T(8,128)(2,1)S(1)}, u32[]{:S(2)}, u32[]{:S(2)}) %collective-permute-start.4) | collective-permute-done | bytes 131104 | tf_op jit(solution)/shard_map/ppermute | solution.py:470
  28.8 2.0 %collective-permute-done.5.refs_5_ = bf16[256,256]{1,0:T(8,128)(2,1)S(1)} collective-permute-done((bf16[256,256]{1,0:T(8,128)(2,1)S(1)}, bf16[256,256]{1,0:T(8,128)(2,1)S(1)}, u32[]{:S(2)}, u32[]{:S(2)}) %collective-permute-start.5) | collective-permute-done | bytes 131104 | tf_op jit(solution)/shard_map/ppermute | solution.py:470
  30.8 1.3 %collective-permute-done.6.refs_6_ = bf16[256,256]{1,0:T(8,128)(2,1)S(1)} collective-permute-done((bf16[256,256]{1,0:T(8,128)(2,1)S(1)}, bf16[256,256]{1,0:T(8,128)(2,1)S(1)}, u32[]{:S(2)}, u32[]{:S(2)}) %collective-permute-start.6) | collective-permute-done | bytes 131104 | tf_op jit(solution)/shard_map/ppermute | solution.py:470
  32.1 11.4 %stack.29 = (bf16[1024,256]{1,0:T(8,128)(2,1)S(1)}, bf16[1536,256]{1,0:T(8,128)(2,1)S(1)}, bf16[1552,256]{1,0:T(8,128)(2,1)S(1)}, bf16[16,256]{1,0:T(8,128)(2,1)S(1)}) custom-call(s32[6]{0:T(128)S(1)} %stack.28.place_ref, s32[1024,1]{1,0:T(8,128)S(1)} %bitcast.18, f32[4,768,256]{2,1,0:T(8,128)} %weight_hbm.1, f32[4,256]{1,0:T(4,128)} %gain_hbm.1, ...), custom_call_target="tpu_custom_call" | custom-call | tf_op jit(solution)/shard_map/stack/pallas_call | solution.py:519
  43.6 0.9 place.1
  45.1 0.8 collective-permute-done.8.refs_0_
  45.9 0.7 fold0.1
  46.6 1.5 %collective-permute-start.9 = (bf16[400,256]{1,0:T(8,128)(2,1)S(1)}, bf16[400,256]{1,0:T(8,128)(2,1)S(1)}, u32[]{:S(2)}, u32[]{:S(2)}) collective-permute-start(bf16[400,256]{1,0:T(8,128)(2,1)S(1)} %get-tuple-element.77), channel_id=1, source_target_pairs={{0,1},{1,0},{2,3},{3,2},{4,5},{5,4},{6,7},{7,6},{8,9},{9,8},{10,11... | collective-permute-start | bytes 614408 | tf_op jit(solution)/shard_map/ppermute | solution.py:470
  48.2 1.1 %collective-permute-start.13 = (bf16[2,256,256]{2,1,0:T(8,128)(2,1)S(1)}, bf16[2,256,256]{2,1,0:T(8,128)(2,1)S(1)}, u32[]{:S(2)}, u32[]{:S(2)}) collective-permute-start(bf16[2,256,256]{2,1,0:T(8,128)(2,1)S(1)} %get-tuple-element.83), channel_id=1, source_target_pairs={{0,8},{1,9},{2,10},{3,11},{4,12},{5,13},{6,14},{7,15},{8,0},{9,1},... | collective-permute-start | bytes 786440 | tf_op jit(solution)/shard_map/ppermute | solution.py:470
  49.3 1.5 %collective-permute-start.10 = (bf16[400,256]{1,0:T(8,128)(2,1)S(1)}, bf16[400,256]{1,0:T(8,128)(2,1)S(1)}, u32[]{:S(2)}, u32[]{:S(2)}) collective-permute-start(bf16[400,256]{1,0:T(8,128)(2,1)S(1)} %get-tuple-element.78), channel_id=1, source_target_pairs={{0,4},{1,5},{2,6},{3,7},{4,0},{5,1},{6,2},{7,3},{8,12},{9,13},{10,... | collective-permute-start | bytes 614408 | tf_op jit(solution)/shard_map/ppermute | solution.py:470
  51.4 1.5 %collective-permute-start.27 = (bf16[2,256,256]{2,1,0:T(8,128)(2,1)S(1)}, bf16[2,256,256]{2,1,0:T(8,128)(2,1)S(1)}, u32[]{:S(2)}, u32[]{:S(2)}) collective-permute-start(bf16[2,256,256]{2,1,0:T(8,128)(2,1)S(1)} %get-tuple-element.94), channel_id=1, source_target_pairs={{0,4},{1,5},{2,6},{3,7},{4,0},{5,1},{6,2},{7,3},{8,12},{9,13},{10,... | collective-permute-start | bytes 786440 | tf_op jit(solution)/shard_map/ppermute | solution.py:470
  52.9 1.7 %collective-permute-done.9.refs_0_ = bf16[400,256]{1,0:T(8,128)(2,1)S(1)} collective-permute-done((bf16[400,256]{1,0:T(8,128)(2,1)S(1)}, bf16[400,256]{1,0:T(8,128)(2,1)S(1)}, u32[]{:S(2)}, u32[]{:S(2)}) %collective-permute-start.9) | collective-permute-done | bytes 204832 | tf_op jit(solution)/shard_map/ppermute | solution.py:470
  54.6 2.0 %collective-permute-start.28 = (bf16[2,256,256]{2,1,0:T(8,128)(2,1)S(1)}, bf16[2,256,256]{2,1,0:T(8,128)(2,1)S(1)}, u32[]{:S(2)}, u32[]{:S(2)}) collective-permute-start(bf16[2,256,256]{2,1,0:T(8,128)(2,1)S(1)} %get-tuple-element.95), channel_id=1, source_target_pairs={{0,12},{1,13},{2,14},{3,15},{4,8},{5,9},{6,10},{7,11},{8,4},{9,5},... | collective-permute-start | bytes 786440 | tf_op jit(solution)/shard_map/ppermute | solution.py:470
  56.6 10.7 %collective-permute-done.10.refs_1_ = bf16[400,256]{1,0:T(8,128)(2,1)S(1)} collective-permute-done((bf16[400,256]{1,0:T(8,128)(2,1)S(1)}, bf16[400,256]{1,0:T(8,128)(2,1)S(1)}, u32[]{:S(2)}, u32[]{:S(2)}) %collective-permute-start.10) | collective-permute-done | bytes 204832 | tf_op jit(solution)/shard_map/ppermute | solution.py:470
  67.4 0.6 fold1.1
  68.0 1.0 %collective-permute-start.14 = (bf16[112,256]{1,0:T(8,128)(2,1)S(1)}, bf16[112,256]{1,0:T(8,128)(2,1)S(1)}, u32[]{:S(2)}, u32[]{:S(2)}) collective-permute-start(bf16[112,256]{1,0:T(8,128)(2,1)S(1)} %get-tuple-element.86), channel_id=1, source_target_pairs={{0,8},{1,9},{2,10},{3,11},{4,12},{5,13},{6,14},{7,15},{8,0},{9,1},... | collective-permute-start | bytes 172040 | tf_op jit(solution)/shard_map/ppermute | solution.py:470
  69.0 2.7 %collective-permute-start.15 = (bf16[112,256]{1,0:T(8,128)(2,1)S(1)}, bf16[112,256]{1,0:T(8,128)(2,1)S(1)}, u32[]{:S(2)}, u32[]{:S(2)}) collective-permute-start(bf16[112,256]{1,0:T(8,128)(2,1)S(1)} %get-tuple-element.87), channel_id=1, source_target_pairs={{0,16},{1,17},{2,18},{3,19},{4,20},{5,21},{6,22},{7,23},{8,24},{9,... | collective-permute-start | bytes 172040 | tf_op jit(solution)/shard_map/ppermute | solution.py:470
  71.7 1.1 %collective-permute-start.16 = (bf16[112,256]{1,0:T(8,128)(2,1)S(1)}, bf16[112,256]{1,0:T(8,128)(2,1)S(1)}, u32[]{:S(2)}, u32[]{:S(2)}) collective-permute-start(bf16[112,256]{1,0:T(8,128)(2,1)S(1)} %get-tuple-element.88), channel_id=1, source_target_pairs={{0,24},{1,25},{2,26},{3,27},{4,28},{5,29},{6,30},{7,31},{8,16},{9,... | collective-permute-start | bytes 172040 | tf_op jit(solution)/shard_map/ppermute | solution.py:470
  72.8 1.3 %collective-permute-done.15.refs_1_ = bf16[112,256]{1,0:T(8,128)(2,1)S(1)} collective-permute-done((bf16[112,256]{1,0:T(8,128)(2,1)S(1)}, bf16[112,256]{1,0:T(8,128)(2,1)S(1)}, u32[]{:S(2)}, u32[]{:S(2)}) %collective-permute-start.15) | collective-permute-done | bytes 57376 | tf_op jit(solution)/shard_map/ppermute | solution.py:470
  74.1 3.6 %collective-permute-done.16.refs_2_ = bf16[112,256]{1,0:T(8,128)(2,1)S(1)} collective-permute-done((bf16[112,256]{1,0:T(8,128)(2,1)S(1)}, bf16[112,256]{1,0:T(8,128)(2,1)S(1)}, u32[]{:S(2)}, u32[]{:S(2)}) %collective-permute-start.16) | collective-permute-done | bytes 57376 | tf_op jit(solution)/shard_map/ppermute | solution.py:470
  77.7 0.6 last.1
  78.3 1.3 %collect.1 = (f32[256,256]{1,0:T(8,128)S(1)}, f32[256,256]{1,0:T(8,128)S(1)}, bf16[512,256]{1,0:T(8,128)(2,1)S(1)}) custom-call(s32[6]{0:T(128)S(1)} %stack.28.place_ref, s32[8,256]{1,0:T(8,128)S(1)} %get-tuple-element.55.asked_ref, bf16[96,256]{1,0:T(8,128)(2,1)S(1)} %get-tuple-element.89.refs_0_.after_ref, ...), custom_call_target="tpu_custom_call" | custom-call | tf_op jit(solution)/shard_map/collect/pallas_call | solution.py:607
  79.6 0.6 collective-permute-start.29
  80.2 1.2 %collective-permute-start.19 = (bf16[96,256]{1,0:T(8,128)(2,1)S(1)}, bf16[96,256]{1,0:T(8,128)(2,1)S(1)}, u32[]{:S(2)}, u32[]{:S(2)}) collective-permute-start(bf16[96,256]{1,0:T(8,128)(2,1)S(1)} %get-tuple-element.89.refs_0_.after_ref), channel_id=1, source_target_pairs={{0,24},{1,25},{2,26},{3,27},{4,28},{5,29},{6,30},{7,31},{8,16},{9,... | collective-permute-start | bytes 147464 | tf_op jit(solution)/shard_map/ppermute | solution.py:470
  81.6 3.0 %collective-permute-start.17 = (bf16[96,256]{1,0:T(8,128)(2,1)S(1)}, bf16[96,256]{1,0:T(8,128)(2,1)S(1)}, u32[]{:S(2)}, u32[]{:S(2)}) collective-permute-start(bf16[96,256]{1,0:T(8,128)(2,1)S(1)} %get-tuple-element.89.refs_0_.after_ref), channel_id=1, source_target_pairs={{0,8},{1,9},{2,10},{3,11},{4,12},{5,13},{6,14},{7,15},{8,0},{9,1},... | collective-permute-start | bytes 147464 | tf_op jit(solution)/shard_map/ppermute | solution.py:470
  84.6 1.5 %collective-permute-done.19.refs_3_ = bf16[96,256]{1,0:T(8,128)(2,1)S(1)} collective-permute-done((bf16[96,256]{1,0:T(8,128)(2,1)S(1)}, bf16[96,256]{1,0:T(8,128)(2,1)S(1)}, u32[]{:S(2)}, u32[]{:S(2)}) %collective-permute-start.19) | collective-permute-done | bytes 49184 | tf_op jit(solution)/shard_map/ppermute | solution.py:470
  86.1 1.1 %collective-permute-done.18.refs_2_ = bf16[96,256]{1,0:T(8,128)(2,1)S(1)} collective-permute-done((bf16[96,256]{1,0:T(8,128)(2,1)S(1)}, bf16[96,256]{1,0:T(8,128)(2,1)S(1)}, u32[]{:S(2)}, u32[]{:S(2)}) %collective-permute-start.18) | collective-permute-done | bytes 49184 | tf_op jit(solution)/shard_map/ppermute | solution.py:470
  87.2 2.3 %collective-permute-start.24 = (bf16[384,256]{1,0:T(8,128)(2,1)S(1)}, bf16[384,256]{1,0:T(8,128)(2,1)S(1)}, u32[]{:S(2)}, u32[]{:S(2)}) collective-permute-start(bf16[384,256]{1,0:T(8,128)(2,1)S(1)} %line.1.refs_0_.after_ref), channel_id=1, source_target_pairs={{0,5},{1,4},{2,7},{3,6},{4,1},{5,0},{6,3},{7,2},{8,13},{9,12},{10,... | collective-permute-start | bytes 589832 | tf_op jit(solution)/shard_map/ppermute | solution.py:470
  89.5 0.7 collective-permute-start.22
  90.8 1.4 %collective-permute-start.30 = (bf16[256,256]{1,0:T(8,128)(2,1)S(1)}, bf16[256,256]{1,0:T(8,128)(2,1)S(1)}, u32[]{:S(2)}, u32[]{:S(2)}) collective-permute-start(bf16[256,256]{1,0:T(8,128)(2,1)S(1)} %get-tuple-element.100), channel_id=1, source_target_pairs={{0,16},{1,17},{2,18},{3,19},{4,20},{5,21},{6,22},{7,23},{8,24},{9,... | collective-permute-start | bytes 393224 | tf_op jit(solution)/shard_map/ppermute | solution.py:470
  92.2 1.7 %collective-permute-done.24.refs_3_.after_ref = bf16[384,256]{1,0:T(8,128)(2,1)S(1)} collective-permute-done((bf16[384,256]{1,0:T(8,128)(2,1)S(1)}, bf16[384,256]{1,0:T(8,128)(2,1)S(1)}, u32[]{:S(2)}, u32[]{:S(2)}) %collective-permute-start.24) | collective-permute-done | bytes 196640 | tf_op jit(solution)/shard_map/ppermute | solution.py:470
  93.9 2.0 %collective-permute-done.22.refs_2_ = bf16[384,256]{1,0:T(8,128)(2,1)S(1)} collective-permute-done((bf16[384,256]{1,0:T(8,128)(2,1)S(1)}, bf16[384,256]{1,0:T(8,128)(2,1)S(1)}, u32[]{:S(2)}, u32[]{:S(2)}) %collective-permute-start.22) | collective-permute-done | bytes 196640 | tf_op jit(solution)/shard_map/ppermute | solution.py:470
  96.8 1.6 %collective-permute-start.31 = (bf16[256,256]{1,0:T(8,128)(2,1)S(1)}, bf16[256,256]{1,0:T(8,128)(2,1)S(1)}, u32[]{:S(2)}, u32[]{:S(2)}) collective-permute-start(bf16[256,256]{1,0:T(8,128)(2,1)S(1)} %share.1.refs_0_), channel_id=1, source_target_pairs={{0,1},{1,0},{2,3},{3,2},{4,5},{5,4},{6,7},{7,6},{8,9},{9,8},{10,11... | collective-permute-start | bytes 393224 | tf_op jit(solution)/shard_map/ppermute | solution.py:470
  98.4 1.9 %finish0.1.refs_3_ = f32[3072,256]{1,0:T(8,128)} custom-call(s32[6]{0:T(128)S(1)} %stack.28.place_ref, bf16[384,256]{1,0:T(8,128)(2,1)S(1)} %line.1.refs_0_.after_ref, bf16[384,256]{1,0:T(8,128)(2,1)S(1)} %collective-permute-done.20.refs_1_, bf16[384,256]{1,0:T(8,128)(2,1)S(1)} %collective-permute-done.22.refs_2_, ...), custom_call_target="tpu_custom_call" | custom-call | tf_op jit(solution)/shard_map/finish0/pallas_call | solution.py:653
  100.3 1.6 %finish1.1 = (f32[3072,256]{1,0:T(8,128)}, f32[8,128]{1,0:T(8,128)S(1)}) custom-call(s32[6]{0:T(128)S(1)} %stack.28.place_ref, bf16[384,256]{1,0:T(8,128)(2,1)S(1)} %collective-permute-done.21.refs_0_, bf16[384,256]{1,0:T(8,128)(2,1)S(1)} %collective-permute-done.23.refs_1_, ...), custom_call_target="tpu_custom_call", output_to_operand_aliasing={{0}: (4, {})} | custom-call | tf_op jit(solution)/shard_map/finish1/pallas_call | solution.py:653
  102.0 1.4 %table.1 = f32[512,256]{1,0:T(8,128)} custom-call(s32[6]{0:T(128)S(1)} %stack.28.place_ref, f32[8,128]{1,0:T(8,128)S(1)} %get-tuple-element.92.after_ref, bf16[256,256]{1,0:T(8,128)(2,1)S(1)} %share.1.refs_0_, bf16[256,256]{1,0:T(8,128)(2,1)S(1)} %collective-permute-done.31.refs_1_), custom_call_target="tpu_custom_call" | custom-call | tf_op jit(solution)/shard_map/table/pallas_call | solution.py:667
  (39 shorter events, 4.4 us)
Async XLA Ops:
  0.6 16.3 %collective-permute-start = (bf16[512,256]{1,0:T(8,128)(2,1)}, bf16[512,256]{1,0:T(8,128)(2,1)S(1)}, u32[]{:S(2)}, u32[]{:S(2)}) collective-permute-start(bf16[512,256]{1,0:T(8,128)(2,1)} %table_hbm.1), channel_id=1, source_target_pairs={{0,16},{1,17},{2,18},{3,19},{4,20},{5,21},{6,22},{7,23},{8,24},{9,... | collective-permute-start | bytes 786440 | tf_op jit(solution)/shard_map/ppermute | solution.py:470
  17.6 7.4 %collective-permute-start.1 = (bf16[256,256]{1,0:T(8,128)(2,1)S(1)}, bf16[256,256]{1,0:T(8,128)(2,1)S(1)}, u32[]{:S(2)}, u32[]{:S(2)}) collective-permute-start(bf16[256,256]{1,0:T(8,128)(2,1)S(1)} %get-tuple-element.65), channel_id=1, source_target_pairs={{0,12},{1,13},{2,14},{3,15},{4,8},{5,9},{6,10},{7,11},{8,4},{9,5},... | collective-permute-start | bytes 393224 | tf_op jit(solution)/shard_map/ppermute | solution.py:470
  19.3 7.2 %collective-permute-start.2 = (bf16[256,256]{1,0:T(8,128)(2,1)S(1)}, bf16[256,256]{1,0:T(8,128)(2,1)S(1)}, u32[]{:S(2)}, u32[]{:S(2)}) collective-permute-start(bf16[256,256]{1,0:T(8,128)(2,1)S(1)} %get-tuple-element.66), channel_id=1, source_target_pairs={{0,8},{1,9},{2,10},{3,11},{4,12},{5,13},{6,14},{7,15},{8,0},{9,1},... | collective-permute-start | bytes 393224 | tf_op jit(solution)/shard_map/ppermute | solution.py:470
  20.7 7.1 %collective-permute-start.3 = (bf16[256,256]{1,0:T(8,128)(2,1)S(1)}, bf16[256,256]{1,0:T(8,128)(2,1)S(1)}, u32[]{:S(2)}, u32[]{:S(2)}) collective-permute-start(bf16[256,256]{1,0:T(8,128)(2,1)S(1)} %get-tuple-element.67), channel_id=1, source_target_pairs={{0,4},{1,5},{2,6},{3,7},{4,0},{5,1},{6,2},{7,3},{8,12},{9,13},{10,... | collective-permute-start | bytes 393224 | tf_op jit(solution)/shard_map/ppermute | solution.py:470
  21.1 7.7 %collective-permute-start.4 = (bf16[256,256]{1,0:T(8,128)(2,1)S(1)}, bf16[256,256]{1,0:T(8,128)(2,1)S(1)}, u32[]{:S(2)}, u32[]{:S(2)}) collective-permute-start(bf16[256,256]{1,0:T(8,128)(2,1)S(1)} %get-tuple-element.68), channel_id=1, source_target_pairs={{0,14},{1,15},{2,12},{3,13},{4,10},{5,11},{6,8},{7,9},{8,6},{9,7},... | collective-permute-start | bytes 393224 | tf_op jit(solution)/shard_map/ppermute | solution.py:470
  21.6 9.2 %collective-permute-start.5 = (bf16[256,256]{1,0:T(8,128)(2,1)S(1)}, bf16[256,256]{1,0:T(8,128)(2,1)S(1)}, u32[]{:S(2)}, u32[]{:S(2)}) collective-permute-start(bf16[256,256]{1,0:T(8,128)(2,1)S(1)} %get-tuple-element.69), channel_id=1, source_target_pairs={{0,10},{1,11},{2,8},{3,9},{4,14},{5,15},{6,12},{7,13},{8,2},{9,3},... | collective-permute-start | bytes 393224 | tf_op jit(solution)/shard_map/ppermute | solution.py:470
  24.9 7.1 %collective-permute-start.6 = (bf16[256,256]{1,0:T(8,128)(2,1)S(1)}, bf16[256,256]{1,0:T(8,128)(2,1)S(1)}, u32[]{:S(2)}, u32[]{:S(2)}) collective-permute-start(bf16[256,256]{1,0:T(8,128)(2,1)S(1)} %get-tuple-element.70), channel_id=1, source_target_pairs={{0,6},{1,7},{2,4},{3,5},{4,2},{5,3},{6,0},{7,1},{8,14},{9,15},{10,... | collective-permute-start | bytes 393224 | tf_op jit(solution)/shard_map/ppermute | solution.py:470
  26.5 5.5 %collective-permute-start.7 = (bf16[256,256]{1,0:T(8,128)(2,1)S(1)}, bf16[256,256]{1,0:T(8,128)(2,1)S(1)}, u32[]{:S(2)}, u32[]{:S(2)}) collective-permute-start(bf16[256,256]{1,0:T(8,128)(2,1)S(1)} %get-tuple-element.71), channel_id=1, source_target_pairs={{0,2},{1,3},{2,0},{3,1},{4,6},{5,7},{6,4},{7,5},{8,10},{9,11},{10,... | collective-permute-start | bytes 393224 | tf_op jit(solution)/shard_map/ppermute | solution.py:470
  43.5 2.4 %collective-permute-start.8 = (bf16[1552,256]{1,0:T(8,128)(2,1)S(1)}, bf16[1552,256]{1,0:T(8,128)(2,1)S(1)}, u32[]{:S(2)}, u32[]{:S(2)}) collective-permute-start(bf16[1552,256]{1,0:T(8,128)(2,1)S(1)} %get-tuple-element.74), channel_id=1, source_target_pairs={{0,2},{1,3},{2,0},{3,1},{4,6},{5,7},{6,4},{7,5},{8,10},{9,11},{10,... | collective-permute-start | bytes 2383880 | tf_op jit(solution)/shard_map/ppermute | solution.py:470
  44.6 3.6 %collective-permute-start.12 = (bf16[4,256,256]{2,1,0:T(8,128)(2,1)S(1)}, bf16[4,256,256]{2,1,0:T(8,128)(2,1)S(1)}, u32[]{:S(2)}, u32[]{:S(2)}) collective-permute-start(bf16[4,256,256]{2,1,0:T(8,128)(2,1)S(1)} %get-tuple-element.82), channel_id=1, source_target_pairs={{0,2},{1,3},{2,0},{3,1},{4,6},{5,7},{6,4},{7,5},{8,10},{9,11},{10,... | collective-permute-start | bytes 1572872 | tf_op jit(solution)/shard_map/ppermute | solution.py:470
  46.6 8.0 %collective-permute-start.9 = (bf16[400,256]{1,0:T(8,128)(2,1)S(1)}, bf16[400,256]{1,0:T(8,128)(2,1)S(1)}, u32[]{:S(2)}, u32[]{:S(2)}) collective-permute-start(bf16[400,256]{1,0:T(8,128)(2,1)S(1)} %get-tuple-element.77), channel_id=1, source_target_pairs={{0,1},{1,0},{2,3},{3,2},{4,5},{5,4},{6,7},{7,6},{8,9},{9,8},{10,11... | collective-permute-start | bytes 614408 | tf_op jit(solution)/shard_map/ppermute | solution.py:470
  48.2 19.1 %collective-permute-start.13 = (bf16[2,256,256]{2,1,0:T(8,128)(2,1)S(1)}, bf16[2,256,256]{2,1,0:T(8,128)(2,1)S(1)}, u32[]{:S(2)}, u32[]{:S(2)}) collective-permute-start(bf16[2,256,256]{2,1,0:T(8,128)(2,1)S(1)} %get-tuple-element.83), channel_id=1, source_target_pairs={{0,8},{1,9},{2,10},{3,11},{4,12},{5,13},{6,14},{7,15},{8,0},{9,1},... | collective-permute-start | bytes 786440 | tf_op jit(solution)/shard_map/ppermute | solution.py:470
  49.3 18.0 %collective-permute-start.10 = (bf16[400,256]{1,0:T(8,128)(2,1)S(1)}, bf16[400,256]{1,0:T(8,128)(2,1)S(1)}, u32[]{:S(2)}, u32[]{:S(2)}) collective-permute-start(bf16[400,256]{1,0:T(8,128)(2,1)S(1)} %get-tuple-element.78), channel_id=1, source_target_pairs={{0,4},{1,5},{2,6},{3,7},{4,0},{5,1},{6,2},{7,3},{8,12},{9,13},{10,... | collective-permute-start | bytes 614408 | tf_op jit(solution)/shard_map/ppermute | solution.py:470
  50.9 16.5 %collective-permute-start.11 = (bf16[400,256]{1,0:T(8,128)(2,1)S(1)}, bf16[400,256]{1,0:T(8,128)(2,1)S(1)}, u32[]{:S(2)}, u32[]{:S(2)}) collective-permute-start(bf16[400,256]{1,0:T(8,128)(2,1)S(1)} %get-tuple-element.79), channel_id=1, source_target_pairs={{0,5},{1,4},{2,7},{3,6},{4,1},{5,0},{6,3},{7,2},{8,13},{9,12},{10,... | collective-permute-start | bytes 614408 | tf_op jit(solution)/shard_map/ppermute | solution.py:470
  51.4 26.9 %collective-permute-start.27 = (bf16[2,256,256]{2,1,0:T(8,128)(2,1)S(1)}, bf16[2,256,256]{2,1,0:T(8,128)(2,1)S(1)}, u32[]{:S(2)}, u32[]{:S(2)}) collective-permute-start(bf16[2,256,256]{2,1,0:T(8,128)(2,1)S(1)} %get-tuple-element.94), channel_id=1, source_target_pairs={{0,4},{1,5},{2,6},{3,7},{4,0},{5,1},{6,2},{7,3},{8,12},{9,13},{10,... | collective-permute-start | bytes 786440 | tf_op jit(solution)/shard_map/ppermute | solution.py:470
  54.6 23.7 %collective-permute-start.28 = (bf16[2,256,256]{2,1,0:T(8,128)(2,1)S(1)}, bf16[2,256,256]{2,1,0:T(8,128)(2,1)S(1)}, u32[]{:S(2)}, u32[]{:S(2)}) collective-permute-start(bf16[2,256,256]{2,1,0:T(8,128)(2,1)S(1)} %get-tuple-element.95), channel_id=1, source_target_pairs={{0,12},{1,13},{2,14},{3,15},{4,8},{5,9},{6,10},{7,11},{8,4},{9,5},... | collective-permute-start | bytes 786440 | tf_op jit(solution)/shard_map/ppermute | solution.py:470
  68.0 4.8 %collective-permute-start.14 = (bf16[112,256]{1,0:T(8,128)(2,1)S(1)}, bf16[112,256]{1,0:T(8,128)(2,1)S(1)}, u32[]{:S(2)}, u32[]{:S(2)}) collective-permute-start(bf16[112,256]{1,0:T(8,128)(2,1)S(1)} %get-tuple-element.86), channel_id=1, source_target_pairs={{0,8},{1,9},{2,10},{3,11},{4,12},{5,13},{6,14},{7,15},{8,0},{9,1},... | collective-permute-start | bytes 172040 | tf_op jit(solution)/shard_map/ppermute | solution.py:470
  69.0 5.1 %collective-permute-start.15 = (bf16[112,256]{1,0:T(8,128)(2,1)S(1)}, bf16[112,256]{1,0:T(8,128)(2,1)S(1)}, u32[]{:S(2)}, u32[]{:S(2)}) collective-permute-start(bf16[112,256]{1,0:T(8,128)(2,1)S(1)} %get-tuple-element.87), channel_id=1, source_target_pairs={{0,16},{1,17},{2,18},{3,19},{4,20},{5,21},{6,22},{7,23},{8,24},{9,... | collective-permute-start | bytes 172040 | tf_op jit(solution)/shard_map/ppermute | solution.py:470
  71.7 6.0 %collective-permute-start.16 = (bf16[112,256]{1,0:T(8,128)(2,1)S(1)}, bf16[112,256]{1,0:T(8,128)(2,1)S(1)}, u32[]{:S(2)}, u32[]{:S(2)}) collective-permute-start(bf16[112,256]{1,0:T(8,128)(2,1)S(1)} %get-tuple-element.88), channel_id=1, source_target_pairs={{0,24},{1,25},{2,26},{3,27},{4,28},{5,29},{6,30},{7,31},{8,16},{9,... | collective-permute-start | bytes 172040 | tf_op jit(solution)/shard_map/ppermute | solution.py:470
  79.6 11.1 %collective-permute-start.29 = (bf16[512,256]{1,0:T(8,128)(2,1)S(1)}, bf16[512,256]{1,0:T(8,128)(2,1)S(1)}, u32[]{:S(2)}, u32[]{:S(2)}) collective-permute-start(bf16[512,256]{1,0:T(8,128)(2,1)S(1)} %get-tuple-element.98), channel_id=1, source_target_pairs={{0,1},{1,0},{2,3},{3,2},{4,5},{5,4},{6,7},{7,6},{8,9},{9,8},{10,11... | collective-permute-start | bytes 786440 | tf_op jit(solution)/shard_map/ppermute | solution.py:470
  80.2 5.9 %collective-permute-start.19 = (bf16[96,256]{1,0:T(8,128)(2,1)S(1)}, bf16[96,256]{1,0:T(8,128)(2,1)S(1)}, u32[]{:S(2)}, u32[]{:S(2)}) collective-permute-start(bf16[96,256]{1,0:T(8,128)(2,1)S(1)} %get-tuple-element.89.refs_0_.after_ref), channel_id=1, source_target_pairs={{0,24},{1,25},{2,26},{3,27},{4,28},{5,29},{6,30},{7,31},{8,16},{9,... | collective-permute-start | bytes 147464 | tf_op jit(solution)/shard_map/ppermute | solution.py:470
  81.5 5.7 %collective-permute-start.18 = (bf16[96,256]{1,0:T(8,128)(2,1)S(1)}, bf16[96,256]{1,0:T(8,128)(2,1)S(1)}, u32[]{:S(2)}, u32[]{:S(2)}) collective-permute-start(bf16[96,256]{1,0:T(8,128)(2,1)S(1)} %get-tuple-element.89.refs_0_.after_ref), channel_id=1, source_target_pairs={{0,16},{1,17},{2,18},{3,19},{4,20},{5,21},{6,22},{7,23},{8,24},{9,... | collective-permute-start | bytes 147464 | tf_op jit(solution)/shard_map/ppermute | solution.py:470
  81.6 5.6 %collective-permute-start.17 = (bf16[96,256]{1,0:T(8,128)(2,1)S(1)}, bf16[96,256]{1,0:T(8,128)(2,1)S(1)}, u32[]{:S(2)}, u32[]{:S(2)}) collective-permute-start(bf16[96,256]{1,0:T(8,128)(2,1)S(1)} %get-tuple-element.89.refs_0_.after_ref), channel_id=1, source_target_pairs={{0,8},{1,9},{2,10},{3,11},{4,12},{5,13},{6,14},{7,15},{8,0},{9,1},... | collective-permute-start | bytes 147464 | tf_op jit(solution)/shard_map/ppermute | solution.py:470
  87.2 6.7 %collective-permute-start.24 = (bf16[384,256]{1,0:T(8,128)(2,1)S(1)}, bf16[384,256]{1,0:T(8,128)(2,1)S(1)}, u32[]{:S(2)}, u32[]{:S(2)}) collective-permute-start(bf16[384,256]{1,0:T(8,128)(2,1)S(1)} %line.1.refs_0_.after_ref), channel_id=1, source_target_pairs={{0,5},{1,4},{2,7},{3,6},{4,1},{5,0},{6,3},{7,2},{8,13},{9,12},{10,... | collective-permute-start | bytes 589832 | tf_op jit(solution)/shard_map/ppermute | solution.py:470
  89.5 6.4 %collective-permute-start.22 = (bf16[384,256]{1,0:T(8,128)(2,1)S(1)}, bf16[384,256]{1,0:T(8,128)(2,1)S(1)}, u32[]{:S(2)}, u32[]{:S(2)}) collective-permute-start(bf16[384,256]{1,0:T(8,128)(2,1)S(1)} %line.1.refs_0_.after_ref), channel_id=1, source_target_pairs={{0,4},{1,5},{2,6},{3,7},{4,0},{5,1},{6,2},{7,3},{8,12},{9,13},{10,... | collective-permute-start | bytes 589832 | tf_op jit(solution)/shard_map/ppermute | solution.py:470
  90.2 5.7 %collective-permute-start.20 = (bf16[384,256]{1,0:T(8,128)(2,1)S(1)}, bf16[384,256]{1,0:T(8,128)(2,1)S(1)}, u32[]{:S(2)}, u32[]{:S(2)}) collective-permute-start(bf16[384,256]{1,0:T(8,128)(2,1)S(1)} %line.1.refs_0_.after_ref), channel_id=1, source_target_pairs={{0,1},{1,0},{2,3},{3,2},{4,5},{5,4},{6,7},{7,6},{8,9},{9,8},{10,11... | collective-permute-start | bytes 589832 | tf_op jit(solution)/shard_map/ppermute | solution.py:470
  90.8 5.9 %collective-permute-start.30 = (bf16[256,256]{1,0:T(8,128)(2,1)S(1)}, bf16[256,256]{1,0:T(8,128)(2,1)S(1)}, u32[]{:S(2)}, u32[]{:S(2)}) collective-permute-start(bf16[256,256]{1,0:T(8,128)(2,1)S(1)} %get-tuple-element.100), channel_id=1, source_target_pairs={{0,16},{1,17},{2,18},{3,19},{4,20},{5,21},{6,22},{7,23},{8,24},{9,... | collective-permute-start | bytes 393224 | tf_op jit(solution)/shard_map/ppermute | solution.py:470
  92.2 6.2 %collective-permute-start.26 = (bf16[384,256]{1,0:T(8,128)(2,1)S(1)}, bf16[384,256]{1,0:T(8,128)(2,1)S(1)}, u32[]{:S(2)}, u32[]{:S(2)}) collective-permute-start(bf16[384,256]{1,0:T(8,128)(2,1)S(1)} %line.1.refs_0_.after_ref), channel_id=1, source_target_pairs={{0,2},{1,3},{2,0},{3,1},{4,6},{5,7},{6,4},{7,5},{8,10},{9,11},{10,... | collective-permute-start | bytes 589832 | tf_op jit(solution)/shard_map/ppermute | solution.py:470
  93.9 6.3 %collective-permute-start.25 = (bf16[384,256]{1,0:T(8,128)(2,1)S(1)}, bf16[384,256]{1,0:T(8,128)(2,1)S(1)}, u32[]{:S(2)}, u32[]{:S(2)}) collective-permute-start(bf16[384,256]{1,0:T(8,128)(2,1)S(1)} %collective-permute-done.24.refs_3_.after_ref), channel_id=1, source_target_pairs={{0,2},{1,3},{2,0},{3,1},{4,6},{5,7},{6,4},{7,5},{8,10},{9,11},{10,... | collective-permute-start | bytes 589832 | tf_op jit(solution)/shard_map/ppermute | solution.py:470
  95.9 4.3 %collective-permute-start.23 = (bf16[384,256]{1,0:T(8,128)(2,1)S(1)}, bf16[384,256]{1,0:T(8,128)(2,1)S(1)}, u32[]{:S(2)}, u32[]{:S(2)}) collective-permute-start(bf16[384,256]{1,0:T(8,128)(2,1)S(1)} %collective-permute-done.22.refs_2_), channel_id=1, source_target_pairs={{0,2},{1,3},{2,0},{3,1},{4,6},{5,7},{6,4},{7,5},{8,10},{9,11},{10,... | collective-permute-start | bytes 589832 | tf_op jit(solution)/shard_map/ppermute | solution.py:470
  95.9 4.3 %collective-permute-start.21 = (bf16[384,256]{1,0:T(8,128)(2,1)S(1)}, bf16[384,256]{1,0:T(8,128)(2,1)S(1)}, u32[]{:S(2)}, u32[]{:S(2)}) collective-permute-start(bf16[384,256]{1,0:T(8,128)(2,1)S(1)} %collective-permute-done.20.refs_1_), channel_id=1, source_target_pairs={{0,2},{1,3},{2,0},{3,1},{4,6},{5,7},{6,4},{7,5},{8,10},{9,11},{10,... | collective-permute-start | bytes 589832 | tf_op jit(solution)/shard_map/ppermute | solution.py:470
  96.8 5.2 %collective-permute-start.31 = (bf16[256,256]{1,0:T(8,128)(2,1)S(1)}, bf16[256,256]{1,0:T(8,128)(2,1)S(1)}, u32[]{:S(2)}, u32[]{:S(2)}) collective-permute-start(bf16[256,256]{1,0:T(8,128)(2,1)S(1)} %share.1.refs_0_), channel_id=1, source_target_pairs={{0,1},{1,0},{2,3},{3,2},{4,5},{5,4},{6,7},{7,6},{8,9},{9,8},{10,11... | collective-permute-start | bytes 393224 | tf_op jit(solution)/shard_map/ppermute | solution.py:470

commit v4 on v3

--- a/solution.py
+++ b/solution.py
@@ -167,8 +167,8 @@
         ),
         pltpu.make_async_copy(upstream_hbm, upstream_ref, sems.at[1]),
     ]
-    for copy in copies:
-        copy.start()
+    copies[0].start()
+    copies[1].start()
     order = ordered(len(arrived_refs))
     fetched_refs = [arrived_refs[order.index(step)] for step in range(len(order))]
     g_ref, keep_ref, sent_ref, block_ref = refs[:4]
@@ -195,7 +195,6 @@
         for side in range(2):
             h_s[side, start : start + PAD, :] = jnp.zeros((PAD, width), F32)
             dconv_s[side, start + length : start + length + PAD, :] = jnp.zeros((PAD, width), F32)
-    dw_s[...] = jnp.zeros(dw_s.shape, F32)
 
     copies[0].wait()
 
@@ -228,6 +227,9 @@
     for layer in range(layers):
         dilation = 2**layer
         copies[1 + layer].wait()
+        if layer == 0:
+            for copy in copies[2:]:
+                copy.start()
         for start in range(0, taps, width):
             value = weight_ref[layer, start : start + width, :]
             rounded_s[layer, start : start + width, :] = value.astype(BF16)
@@ -256,12 +258,11 @@
                     x_s[at(seq, j), :] = value
                     normalise(seq, j, layer + 1, value)
 
-    def weigh(seq, layer):
-        whole = pl.ds(seq * length, length)
-        term = dot(hidden_s[layer, whole, :], spread_s[layer % 2, whole, :], (0, 0))
+    def weigh(layer):
+        term = dot(hidden_s[layer], spread_s[layer % 2], (0, 0))
         for tap in range(steps):
             rows = pl.ds(layer * taps + tap * width, width)
-            dw_s[rows, :] += term[:, tap * width : (tap + 1) * width]
+            dw_s[rows, :] = term[:, tap * width : (tap + 1) * width]
 
     copies[-1].wait()
     for seq in range(batches):
@@ -275,9 +276,9 @@
         dilation = 2**layer
 
         total = jnp.zeros((8, width), F32)
+        if layer + 1 < layers:
+            weigh(layer + 1)
         for seq in range(batches):
-            if layer + 1 < layers:
-                weigh(seq, layer + 1)
             for j in range(per):
                 view = dconv_s[layer % 2, inside(seq, j, 0, CHUNK + PAD), :]
                 spread = jnp.concatenate(
@@ -309,8 +310,7 @@
                 total = total + jnp.sum(product.reshape(CHUNK // 8, 8, width), axis=0)
         gains[layer] = jnp.sum(total, axis=0, keepdims=True)
 
-    for batch in range(batches):
-        weigh(batch, 0)
+    weigh(0)
     half = keep_ref.shape[0]
     mine = place_ref[0]
     keep_ref[...] = dw_s[pl.ds(pl.multiple_of(mine * half, half), half), :].astype(BF16)

time: 104 us -> 104 us (level)
  no operation moved by 1% of the time
where the time goes in v4:
time: 104 us; the launch traced here: 103 us
  starting transfers between devices  36 us (35%)
  waiting for transfers between devices  33.2 us (32%)
  Pallas kernels  24 us (23%)
  blocking collectives  8.43 us (8%)
    ppermute x32, starting transfers between devices, swap(): return lax.ppermute(value, axes, [(i, i ^ mask) for i in range(devices)])  36 us
    ppermute x32, waiting for transfers between devices, swap(): return lax.ppermute(value, axes, [(i, i ^ mask) for i in range(devices)])  33.2 us
    pallas_call x1, Pallas kernels, body(): pl.pallas_call(stack_kernel, out_shape=(shape((tokens, width), BF16), sha...  11.5 us
    all_to_all x1, blocking collectives, exchange(): lax.all_to_all(value, 'emb', split_axis=0, concat_axis=0, axis_index_grou...  8.43 us
    pallas_call x2, Pallas kernels, body(): pl.pallas_call(functools.partial(finish_kernel, 2 ** len(stages[2]), scal...  3.49 us
  transfers between devices with their start and end apart: 32, of which 18 were waited for; matrix products, arithmetic and copies ran while one was open for 1% of the time, Pallas kernels for 9%

profile of v4, /device:TPU:0, one launch (start us, length us, event | category | flops | bytes accessed | tf_op | source)
XLA Modules:
  0.0 103.4 jit_solution(11574094133772196461)
XLA Ops:
  0.6 4.1 %collective-permute-start = (bf16[512,256]{1,0:T(8,128)(2,1)}, bf16[512,256]{1,0:T(8,128)(2,1)S(1)}, u32[]{:S(2)}, u32[]{:S(2)}) collective-permute-start(bf16[512,256]{1,0:T(8,128)(2,1)} %table_hbm.1), channel_id=1, source_target_pairs={{0,16},{1,17},{2,18},{3,19},{4,20},{5,21},{6,22},{7,23},{8,24},{9,... | collective-permute-start | bytes 786440 | tf_op jit(solution)/shard_map/ppermute | solution.py:470
  4.8 0.7 bitcast_add_fusion.ids_ref
  5.5 1.5 %request.1 = (s32[8,256]{1,0:T(8,128)S(1)}, s32[2,512]{1,0:T(2,128)S(1)}, bf16[512,256]{1,0:T(8,128)(2,1)S(1)}) custom-call(s32[6]{0:T(128)S(1)} %stack.28.place_ref, s32[2,512]{1,0:T(2,128)S(1)} %bitcast_add_fusion.ids_ref, bf16[512,256]{1,0:T(8,128)(2,1)} %table_hbm.1), custom_call_target="tpu_custom_call" | custom-call | tf_op jit(solution)/shard_map/request/pallas_call | solution.py:483
  7.0 8.4 %all_to_all.11 = s32[8,1,256]{2,1,0:T(1,128)S(1)} all-to-all(s32[8,1,256]{2,1,0:T(1,128)S(1)} %copy.14), channel_id=1, replica_groups={{0,2,4,6,8,10,12,14},{16,18,20,22,24,26,28,30},{1,3,5,7,9,11,13,15},{17..., dimensions={0} | all-to-all | bytes 16384 | tf_op jit(solution)/shard_map/all_to_all | solution.py:476
  15.5 1.1 %near.1 = (s32[8,256]{1,0:T(8,128)S(1)}, bf16[128,256]{1,0:T(8,128)(2,1)S(1)}, bf16[128,256]{1,0:T(8,128)(2,1)S(1)}, bf16[128,256]{1,0:T(8,128)(2,1)S(1)}, bf16[...) custom-call(s32[6]{0:T(128)S(1)} %stack.28.place_ref, ...), custom_call_target="tpu_custom_call" | custom-call | tf_op jit(solution)/shard_map/near/pallas_call | solution.py:497
  17.0 0.6 far.1
  17.6 1.8 %collective-permute-start.1 = (bf16[256,256]{1,0:T(8,128)(2,1)S(1)}, bf16[256,256]{1,0:T(8,128)(2,1)S(1)}, u32[]{:S(2)}, u32[]{:S(2)}) collective-permute-start(bf16[256,256]{1,0:T(8,128)(2,1)S(1)} %get-tuple-element.65), channel_id=1, source_target_pairs={{0,12},{1,13},{2,14},{3,15},{4,8},{5,9},{6,10},{7,11},{8,4},{9,5},... | collective-permute-start | bytes 393224 | tf_op jit(solution)/shard_map/ppermute | solution.py:470
  19.3 1.3 %collective-permute-start.2 = (bf16[256,256]{1,0:T(8,128)(2,1)S(1)}, bf16[256,256]{1,0:T(8,128)(2,1)S(1)}, u32[]{:S(2)}, u32[]{:S(2)}) collective-permute-start(bf16[256,256]{1,0:T(8,128)(2,1)S(1)} %get-tuple-element.66), channel_id=1, source_target_pairs={{0,8},{1,9},{2,10},{3,11},{4,12},{5,13},{6,14},{7,15},{8,0},{9,1},... | collective-permute-start | bytes 393224 | tf_op jit(solution)/shard_map/ppermute | solution.py:470
  21.6 2.3 %collective-permute-start.5 = (bf16[256,256]{1,0:T(8,128)(2,1)S(1)}, bf16[256,256]{1,0:T(8,128)(2,1)S(1)}, u32[]{:S(2)}, u32[]{:S(2)}) collective-permute-start(bf16[256,256]{1,0:T(8,128)(2,1)S(1)} %get-tuple-element.69), channel_id=1, source_target_pairs={{0,10},{1,11},{2,8},{3,9},{4,14},{5,15},{6,12},{7,13},{8,2},{9,3},... | collective-permute-start | bytes 393224 | tf_op jit(solution)/shard_map/ppermute | solution.py:470
  23.9 1.1 %collective-permute-done.1.refs_1_ = bf16[256,256]{1,0:T(8,128)(2,1)S(1)} collective-permute-done((bf16[256,256]{1,0:T(8,128)(2,1)S(1)}, bf16[256,256]{1,0:T(8,128)(2,1)S(1)}, u32[]{:S(2)}, u32[]{:S(2)}) %collective-permute-start.1) | collective-permute-done | bytes 131104 | tf_op jit(solution)/shard_map/ppermute | solution.py:470
  24.9 1.6 %collective-permute-done.2.refs_2_ = bf16[256,256]{1,0:T(8,128)(2,1)S(1)} collective-permute-done((bf16[256,256]{1,0:T(8,128)(2,1)S(1)}, bf16[256,256]{1,0:T(8,128)(2,1)S(1)}, u32[]{:S(2)}, u32[]{:S(2)}) %collective-permute-start.2) | collective-permute-done | bytes 131104 | tf_op jit(solution)/shard_map/ppermute | solution.py:470
  26.8 0.9 collective-permute-done.3.refs_3_
  27.7 1.1 %collective-permute-done.4.refs_4_ = bf16[256,256]{1,0:T(8,128)(2,1)S(1)} collective-permute-done((bf16[256,256]{1,0:T(8,128)(2,1)S(1)}, bf16[256,256]{1,0:T(8,128)(2,1)S(1)}, u32[]{:S(2)}, u32[]{:S(2)}) %collective-permute-start.4) | collective-permute-done | bytes 131104 | tf_op jit(solution)/shard_map/ppermute | solution.py:470
  28.8 2.0 %collective-permute-done.5.refs_5_ = bf16[256,256]{1,0:T(8,128)(2,1)S(1)} collective-permute-done((bf16[256,256]{1,0:T(8,128)(2,1)S(1)}, bf16[256,256]{1,0:T(8,128)(2,1)S(1)}, u32[]{:S(2)}, u32[]{:S(2)}) %collective-permute-start.5) | collective-permute-done | bytes 131104 | tf_op jit(solution)/shard_map/ppermute | solution.py:470
  30.8 1.3 %collective-permute-done.6.refs_6_ = bf16[256,256]{1,0:T(8,128)(2,1)S(1)} collective-permute-done((bf16[256,256]{1,0:T(8,128)(2,1)S(1)}, bf16[256,256]{1,0:T(8,128)(2,1)S(1)}, u32[]{:S(2)}, u32[]{:S(2)}) %collective-permute-start.6) | collective-permute-done | bytes 131104 | tf_op jit(solution)/shard_map/ppermute | solution.py:470
  32.1 11.5 %stack.29 = (bf16[1024,256]{1,0:T(8,128)(2,1)S(1)}, bf16[1536,256]{1,0:T(8,128)(2,1)S(1)}, bf16[1552,256]{1,0:T(8,128)(2,1)S(1)}, bf16[16,256]{1,0:T(8,128)(2,1)S(1)}) custom-call(s32[6]{0:T(128)S(1)} %stack.28.place_ref, s32[1024,1]{1,0:T(8,128)S(1)} %bitcast.18, f32[4,768,256]{2,1,0:T(8,128)} %weight_hbm.1, f32[4,256]{1,0:T(4,128)} %gain_hbm.1, ...), custom_call_target="tpu_custom_call" | custom-call | tf_op jit(solution)/shard_map/stack/pallas_call | solution.py:519
  43.6 0.9 place.1
  45.1 0.8 collective-permute-done.8.refs_0_
  45.9 0.7 fold0.1
  46.6 1.5 %collective-permute-start.9 = (bf16[400,256]{1,0:T(8,128)(2,1)S(1)}, bf16[400,256]{1,0:T(8,128)(2,1)S(1)}, u32[]{:S(2)}, u32[]{:S(2)}) collective-permute-start(bf16[400,256]{1,0:T(8,128)(2,1)S(1)} %get-tuple-element.77), channel_id=1, source_target_pairs={{0,1},{1,0},{2,3},{3,2},{4,5},{5,4},{6,7},{7,6},{8,9},{9,8},{10,11... | collective-permute-start | bytes 614408 | tf_op jit(solution)/shard_map/ppermute | solution.py:470
  48.2 1.1 %collective-permute-start.13 = (bf16[2,256,256]{2,1,0:T(8,128)(2,1)S(1)}, bf16[2,256,256]{2,1,0:T(8,128)(2,1)S(1)}, u32[]{:S(2)}, u32[]{:S(2)}) collective-permute-start(bf16[2,256,256]{2,1,0:T(8,128)(2,1)S(1)} %get-tuple-element.83), channel_id=1, source_target_pairs={{0,8},{1,9},{2,10},{3,11},{4,12},{5,13},{6,14},{7,15},{8,0},{9,1},... | collective-permute-start | bytes 786440 | tf_op jit(solution)/shard_map/ppermute | solution.py:470
  49.4 1.5 %collective-permute-start.10 = (bf16[400,256]{1,0:T(8,128)(2,1)S(1)}, bf16[400,256]{1,0:T(8,128)(2,1)S(1)}, u32[]{:S(2)}, u32[]{:S(2)}) collective-permute-start(bf16[400,256]{1,0:T(8,128)(2,1)S(1)} %get-tuple-element.78), channel_id=1, source_target_pairs={{0,4},{1,5},{2,6},{3,7},{4,0},{5,1},{6,2},{7,3},{8,12},{9,13},{10,... | collective-permute-start | bytes 614408 | tf_op jit(solution)/shard_map/ppermute | solution.py:470
  51.4 1.5 %collective-permute-start.27 = (bf16[2,256,256]{2,1,0:T(8,128)(2,1)S(1)}, bf16[2,256,256]{2,1,0:T(8,128)(2,1)S(1)}, u32[]{:S(2)}, u32[]{:S(2)}) collective-permute-start(bf16[2,256,256]{2,1,0:T(8,128)(2,1)S(1)} %get-tuple-element.94), channel_id=1, source_target_pairs={{0,4},{1,5},{2,6},{3,7},{4,0},{5,1},{6,2},{7,3},{8,12},{9,13},{10,... | collective-permute-start | bytes 786440 | tf_op jit(solution)/shard_map/ppermute | solution.py:470
  52.9 1.7 %collective-permute-done.9.refs_0_ = bf16[400,256]{1,0:T(8,128)(2,1)S(1)} collective-permute-done((bf16[400,256]{1,0:T(8,128)(2,1)S(1)}, bf16[400,256]{1,0:T(8,128)(2,1)S(1)}, u32[]{:S(2)}, u32[]{:S(2)}) %collective-permute-start.9) | collective-permute-done | bytes 204832 | tf_op jit(solution)/shard_map/ppermute | solution.py:470
  54.6 2.0 %collective-permute-start.28 = (bf16[2,256,256]{2,1,0:T(8,128)(2,1)S(1)}, bf16[2,256,256]{2,1,0:T(8,128)(2,1)S(1)}, u32[]{:S(2)}, u32[]{:S(2)}) collective-permute-start(bf16[2,256,256]{2,1,0:T(8,128)(2,1)S(1)} %get-tuple-element.95), channel_id=1, source_target_pairs={{0,12},{1,13},{2,14},{3,15},{4,8},{5,9},{6,10},{7,11},{8,4},{9,5},... | collective-permute-start | bytes 786440 | tf_op jit(solution)/shard_map/ppermute | solution.py:470
  56.6 10.8 %collective-permute-done.10.refs_1_ = bf16[400,256]{1,0:T(8,128)(2,1)S(1)} collective-permute-done((bf16[400,256]{1,0:T(8,128)(2,1)S(1)}, bf16[400,256]{1,0:T(8,128)(2,1)S(1)}, u32[]{:S(2)}, u32[]{:S(2)}) %collective-permute-start.10) | collective-permute-done | bytes 204832 | tf_op jit(solution)/shard_map/ppermute | solution.py:470
  67.4 0.6 fold1.1
  68.0 1.0 %collective-permute-start.14 = (bf16[112,256]{1,0:T(8,128)(2,1)S(1)}, bf16[112,256]{1,0:T(8,128)(2,1)S(1)}, u32[]{:S(2)}, u32[]{:S(2)}) collective-permute-start(bf16[112,256]{1,0:T(8,128)(2,1)S(1)} %get-tuple-element.86), channel_id=1, source_target_pairs={{0,8},{1,9},{2,10},{3,11},{4,12},{5,13},{6,14},{7,15},{8,0},{9,1},... | collective-permute-start | bytes 172040 | tf_op jit(solution)/shard_map/ppermute | solution.py:470
  69.1 2.7 %collective-permute-start.15 = (bf16[112,256]{1,0:T(8,128)(2,1)S(1)}, bf16[112,256]{1,0:T(8,128)(2,1)S(1)}, u32[]{:S(2)}, u32[]{:S(2)}) collective-permute-start(bf16[112,256]{1,0:T(8,128)(2,1)S(1)} %get-tuple-element.87), channel_id=1, source_target_pairs={{0,16},{1,17},{2,18},{3,19},{4,20},{5,21},{6,22},{7,23},{8,24},{9,... | collective-permute-start | bytes 172040 | tf_op jit(solution)/shard_map/ppermute | solution.py:470
  71.7 1.1 %collective-permute-start.16 = (bf16[112,256]{1,0:T(8,128)(2,1)S(1)}, bf16[112,256]{1,0:T(8,128)(2,1)S(1)}, u32[]{:S(2)}, u32[]{:S(2)}) collective-permute-start(bf16[112,256]{1,0:T(8,128)(2,1)S(1)} %get-tuple-element.88), channel_id=1, source_target_pairs={{0,24},{1,25},{2,26},{3,27},{4,28},{5,29},{6,30},{7,31},{8,16},{9,... | collective-permute-start | bytes 172040 | tf_op jit(solution)/shard_map/ppermute | solution.py:470
  72.8 1.3 %collective-permute-done.15.refs_1_ = bf16[112,256]{1,0:T(8,128)(2,1)S(1)} collective-permute-done((bf16[112,256]{1,0:T(8,128)(2,1)S(1)}, bf16[112,256]{1,0:T(8,128)(2,1)S(1)}, u32[]{:S(2)}, u32[]{:S(2)}) %collective-permute-start.15) | collective-permute-done | bytes 57376 | tf_op jit(solution)/shard_map/ppermute | solution.py:470
  74.1 3.6 %collective-permute-done.16.refs_2_ = bf16[112,256]{1,0:T(8,128)(2,1)S(1)} collective-permute-done((bf16[112,256]{1,0:T(8,128)(2,1)S(1)}, bf16[112,256]{1,0:T(8,128)(2,1)S(1)}, u32[]{:S(2)}, u32[]{:S(2)}) %collective-permute-start.16) | collective-permute-done | bytes 57376 | tf_op jit(solution)/shard_map/ppermute | solution.py:470
  77.7 0.6 last.1
  78.3 1.3 %collect.1 = (f32[256,256]{1,0:T(8,128)S(1)}, f32[256,256]{1,0:T(8,128)S(1)}, bf16[512,256]{1,0:T(8,128)(2,1)S(1)}) custom-call(s32[6]{0:T(128)S(1)} %stack.28.place_ref, s32[8,256]{1,0:T(8,128)S(1)} %get-tuple-element.55.asked_ref, bf16[96,256]{1,0:T(8,128)(2,1)S(1)} %get-tuple-element.89.refs_0_.after_ref, ...), custom_call_target="tpu_custom_call" | custom-call | tf_op jit(solution)/shard_map/collect/pallas_call | solution.py:607
  79.7 0.6 collective-permute-start.29
  80.3 1.2 %collective-permute-start.19 = (bf16[96,256]{1,0:T(8,128)(2,1)S(1)}, bf16[96,256]{1,0:T(8,128)(2,1)S(1)}, u32[]{:S(2)}, u32[]{:S(2)}) collective-permute-start(bf16[96,256]{1,0:T(8,128)(2,1)S(1)} %get-tuple-element.89.refs_0_.after_ref), channel_id=1, source_target_pairs={{0,24},{1,25},{2,26},{3,27},{4,28},{5,29},{6,30},{7,31},{8,16},{9,... | collective-permute-start | bytes 147464 | tf_op jit(solution)/shard_map/ppermute | solution.py:470
  81.6 3.1 %collective-permute-start.17 = (bf16[96,256]{1,0:T(8,128)(2,1)S(1)}, bf16[96,256]{1,0:T(8,128)(2,1)S(1)}, u32[]{:S(2)}, u32[]{:S(2)}) collective-permute-start(bf16[96,256]{1,0:T(8,128)(2,1)S(1)} %get-tuple-element.89.refs_0_.after_ref), channel_id=1, source_target_pairs={{0,8},{1,9},{2,10},{3,11},{4,12},{5,13},{6,14},{7,15},{8,0},{9,1},... | collective-permute-start | bytes 147464 | tf_op jit(solution)/shard_map/ppermute | solution.py:470
  84.7 1.5 %collective-permute-done.19.refs_3_ = bf16[96,256]{1,0:T(8,128)(2,1)S(1)} collective-permute-done((bf16[96,256]{1,0:T(8,128)(2,1)S(1)}, bf16[96,256]{1,0:T(8,128)(2,1)S(1)}, u32[]{:S(2)}, u32[]{:S(2)}) %collective-permute-start.19) | collective-permute-done | bytes 49184 | tf_op jit(solution)/shard_map/ppermute | solution.py:470
  86.2 1.1 %collective-permute-done.18.refs_2_ = bf16[96,256]{1,0:T(8,128)(2,1)S(1)} collective-permute-done((bf16[96,256]{1,0:T(8,128)(2,1)S(1)}, bf16[96,256]{1,0:T(8,128)(2,1)S(1)}, u32[]{:S(2)}, u32[]{:S(2)}) %collective-permute-start.18) | collective-permute-done | bytes 49184 | tf_op jit(solution)/shard_map/ppermute | solution.py:470
  87.2 2.3 %collective-permute-start.24 = (bf16[384,256]{1,0:T(8,128)(2,1)S(1)}, bf16[384,256]{1,0:T(8,128)(2,1)S(1)}, u32[]{:S(2)}, u32[]{:S(2)}) collective-permute-start(bf16[384,256]{1,0:T(8,128)(2,1)S(1)} %line.1.refs_0_.after_ref), channel_id=1, source_target_pairs={{0,5},{1,4},{2,7},{3,6},{4,1},{5,0},{6,3},{7,2},{8,13},{9,12},{10,... | collective-permute-start | bytes 589832 | tf_op jit(solution)/shard_map/ppermute | solution.py:470
  89.6 0.7 collective-permute-start.22
  90.9 1.4 %collective-permute-start.30 = (bf16[256,256]{1,0:T(8,128)(2,1)S(1)}, bf16[256,256]{1,0:T(8,128)(2,1)S(1)}, u32[]{:S(2)}, u32[]{:S(2)}) collective-permute-start(bf16[256,256]{1,0:T(8,128)(2,1)S(1)} %get-tuple-element.100), channel_id=1, source_target_pairs={{0,16},{1,17},{2,18},{3,19},{4,20},{5,21},{6,22},{7,23},{8,24},{9,... | collective-permute-start | bytes 393224 | tf_op jit(solution)/shard_map/ppermute | solution.py:470
  92.2 1.7 %collective-permute-done.24.refs_3_.after_ref = bf16[384,256]{1,0:T(8,128)(2,1)S(1)} collective-permute-done((bf16[384,256]{1,0:T(8,128)(2,1)S(1)}, bf16[384,256]{1,0:T(8,128)(2,1)S(1)}, u32[]{:S(2)}, u32[]{:S(2)}) %collective-permute-start.24) | collective-permute-done | bytes 196640 | tf_op jit(solution)/shard_map/ppermute | solution.py:470
  94.0 2.0 %collective-permute-done.22.refs_2_ = bf16[384,256]{1,0:T(8,128)(2,1)S(1)} collective-permute-done((bf16[384,256]{1,0:T(8,128)(2,1)S(1)}, bf16[384,256]{1,0:T(8,128)(2,1)S(1)}, u32[]{:S(2)}, u32[]{:S(2)}) %collective-permute-start.22) | collective-permute-done | bytes 196640 | tf_op jit(solution)/shard_map/ppermute | solution.py:470
  96.8 1.6 %collective-permute-start.31 = (bf16[256,256]{1,0:T(8,128)(2,1)S(1)}, bf16[256,256]{1,0:T(8,128)(2,1)S(1)}, u32[]{:S(2)}, u32[]{:S(2)}) collective-permute-start(bf16[256,256]{1,0:T(8,128)(2,1)S(1)} %share.1.refs_0_), channel_id=1, source_target_pairs={{0,1},{1,0},{2,3},{3,2},{4,5},{5,4},{6,7},{7,6},{8,9},{9,8},{10,11... | collective-permute-start | bytes 393224 | tf_op jit(solution)/shard_map/ppermute | solution.py:470
  98.4 1.9 %finish0.1.refs_3_ = f32[3072,256]{1,0:T(8,128)} custom-call(s32[6]{0:T(128)S(1)} %stack.28.place_ref, bf16[384,256]{1,0:T(8,128)(2,1)S(1)} %line.1.refs_0_.after_ref, bf16[384,256]{1,0:T(8,128)(2,1)S(1)} %collective-permute-done.20.refs_1_, bf16[384,256]{1,0:T(8,128)(2,1)S(1)} %collective-permute-done.22.refs_2_, ...), custom_call_target="tpu_custom_call" | custom-call | tf_op jit(solution)/shard_map/finish0/pallas_call | solution.py:653
  100.3 1.6 %finish1.1 = (f32[3072,256]{1,0:T(8,128)}, f32[8,128]{1,0:T(8,128)S(1)}) custom-call(s32[6]{0:T(128)S(1)} %stack.28.place_ref, bf16[384,256]{1,0:T(8,128)(2,1)S(1)} %collective-permute-done.21.refs_0_, bf16[384,256]{1,0:T(8,128)(2,1)S(1)} %collective-permute-done.23.refs_1_, ...), custom_call_target="tpu_custom_call", output_to_operand_aliasing={{0}: (4, {})} | custom-call | tf_op jit(solution)/shard_map/finish1/pallas_call | solution.py:653
  102.0 1.4 %table.1 = f32[512,256]{1,0:T(8,128)} custom-call(s32[6]{0:T(128)S(1)} %stack.28.place_ref, f32[8,128]{1,0:T(8,128)S(1)} %get-tuple-element.92.after_ref, bf16[256,256]{1,0:T(8,128)(2,1)S(1)} %share.1.refs_0_, bf16[256,256]{1,0:T(8,128)(2,1)S(1)} %collective-permute-done.31.refs_1_), custom_call_target="tpu_custom_call" | custom-call | tf_op jit(solution)/shard_map/table/pallas_call | solution.py:667
  (39 shorter events, 4.4 us)
Async XLA Ops:
  0.6 16.3 %collective-permute-start = (bf16[512,256]{1,0:T(8,128)(2,1)}, bf16[512,256]{1,0:T(8,128)(2,1)S(1)}, u32[]{:S(2)}, u32[]{:S(2)}) collective-permute-start(bf16[512,256]{1,0:T(8,128)(2,1)} %table_hbm.1), channel_id=1, source_target_pairs={{0,16},{1,17},{2,18},{3,19},{4,20},{5,21},{6,22},{7,23},{8,24},{9,... | collective-permute-start | bytes 786440 | tf_op jit(solution)/shard_map/ppermute | solution.py:470
  17.6 7.4 %collective-permute-start.1 = (bf16[256,256]{1,0:T(8,128)(2,1)S(1)}, bf16[256,256]{1,0:T(8,128)(2,1)S(1)}, u32[]{:S(2)}, u32[]{:S(2)}) collective-permute-start(bf16[256,256]{1,0:T(8,128)(2,1)S(1)} %get-tuple-element.65), channel_id=1, source_target_pairs={{0,12},{1,13},{2,14},{3,15},{4,8},{5,9},{6,10},{7,11},{8,4},{9,5},... | collective-permute-start | bytes 393224 | tf_op jit(solution)/shard_map/ppermute | solution.py:470
  19.3 7.2 %collective-permute-start.2 = (bf16[256,256]{1,0:T(8,128)(2,1)S(1)}, bf16[256,256]{1,0:T(8,128)(2,1)S(1)}, u32[]{:S(2)}, u32[]{:S(2)}) collective-permute-start(bf16[256,256]{1,0:T(8,128)(2,1)S(1)} %get-tuple-element.66), channel_id=1, source_target_pairs={{0,8},{1,9},{2,10},{3,11},{4,12},{5,13},{6,14},{7,15},{8,0},{9,1},... | collective-permute-start | bytes 393224 | tf_op jit(solution)/shard_map/ppermute | solution.py:470
  20.7 7.1 %collective-permute-start.3 = (bf16[256,256]{1,0:T(8,128)(2,1)S(1)}, bf16[256,256]{1,0:T(8,128)(2,1)S(1)}, u32[]{:S(2)}, u32[]{:S(2)}) collective-permute-start(bf16[256,256]{1,0:T(8,128)(2,1)S(1)} %get-tuple-element.67), channel_id=1, source_target_pairs={{0,4},{1,5},{2,6},{3,7},{4,0},{5,1},{6,2},{7,3},{8,12},{9,13},{10,... | collective-permute-start | bytes 393224 | tf_op jit(solution)/shard_map/ppermute | solution.py:470
  21.1 7.7 %collective-permute-start.4 = (bf16[256,256]{1,0:T(8,128)(2,1)S(1)}, bf16[256,256]{1,0:T(8,128)(2,1)S(1)}, u32[]{:S(2)}, u32[]{:S(2)}) collective-permute-start(bf16[256,256]{1,0:T(8,128)(2,1)S(1)} %get-tuple-element.68), channel_id=1, source_target_pairs={{0,14},{1,15},{2,12},{3,13},{4,10},{5,11},{6,8},{7,9},{8,6},{9,7},... | collective-permute-start | bytes 393224 | tf_op jit(solution)/shard_map/ppermute | solution.py:470
  21.6 9.2 %collective-permute-start.5 = (bf16[256,256]{1,0:T(8,128)(2,1)S(1)}, bf16[256,256]{1,0:T(8,128)(2,1)S(1)}, u32[]{:S(2)}, u32[]{:S(2)}) collective-permute-start(bf16[256,256]{1,0:T(8,128)(2,1)S(1)} %get-tuple-element.69), channel_id=1, source_target_pairs={{0,10},{1,11},{2,8},{3,9},{4,14},{5,15},{6,12},{7,13},{8,2},{9,3},... | collective-permute-start | bytes 393224 | tf_op jit(solution)/shard_map/ppermute | solution.py:470
  24.9 7.1 %collective-permute-start.6 = (bf16[256,256]{1,0:T(8,128)(2,1)S(1)}, bf16[256,256]{1,0:T(8,128)(2,1)S(1)}, u32[]{:S(2)}, u32[]{:S(2)}) collective-permute-start(bf16[256,256]{1,0:T(8,128)(2,1)S(1)} %get-tuple-element.70), channel_id=1, source_target_pairs={{0,6},{1,7},{2,4},{3,5},{4,2},{5,3},{6,0},{7,1},{8,14},{9,15},{10,... | collective-permute-start | bytes 393224 | tf_op jit(solution)/shard_map/ppermute | solution.py:470
  26.5 5.5 %collective-permute-start.7 = (bf16[256,256]{1,0:T(8,128)(2,1)S(1)}, bf16[256,256]{1,0:T(8,128)(2,1)S(1)}, u32[]{:S(2)}, u32[]{:S(2)}) collective-permute-start(bf16[256,256]{1,0:T(8,128)(2,1)S(1)} %get-tuple-element.71), channel_id=1, source_target_pairs={{0,2},{1,3},{2,0},{3,1},{4,6},{5,7},{6,4},{7,5},{8,10},{9,11},{10,... | collective-permute-start | bytes 393224 | tf_op jit(solution)/shard_map/ppermute | solution.py:470
  43.5 2.4 %collective-permute-start.8 = (bf16[1552,256]{1,0:T(8,128)(2,1)S(1)}, bf16[1552,256]{1,0:T(8,128)(2,1)S(1)}, u32[]{:S(2)}, u32[]{:S(2)}) collective-permute-start(bf16[1552,256]{1,0:T(8,128)(2,1)S(1)} %get-tuple-element.74), channel_id=1, source_target_pairs={{0,2},{1,3},{2,0},{3,1},{4,6},{5,7},{6,4},{7,5},{8,10},{9,11},{10,... | collective-permute-start | bytes 2383880 | tf_op jit(solution)/shard_map/ppermute | solution.py:470
  44.6 3.6 %collective-permute-start.12 = (bf16[4,256,256]{2,1,0:T(8,128)(2,1)S(1)}, bf16[4,256,256]{2,1,0:T(8,128)(2,1)S(1)}, u32[]{:S(2)}, u32[]{:S(2)}) collective-permute-start(bf16[4,256,256]{2,1,0:T(8,128)(2,1)S(1)} %get-tuple-element.82), channel_id=1, source_target_pairs={{0,2},{1,3},{2,0},{3,1},{4,6},{5,7},{6,4},{7,5},{8,10},{9,11},{10,... | collective-permute-start | bytes 1572872 | tf_op jit(solution)/shard_map/ppermute | solution.py:470
  46.6 8.0 %collective-permute-start.9 = (bf16[400,256]{1,0:T(8,128)(2,1)S(1)}, bf16[400,256]{1,0:T(8,128)(2,1)S(1)}, u32[]{:S(2)}, u32[]{:S(2)}) collective-permute-start(bf16[400,256]{1,0:T(8,128)(2,1)S(1)} %get-tuple-element.77), channel_id=1, source_target_pairs={{0,1},{1,0},{2,3},{3,2},{4,5},{5,4},{6,7},{7,6},{8,9},{9,8},{10,11... | collective-permute-start | bytes 614408 | tf_op jit(solution)/shard_map/ppermute | solution.py:470
  48.2 19.1 %collective-permute-start.13 = (bf16[2,256,256]{2,1,0:T(8,128)(2,1)S(1)}, bf16[2,256,256]{2,1,0:T(8,128)(2,1)S(1)}, u32[]{:S(2)}, u32[]{:S(2)}) collective-permute-start(bf16[2,256,256]{2,1,0:T(8,128)(2,1)S(1)} %get-tuple-element.83), channel_id=1, source_target_pairs={{0,8},{1,9},{2,10},{3,11},{4,12},{5,13},{6,14},{7,15},{8,0},{9,1},... | collective-permute-start | bytes 786440 | tf_op jit(solution)/shard_map/ppermute | solution.py:470
  49.4 18.0 %collective-permute-start.10 = (bf16[400,256]{1,0:T(8,128)(2,1)S(1)}, bf16[400,256]{1,0:T(8,128)(2,1)S(1)}, u32[]{:S(2)}, u32[]{:S(2)}) collective-permute-start(bf16[400,256]{1,0:T(8,128)(2,1)S(1)} %get-tuple-element.78), channel_id=1, source_target_pairs={{0,4},{1,5},{2,6},{3,7},{4,0},{5,1},{6,2},{7,3},{8,12},{9,13},{10,... | collective-permute-start | bytes 614408 | tf_op jit(solution)/shard_map/ppermute | solution.py:470
  50.9 16.5 %collective-permute-start.11 = (bf16[400,256]{1,0:T(8,128)(2,1)S(1)}, bf16[400,256]{1,0:T(8,128)(2,1)S(1)}, u32[]{:S(2)}, u32[]{:S(2)}) collective-permute-start(bf16[400,256]{1,0:T(8,128)(2,1)S(1)} %get-tuple-element.79), channel_id=1, source_target_pairs={{0,5},{1,4},{2,7},{3,6},{4,1},{5,0},{6,3},{7,2},{8,13},{9,12},{10,... | collective-permute-start | bytes 614408 | tf_op jit(solution)/shard_map/ppermute | solution.py:470
  51.4 26.9 %collective-permute-start.27 = (bf16[2,256,256]{2,1,0:T(8,128)(2,1)S(1)}, bf16[2,256,256]{2,1,0:T(8,128)(2,1)S(1)}, u32[]{:S(2)}, u32[]{:S(2)}) collective-permute-start(bf16[2,256,256]{2,1,0:T(8,128)(2,1)S(1)} %get-tuple-element.94), channel_id=1, source_target_pairs={{0,4},{1,5},{2,6},{3,7},{4,0},{5,1},{6,2},{7,3},{8,12},{9,13},{10,... | collective-permute-start | bytes 786440 | tf_op jit(solution)/shard_map/ppermute | solution.py:470
  54.6 23.7 %collective-permute-start.28 = (bf16[2,256,256]{2,1,0:T(8,128)(2,1)S(1)}, bf16[2,256,256]{2,1,0:T(8,128)(2,1)S(1)}, u32[]{:S(2)}, u32[]{:S(2)}) collective-permute-start(bf16[2,256,256]{2,1,0:T(8,128)(2,1)S(1)} %get-tuple-element.95), channel_id=1, source_target_pairs={{0,12},{1,13},{2,14},{3,15},{4,8},{5,9},{6,10},{7,11},{8,4},{9,5},... | collective-permute-start | bytes 786440 | tf_op jit(solution)/shard_map/ppermute | solution.py:470
  68.0 4.8 %collective-permute-start.14 = (bf16[112,256]{1,0:T(8,128)(2,1)S(1)}, bf16[112,256]{1,0:T(8,128)(2,1)S(1)}, u32[]{:S(2)}, u32[]{:S(2)}) collective-permute-start(bf16[112,256]{1,0:T(8,128)(2,1)S(1)} %get-tuple-element.86), channel_id=1, source_target_pairs={{0,8},{1,9},{2,10},{3,11},{4,12},{5,13},{6,14},{7,15},{8,0},{9,1},... | collective-permute-start | bytes 172040 | tf_op jit(solution)/shard_map/ppermute | solution.py:470
  69.1 5.1 %collective-permute-start.15 = (bf16[112,256]{1,0:T(8,128)(2,1)S(1)}, bf16[112,256]{1,0:T(8,128)(2,1)S(1)}, u32[]{:S(2)}, u32[]{:S(2)}) collective-permute-start(bf16[112,256]{1,0:T(8,128)(2,1)S(1)} %get-tuple-element.87), channel_id=1, source_target_pairs={{0,16},{1,17},{2,18},{3,19},{4,20},{5,21},{6,22},{7,23},{8,24},{9,... | collective-permute-start | bytes 172040 | tf_op jit(solution)/shard_map/ppermute | solution.py:470
  71.7 6.0 %collective-permute-start.16 = (bf16[112,256]{1,0:T(8,128)(2,1)S(1)}, bf16[112,256]{1,0:T(8,128)(2,1)S(1)}, u32[]{:S(2)}, u32[]{:S(2)}) collective-permute-start(bf16[112,256]{1,0:T(8,128)(2,1)S(1)} %get-tuple-element.88), channel_id=1, source_target_pairs={{0,24},{1,25},{2,26},{3,27},{4,28},{5,29},{6,30},{7,31},{8,16},{9,... | collective-permute-start | bytes 172040 | tf_op jit(solution)/shard_map/ppermute | solution.py:470
  79.7 11.1 %collective-permute-start.29 = (bf16[512,256]{1,0:T(8,128)(2,1)S(1)}, bf16[512,256]{1,0:T(8,128)(2,1)S(1)}, u32[]{:S(2)}, u32[]{:S(2)}) collective-permute-start(bf16[512,256]{1,0:T(8,128)(2,1)S(1)} %get-tuple-element.98), channel_id=1, source_target_pairs={{0,1},{1,0},{2,3},{3,2},{4,5},{5,4},{6,7},{7,6},{8,9},{9,8},{10,11... | collective-permute-start | bytes 786440 | tf_op jit(solution)/shard_map/ppermute | solution.py:470
  80.3 5.9 %collective-permute-start.19 = (bf16[96,256]{1,0:T(8,128)(2,1)S(1)}, bf16[96,256]{1,0:T(8,128)(2,1)S(1)}, u32[]{:S(2)}, u32[]{:S(2)}) collective-permute-start(bf16[96,256]{1,0:T(8,128)(2,1)S(1)} %get-tuple-element.89.refs_0_.after_ref), channel_id=1, source_target_pairs={{0,24},{1,25},{2,26},{3,27},{4,28},{5,29},{6,30},{7,31},{8,16},{9,... | collective-permute-start | bytes 147464 | tf_op jit(solution)/shard_map/ppermute | solution.py:470
  81.5 5.7 %collective-permute-start.18 = (bf16[96,256]{1,0:T(8,128)(2,1)S(1)}, bf16[96,256]{1,0:T(8,128)(2,1)S(1)}, u32[]{:S(2)}, u32[]{:S(2)}) collective-permute-start(bf16[96,256]{1,0:T(8,128)(2,1)S(1)} %get-tuple-element.89.refs_0_.after_ref), channel_id=1, source_target_pairs={{0,16},{1,17},{2,18},{3,19},{4,20},{5,21},{6,22},{7,23},{8,24},{9,... | collective-permute-start | bytes 147464 | tf_op jit(solution)/shard_map/ppermute | solution.py:470
  81.6 5.6 %collective-permute-start.17 = (bf16[96,256]{1,0:T(8,128)(2,1)S(1)}, bf16[96,256]{1,0:T(8,128)(2,1)S(1)}, u32[]{:S(2)}, u32[]{:S(2)}) collective-permute-start(bf16[96,256]{1,0:T(8,128)(2,1)S(1)} %get-tuple-element.89.refs_0_.after_ref), channel_id=1, source_target_pairs={{0,8},{1,9},{2,10},{3,11},{4,12},{5,13},{6,14},{7,15},{8,0},{9,1},... | collective-permute-start | bytes 147464 | tf_op jit(solution)/shard_map/ppermute | solution.py:470
  87.2 6.7 %collective-permute-start.24 = (bf16[384,256]{1,0:T(8,128)(2,1)S(1)}, bf16[384,256]{1,0:T(8,128)(2,1)S(1)}, u32[]{:S(2)}, u32[]{:S(2)}) collective-permute-start(bf16[384,256]{1,0:T(8,128)(2,1)S(1)} %line.1.refs_0_.after_ref), channel_id=1, source_target_pairs={{0,5},{1,4},{2,7},{3,6},{4,1},{5,0},{6,3},{7,2},{8,13},{9,12},{10,... | collective-permute-start | bytes 589832 | tf_op jit(solution)/shard_map/ppermute | solution.py:470
  89.6 6.4 %collective-permute-start.22 = (bf16[384,256]{1,0:T(8,128)(2,1)S(1)}, bf16[384,256]{1,0:T(8,128)(2,1)S(1)}, u32[]{:S(2)}, u32[]{:S(2)}) collective-permute-start(bf16[384,256]{1,0:T(8,128)(2,1)S(1)} %line.1.refs_0_.after_ref), channel_id=1, source_target_pairs={{0,4},{1,5},{2,6},{3,7},{4,0},{5,1},{6,2},{7,3},{8,12},{9,13},{10,... | collective-permute-start | bytes 589832 | tf_op jit(solution)/shard_map/ppermute | solution.py:470
  90.3 5.7 %collective-permute-start.20 = (bf16[384,256]{1,0:T(8,128)(2,1)S(1)}, bf16[384,256]{1,0:T(8,128)(2,1)S(1)}, u32[]{:S(2)}, u32[]{:S(2)}) collective-permute-start(bf16[384,256]{1,0:T(8,128)(2,1)S(1)} %line.1.refs_0_.after_ref), channel_id=1, source_target_pairs={{0,1},{1,0},{2,3},{3,2},{4,5},{5,4},{6,7},{7,6},{8,9},{9,8},{10,11... | collective-permute-start | bytes 589832 | tf_op jit(solution)/shard_map/ppermute | solution.py:470
  90.9 5.9 %collective-permute-start.30 = (bf16[256,256]{1,0:T(8,128)(2,1)S(1)}, bf16[256,256]{1,0:T(8,128)(2,1)S(1)}, u32[]{:S(2)}, u32[]{:S(2)}) collective-permute-start(bf16[256,256]{1,0:T(8,128)(2,1)S(1)} %get-tuple-element.100), channel_id=1, source_target_pairs={{0,16},{1,17},{2,18},{3,19},{4,20},{5,21},{6,22},{7,23},{8,24},{9,... | collective-permute-start | bytes 393224 | tf_op jit(solution)/shard_map/ppermute | solution.py:470
  92.2 6.2 %collective-permute-start.26 = (bf16[384,256]{1,0:T(8,128)(2,1)S(1)}, bf16[384,256]{1,0:T(8,128)(2,1)S(1)}, u32[]{:S(2)}, u32[]{:S(2)}) collective-permute-start(bf16[384,256]{1,0:T(8,128)(2,1)S(1)} %line.1.refs_0_.after_ref), channel_id=1, source_target_pairs={{0,2},{1,3},{2,0},{3,1},{4,6},{5,7},{6,4},{7,5},{8,10},{9,11},{10,... | collective-permute-start | bytes 589832 | tf_op jit(solution)/shard_map/ppermute | solution.py:470
  94.0 6.3 %collective-permute-start.25 = (bf16[384,256]{1,0:T(8,128)(2,1)S(1)}, bf16[384,256]{1,0:T(8,128)(2,1)S(1)}, u32[]{:S(2)}, u32[]{:S(2)}) collective-permute-start(bf16[384,256]{1,0:T(8,128)(2,1)S(1)} %collective-permute-done.24.refs_3_.after_ref), channel_id=1, source_target_pairs={{0,2},{1,3},{2,0},{3,1},{4,6},{5,7},{6,4},{7,5},{8,10},{9,11},{10,... | collective-permute-start | bytes 589832 | tf_op jit(solution)/shard_map/ppermute | solution.py:470
  96.0 4.3 %collective-permute-start.23 = (bf16[384,256]{1,0:T(8,128)(2,1)S(1)}, bf16[384,256]{1,0:T(8,128)(2,1)S(1)}, u32[]{:S(2)}, u32[]{:S(2)}) collective-permute-start(bf16[384,256]{1,0:T(8,128)(2,1)S(1)} %collective-permute-done.22.refs_2_), channel_id=1, source_target_pairs={{0,2},{1,3},{2,0},{3,1},{4,6},{5,7},{6,4},{7,5},{8,10},{9,11},{10,... | collective-permute-start | bytes 589832 | tf_op jit(solution)/shard_map/ppermute | solution.py:470
  96.0 4.3 %collective-permute-start.21 = (bf16[384,256]{1,0:T(8,128)(2,1)S(1)}, bf16[384,256]{1,0:T(8,128)(2,1)S(1)}, u32[]{:S(2)}, u32[]{:S(2)}) collective-permute-start(bf16[384,256]{1,0:T(8,128)(2,1)S(1)} %collective-permute-done.20.refs_1_), channel_id=1, source_target_pairs={{0,2},{1,3},{2,0},{3,1},{4,6},{5,7},{6,4},{7,5},{8,10},{9,11},{10,... | collective-permute-start | bytes 589832 | tf_op jit(solution)/shard_map/ppermute | solution.py:470
  96.8 5.2 %collective-permute-start.31 = (bf16[256,256]{1,0:T(8,128)(2,1)S(1)}, bf16[256,256]{1,0:T(8,128)(2,1)S(1)}, u32[]{:S(2)}, u32[]{:S(2)}) collective-permute-start(bf16[256,256]{1,0:T(8,128)(2,1)S(1)} %share.1.refs_0_), channel_id=1, source_target_pairs={{0,1},{1,0},{2,3},{3,2},{4,5},{5,4},{6,7},{7,6},{8,9},{9,8},{10,11... | collective-permute-start | bytes 393224 | tf_op jit(solution)/shard_map/ppermute | solution.py:470

commit v5 on v3

--- a/solution.py
+++ b/solution.py
@@ -142,6 +142,22 @@
                 messages[step - 1][side * share : (side + 1) * share, :] = value.astype(BF16)
 
 
+def weight_kernel(weight_hbm, rounded_ref, turned_ref, weight_s, sems):
+    layers, taps, width = weight_s.shape
+    copies = [
+        pltpu.make_async_copy(weight_hbm.at[layer], weight_s.at[layer], sems.at[layer])
+        for layer in range(layers)
+    ]
+    for copy in copies:
+        copy.start()
+    for layer in range(layers):
+        copies[layer].wait()
+        for start in range(0, taps, width):
+            value = weight_s[layer, start : start + width, :]
+            rounded_ref[layer, start : start + width, :] = value.astype(BF16)
+            turned_ref[layer, start : start + width, :] = jnp.transpose(value).astype(BF16)
+
+
 def gain_block(values):
     high = values.astype(BF16)
     low = (values - high.astype(F32)).astype(BF16)
@@ -155,16 +171,12 @@
 
 
 def stack_kernel(
-    place_ref, column_ref, weight_hbm, gain_hbm, upstream_hbm, *refs,
+    place_ref, column_ref, rounded_ref, turned_ref, gain_hbm, upstream_hbm, *refs,
 ):
-    arrived_refs, refs = refs[:-19], refs[-19:]
-    gain_ref, upstream_ref, weight_ref, sems = refs[15:]
+    arrived_refs, refs = refs[:-16], refs[-16:]
+    gain_ref, upstream_ref, sems = refs[13:]
     copies = [
         pltpu.make_async_copy(gain_hbm, gain_ref, sems.at[0]),
-        *(
-            pltpu.make_async_copy(weight_hbm.at[layer], weight_ref.at[layer], sems.at[2 + layer])
-            for layer in range(weight_ref.shape[0])
-        ),
         pltpu.make_async_copy(upstream_hbm, upstream_ref, sems.at[1]),
     ]
     for copy in copies:
@@ -173,8 +185,7 @@
     fetched_refs = [arrived_refs[order.index(step)] for step in range(len(order))]
     g_ref, keep_ref, sent_ref, block_ref = refs[:4]
     x_s, h_s, hidden_s, normed_s, inverse_s, slope_s, dconv_s, spread_s, dw_s = refs[4:13]
-    rounded_s, turned_s = refs[13:15]
-    layers, taps, width = weight_ref.shape
+    layers, taps, width = rounded_ref.shape
     shards, reach = 2 * len(fetched_refs), fetched_refs[0].shape[0] // 2
     tokens = column_ref.shape[0]
     batches = MB
@@ -227,11 +238,6 @@
     root = math.sqrt(2.0 / math.pi)
     for layer in range(layers):
         dilation = 2**layer
-        copies[1 + layer].wait()
-        for start in range(0, taps, width):
-            value = weight_ref[layer, start : start + width, :]
-            rounded_s[layer, start : start + width, :] = value.astype(BF16)
-            turned_s[layer, start : start + width, :] = jnp.transpose(value).astype(BF16)
 
         for seq in range(batches):
             for j in range(per):
@@ -243,7 +249,7 @@
                     ],
                     axis=1,
                 )
-                conv = dot(stacked, rounded_s[layer])
+                conv = dot(stacked, rounded_ref[layer])
                 square = conv * conv
                 curve = jnp.tanh(conv * (root + (0.044715 * root) * square))
                 half = 0.5 + 0.5 * curve
@@ -288,7 +294,7 @@
                     axis=1,
                 )
                 spread_s[layer % 2, at(seq, j), :] = spread
-                dhidden = dot(spread, turned_s[layer])
+                dhidden = dot(spread, turned_ref[layer])
                 normed = normed_s[layer, at(seq, j), :]
                 product = dhidden * normed
                 gain_row = gain_ref[layer : layer + 1, :]
@@ -513,6 +519,18 @@
     order = ordered(near)
     fetched = [swap(served[step], peers, step) if step else served[0] for step in order]
 
+    rounded, turned = pl.pallas_call(
+        weight_kernel,
+        out_shape=(shape(conv_weight.shape, BF16),) * 2,
+        in_specs=[ANY],
+        out_specs=(VMEM, VMEM),
+        scratch_shapes=[
+            pltpu.VMEM(conv_weight.shape, F32),
+            pltpu.SemaphoreType.DMA((layers,)),
+        ],
+        compiler_params=params(16),
+        name="weight",
+    )(held(conv_weight))
     tokens = MB * count
     half = rows // 2
     padded = tokens + MB * PAD
@@ -524,7 +542,7 @@
             shape((half + GROUP, width), BF16),
             shape((GROUP, width), BF16),
         ),
-        in_specs=[SMEM, VMEM, ANY, ANY, ANY] + [VMEM] * near,
+        in_specs=[SMEM, VMEM, VMEM, VMEM, ANY, ANY] + [VMEM] * near,
         out_specs=(VMEM,) * 4,
         scratch_shapes=[
             pltpu.VMEM((tokens, width), F32),
@@ -536,17 +554,14 @@
             pltpu.VMEM((2, padded, width), F32),
             pltpu.VMEM((2, tokens, taps), BF16),
             pltpu.VMEM((rows, width), F32),
-            pltpu.VMEM((layers, taps, width), BF16),
-            pltpu.VMEM((layers, taps, width), BF16),
             pltpu.VMEM((layers, width), F32),
             pltpu.VMEM((tokens, width), BF16),
-            pltpu.VMEM((layers, taps, width), F32),
-            pltpu.SemaphoreType.DMA((2 + layers,)),
+            pltpu.SemaphoreType.DMA((2,)),
         ],
-        compiler_params=params(40),
+        compiler_params=params(36),
         name="stack",
     )(
-        place, codes.reshape(tokens, 1), held(conv_weight), held(gain),
+        place, codes.reshape(tokens, 1), rounded, turned, held(gain),
         held(upstream.reshape(tokens, width)),
         *fetched,
     )

time: 104 us -> 103 us (level)
  waiting for transfers between devices: 33.1 us -> 31.1 us
  Pallas kernels: 23.9 us -> 25.5 us
    pallas_call x0 -> x1, Pallas kernels: none -> 2.07 us  [body(): pl.pallas_call(weight_kernel, out_shape=(shape(conv_weight.shape, BF16),)...]
    ppermute x32, waiting for transfers between devices: 33.1 us -> 31.1 us  [swap(): return lax.ppermute(value, axes, [(i, i ^ mask) for i in range(devices)])]
  transfers between devices with their start and end apart: 32 -> 32, of which waited for: 18 -> 16; matrix products, arithmetic and copies ran while one was open for 1% -> 1% of each run, Pallas kernels for 9% -> 11%
where the time goes in v5:
time: 103 us
  starting transfers between devices  36 us (35%)
  waiting for transfers between devices  31.1 us (30%)
  Pallas kernels  25.5 us (25%)
  blocking collectives  8.43 us (8%)
    ppermute x32, starting transfers between devices, swap(): return lax.ppermute(value, axes, [(i, i ^ mask) for i in range(devices)])  36 us
    ppermute x32, waiting for transfers between devices, swap(): return lax.ppermute(value, axes, [(i, i ^ mask) for i in range(devices)])  31.1 us
    pallas_call x1, Pallas kernels, body(): pl.pallas_call(stack_kernel, out_shape=(shape((tokens, width), BF16), sha...  11 us
    all_to_all x1, blocking collectives, exchange(): lax.all_to_all(value, 'emb', split_axis=0, concat_axis=0, axis_index_grou...  8.43 us
    pallas_call x2, Pallas kernels, body(): pl.pallas_call(functools.partial(finish_kernel, 2 ** len(stages[2]), scal...  3.49 us
    pallas_call x1, Pallas kernels, body(): pl.pallas_call(weight_kernel, out_shape=(shape(conv_weight.shape, BF16),)...  2.07 us
  transfers between devices with their start and end apart: 32, of which 16 were waited for; matrix products, arithmetic and copies ran while one was open for 1% of the time, Pallas kernels for 11%

profile of v5, /device:TPU:0, one launch (start us, length us, event | category | flops | bytes accessed | tf_op | source)
XLA Modules:
  0.0 102.9 jit_solution(3868716934192044479)
XLA Ops:
  0.6 4.1 %collective-permute-start = (bf16[512,256]{1,0:T(8,128)(2,1)}, bf16[512,256]{1,0:T(8,128)(2,1)S(1)}, u32[]{:S(2)}, u32[]{:S(2)}) collective-permute-start(bf16[512,256]{1,0:T(8,128)(2,1)} %table_hbm.1), channel_id=1, source_target_pairs={{0,16},{1,17},{2,18},{3,19},{4,20},{5,21},{6,22},{7,23},{8,24},{9,... | collective-permute-start | bytes 786440 | tf_op jit(solution)/shard_map/ppermute | solution.py:476
  4.8 0.7 bitcast_add_fusion.ids_ref
  5.5 1.5 %request.1 = (s32[8,256]{1,0:T(8,128)S(1)}, s32[2,512]{1,0:T(2,128)S(1)}, bf16[512,256]{1,0:T(8,128)(2,1)S(1)}) custom-call(s32[6]{0:T(128)S(1)} %stack.28.place_ref, s32[2,512]{1,0:T(2,128)S(1)} %bitcast_add_fusion.ids_ref, bf16[512,256]{1,0:T(8,128)(2,1)} %table_hbm.1), custom_call_target="tpu_custom_call" | custom-call | tf_op jit(solution)/shard_map/request/pallas_call | solution.py:489
  7.0 8.4 %all_to_all.11 = s32[8,1,256]{2,1,0:T(1,128)S(1)} all-to-all(s32[8,1,256]{2,1,0:T(1,128)S(1)} %copy.14), channel_id=1, replica_groups={{0,2,4,6,8,10,12,14},{16,18,20,22,24,26,28,30},{1,3,5,7,9,11,13,15},{17..., dimensions={0} | all-to-all | bytes 16384 | tf_op jit(solution)/shard_map/all_to_all | solution.py:482
  15.5 1.1 %near.1 = (s32[8,256]{1,0:T(8,128)S(1)}, bf16[128,256]{1,0:T(8,128)(2,1)S(1)}, bf16[128,256]{1,0:T(8,128)(2,1)S(1)}, bf16[128,256]{1,0:T(8,128)(2,1)S(1)}, bf16[...) custom-call(s32[6]{0:T(128)S(1)} %stack.28.place_ref, ...), custom_call_target="tpu_custom_call" | custom-call | tf_op jit(solution)/shard_map/near/pallas_call | solution.py:503
  17.0 0.6 far.1
  17.6 1.8 %collective-permute-start.1 = (bf16[256,256]{1,0:T(8,128)(2,1)S(1)}, bf16[256,256]{1,0:T(8,128)(2,1)S(1)}, u32[]{:S(2)}, u32[]{:S(2)}) collective-permute-start(bf16[256,256]{1,0:T(8,128)(2,1)S(1)} %get-tuple-element.69), channel_id=1, source_target_pairs={{0,12},{1,13},{2,14},{3,15},{4,8},{5,9},{6,10},{7,11},{8,4},{9,5},... | collective-permute-start | bytes 393224 | tf_op jit(solution)/shard_map/ppermute | solution.py:476
  19.3 1.3 %collective-permute-start.2 = (bf16[256,256]{1,0:T(8,128)(2,1)S(1)}, bf16[256,256]{1,0:T(8,128)(2,1)S(1)}, u32[]{:S(2)}, u32[]{:S(2)}) collective-permute-start(bf16[256,256]{1,0:T(8,128)(2,1)S(1)} %get-tuple-element.70), channel_id=1, source_target_pairs={{0,8},{1,9},{2,10},{3,11},{4,12},{5,13},{6,14},{7,15},{8,0},{9,1},... | collective-permute-start | bytes 393224 | tf_op jit(solution)/shard_map/ppermute | solution.py:476
  21.6 2.3 %collective-permute-start.5 = (bf16[256,256]{1,0:T(8,128)(2,1)S(1)}, bf16[256,256]{1,0:T(8,128)(2,1)S(1)}, u32[]{:S(2)}, u32[]{:S(2)}) collective-permute-start(bf16[256,256]{1,0:T(8,128)(2,1)S(1)} %get-tuple-element.73), channel_id=1, source_target_pairs={{0,10},{1,11},{2,8},{3,9},{4,14},{5,15},{6,12},{7,13},{8,2},{9,3},... | collective-permute-start | bytes 393224 | tf_op jit(solution)/shard_map/ppermute | solution.py:476
  23.9 1.1 %collective-permute-done.1.refs_1_ = bf16[256,256]{1,0:T(8,128)(2,1)S(1)} collective-permute-done((bf16[256,256]{1,0:T(8,128)(2,1)S(1)}, bf16[256,256]{1,0:T(8,128)(2,1)S(1)}, u32[]{:S(2)}, u32[]{:S(2)}) %collective-permute-start.1) | collective-permute-done | bytes 131104 | tf_op jit(solution)/shard_map/ppermute | solution.py:476
  24.9 1.6 %collective-permute-done.2.refs_2_ = bf16[256,256]{1,0:T(8,128)(2,1)S(1)} collective-permute-done((bf16[256,256]{1,0:T(8,128)(2,1)S(1)}, bf16[256,256]{1,0:T(8,128)(2,1)S(1)}, u32[]{:S(2)}, u32[]{:S(2)}) %collective-permute-start.2) | collective-permute-done | bytes 131104 | tf_op jit(solution)/shard_map/ppermute | solution.py:476
  26.8 2.1 %weight.1 = (bf16[4,768,256]{2,1,0:T(8,128)(2,1)S(1)}, bf16[4,768,256]{2,1,0:T(8,128)(2,1)S(1)}) custom-call(f32[4,768,256]{2,1,0:T(8,128)} %weight_hbm.1), custom_call_target="tpu_custom_call" | custom-call | tf_op jit(solution)/shard_map/weight/pallas_call | solution.py:522
  28.9 1.9 %collective-permute-done.5.refs_5_ = bf16[256,256]{1,0:T(8,128)(2,1)S(1)} collective-permute-done((bf16[256,256]{1,0:T(8,128)(2,1)S(1)}, bf16[256,256]{1,0:T(8,128)(2,1)S(1)}, u32[]{:S(2)}, u32[]{:S(2)}) %collective-permute-start.5) | collective-permute-done | bytes 131104 | tf_op jit(solution)/shard_map/ppermute | solution.py:476
  30.8 1.3 %collective-permute-done.6.refs_6_ = bf16[256,256]{1,0:T(8,128)(2,1)S(1)} collective-permute-done((bf16[256,256]{1,0:T(8,128)(2,1)S(1)}, bf16[256,256]{1,0:T(8,128)(2,1)S(1)}, u32[]{:S(2)}, u32[]{:S(2)}) %collective-permute-start.6) | collective-permute-done | bytes 131104 | tf_op jit(solution)/shard_map/ppermute | solution.py:476
  32.1 11.0 %stack.29 = (bf16[1024,256]{1,0:T(8,128)(2,1)S(1)}, bf16[1536,256]{1,0:T(8,128)(2,1)S(1)}, bf16[1552,256]{1,0:T(8,128)(2,1)S(1)}, bf16[16,256]{1,0:T(8,128)(2,1)S(1)}) custom-call(s32[6]{0:T(128)S(1)} %stack.28.place_ref, s32[1024,1]{1,0:T(8,128)S(1)} %bitcast.18, bf16[4,768,256]{2,1,0:T(8,128)(2,1)S(1)} %get-tuple-element.55.rounded_ref, ...), custom_call_target="tpu_custom_call" | custom-call | tf_op jit(solution)/shard_map/stack/pallas_call | solution.py:537
  43.1 0.9 place.1
  44.1 0.5 collective-permute-start.12
  44.6 0.8 collective-permute-done.8.refs_0_
  45.4 0.7 fold0.1
  46.1 1.6 %collective-permute-start.9 = (bf16[400,256]{1,0:T(8,128)(2,1)S(1)}, bf16[400,256]{1,0:T(8,128)(2,1)S(1)}, u32[]{:S(2)}, u32[]{:S(2)}) collective-permute-start(bf16[400,256]{1,0:T(8,128)(2,1)S(1)} %get-tuple-element.81), channel_id=1, source_target_pairs={{0,1},{1,0},{2,3},{3,2},{4,5},{5,4},{6,7},{7,6},{8,9},{9,8},{10,11... | collective-permute-start | bytes 614408 | tf_op jit(solution)/shard_map/ppermute | solution.py:476
  47.8 1.1 %collective-permute-start.13 = (bf16[2,256,256]{2,1,0:T(8,128)(2,1)S(1)}, bf16[2,256,256]{2,1,0:T(8,128)(2,1)S(1)}, u32[]{:S(2)}, u32[]{:S(2)}) collective-permute-start(bf16[2,256,256]{2,1,0:T(8,128)(2,1)S(1)} %get-tuple-element.87), channel_id=1, source_target_pairs={{0,8},{1,9},{2,10},{3,11},{4,12},{5,13},{6,14},{7,15},{8,0},{9,1},... | collective-permute-start | bytes 786440 | tf_op jit(solution)/shard_map/ppermute | solution.py:476
  48.9 1.5 %collective-permute-start.10 = (bf16[400,256]{1,0:T(8,128)(2,1)S(1)}, bf16[400,256]{1,0:T(8,128)(2,1)S(1)}, u32[]{:S(2)}, u32[]{:S(2)}) collective-permute-start(bf16[400,256]{1,0:T(8,128)(2,1)S(1)} %get-tuple-element.82), channel_id=1, source_target_pairs={{0,4},{1,5},{2,6},{3,7},{4,0},{5,1},{6,2},{7,3},{8,12},{9,13},{10,... | collective-permute-start | bytes 614408 | tf_op jit(solution)/shard_map/ppermute | solution.py:476
  50.9 1.5 %collective-permute-start.27 = (bf16[2,256,256]{2,1,0:T(8,128)(2,1)S(1)}, bf16[2,256,256]{2,1,0:T(8,128)(2,1)S(1)}, u32[]{:S(2)}, u32[]{:S(2)}) collective-permute-start(bf16[2,256,256]{2,1,0:T(8,128)(2,1)S(1)} %get-tuple-element.98), channel_id=1, source_target_pairs={{0,4},{1,5},{2,6},{3,7},{4,0},{5,1},{6,2},{7,3},{8,12},{9,13},{10,... | collective-permute-start | bytes 786440 | tf_op jit(solution)/shard_map/ppermute | solution.py:476
  52.4 1.7 %collective-permute-done.9.refs_0_ = bf16[400,256]{1,0:T(8,128)(2,1)S(1)} collective-permute-done((bf16[400,256]{1,0:T(8,128)(2,1)S(1)}, bf16[400,256]{1,0:T(8,128)(2,1)S(1)}, u32[]{:S(2)}, u32[]{:S(2)}) %collective-permute-start.9) | collective-permute-done | bytes 204832 | tf_op jit(solution)/shard_map/ppermute | solution.py:476
  54.1 2.0 %collective-permute-start.28 = (bf16[2,256,256]{2,1,0:T(8,128)(2,1)S(1)}, bf16[2,256,256]{2,1,0:T(8,128)(2,1)S(1)}, u32[]{:S(2)}, u32[]{:S(2)}) collective-permute-start(bf16[2,256,256]{2,1,0:T(8,128)(2,1)S(1)} %get-tuple-element.99), channel_id=1, source_target_pairs={{0,12},{1,13},{2,14},{3,15},{4,8},{5,9},{6,10},{7,11},{8,4},{9,5},... | collective-permute-start | bytes 786440 | tf_op jit(solution)/shard_map/ppermute | solution.py:476
  56.1 10.8 %collective-permute-done.10.refs_1_ = bf16[400,256]{1,0:T(8,128)(2,1)S(1)} collective-permute-done((bf16[400,256]{1,0:T(8,128)(2,1)S(1)}, bf16[400,256]{1,0:T(8,128)(2,1)S(1)}, u32[]{:S(2)}, u32[]{:S(2)}) %collective-permute-start.10) | collective-permute-done | bytes 204832 | tf_op jit(solution)/shard_map/ppermute | solution.py:476
  66.9 0.6 fold1.1
  67.6 1.0 %collective-permute-start.14 = (bf16[112,256]{1,0:T(8,128)(2,1)S(1)}, bf16[112,256]{1,0:T(8,128)(2,1)S(1)}, u32[]{:S(2)}, u32[]{:S(2)}) collective-permute-start(bf16[112,256]{1,0:T(8,128)(2,1)S(1)} %get-tuple-element.90), channel_id=1, source_target_pairs={{0,8},{1,9},{2,10},{3,11},{4,12},{5,13},{6,14},{7,15},{8,0},{9,1},... | collective-permute-start | bytes 172040 | tf_op jit(solution)/shard_map/ppermute | solution.py:476
  68.6 2.6 %collective-permute-start.15 = (bf16[112,256]{1,0:T(8,128)(2,1)S(1)}, bf16[112,256]{1,0:T(8,128)(2,1)S(1)}, u32[]{:S(2)}, u32[]{:S(2)}) collective-permute-start(bf16[112,256]{1,0:T(8,128)(2,1)S(1)} %get-tuple-element.91), channel_id=1, source_target_pairs={{0,16},{1,17},{2,18},{3,19},{4,20},{5,21},{6,22},{7,23},{8,24},{9,... | collective-permute-start | bytes 172040 | tf_op jit(solution)/shard_map/ppermute | solution.py:476
  71.2 1.1 %collective-permute-start.16 = (bf16[112,256]{1,0:T(8,128)(2,1)S(1)}, bf16[112,256]{1,0:T(8,128)(2,1)S(1)}, u32[]{:S(2)}, u32[]{:S(2)}) collective-permute-start(bf16[112,256]{1,0:T(8,128)(2,1)S(1)} %get-tuple-element.92), channel_id=1, source_target_pairs={{0,24},{1,25},{2,26},{3,27},{4,28},{5,29},{6,30},{7,31},{8,16},{9,... | collective-permute-start | bytes 172040 | tf_op jit(solution)/shard_map/ppermute | solution.py:476
  72.4 1.3 %collective-permute-done.15.refs_1_ = bf16[112,256]{1,0:T(8,128)(2,1)S(1)} collective-permute-done((bf16[112,256]{1,0:T(8,128)(2,1)S(1)}, bf16[112,256]{1,0:T(8,128)(2,1)S(1)}, u32[]{:S(2)}, u32[]{:S(2)}) %collective-permute-start.15) | collective-permute-done | bytes 57376 | tf_op jit(solution)/shard_map/ppermute | solution.py:476
  73.7 3.5 %collective-permute-done.16.refs_2_ = bf16[112,256]{1,0:T(8,128)(2,1)S(1)} collective-permute-done((bf16[112,256]{1,0:T(8,128)(2,1)S(1)}, bf16[112,256]{1,0:T(8,128)(2,1)S(1)}, u32[]{:S(2)}, u32[]{:S(2)}) %collective-permute-start.16) | collective-permute-done | bytes 57376 | tf_op jit(solution)/shard_map/ppermute | solution.py:476
  77.2 0.6 last.1
  77.8 1.3 %collect.1 = (f32[256,256]{1,0:T(8,128)S(1)}, f32[256,256]{1,0:T(8,128)S(1)}, bf16[512,256]{1,0:T(8,128)(2,1)S(1)}) custom-call(s32[6]{0:T(128)S(1)} %stack.28.place_ref, s32[8,256]{1,0:T(8,128)S(1)} %get-tuple-element.59.asked_ref, bf16[96,256]{1,0:T(8,128)(2,1)S(1)} %get-tuple-element.93.refs_0_.after_ref, ...), custom_call_target="tpu_custom_call" | custom-call | tf_op jit(solution)/shard_map/collect/pallas_call | solution.py:622
  79.2 0.6 collective-permute-start.29
  79.8 1.2 %collective-permute-start.19 = (bf16[96,256]{1,0:T(8,128)(2,1)S(1)}, bf16[96,256]{1,0:T(8,128)(2,1)S(1)}, u32[]{:S(2)}, u32[]{:S(2)}) collective-permute-start(bf16[96,256]{1,0:T(8,128)(2,1)S(1)} %get-tuple-element.93.refs_0_.after_ref), channel_id=1, source_target_pairs={{0,24},{1,25},{2,26},{3,27},{4,28},{5,29},{6,30},{7,31},{8,16},{9,... | collective-permute-start | bytes 147464 | tf_op jit(solution)/shard_map/ppermute | solution.py:476
  81.1 3.0 %collective-permute-start.17 = (bf16[96,256]{1,0:T(8,128)(2,1)S(1)}, bf16[96,256]{1,0:T(8,128)(2,1)S(1)}, u32[]{:S(2)}, u32[]{:S(2)}) collective-permute-start(bf16[96,256]{1,0:T(8,128)(2,1)S(1)} %get-tuple-element.93.refs_0_.after_ref), channel_id=1, source_target_pairs={{0,8},{1,9},{2,10},{3,11},{4,12},{5,13},{6,14},{7,15},{8,0},{9,1},... | collective-permute-start | bytes 147464 | tf_op jit(solution)/shard_map/ppermute | solution.py:476
  84.2 1.5 %collective-permute-done.19.refs_3_ = bf16[96,256]{1,0:T(8,128)(2,1)S(1)} collective-permute-done((bf16[96,256]{1,0:T(8,128)(2,1)S(1)}, bf16[96,256]{1,0:T(8,128)(2,1)S(1)}, u32[]{:S(2)}, u32[]{:S(2)}) %collective-permute-start.19) | collective-permute-done | bytes 49184 | tf_op jit(solution)/shard_map/ppermute | solution.py:476
  85.7 1.1 %collective-permute-done.18.refs_2_ = bf16[96,256]{1,0:T(8,128)(2,1)S(1)} collective-permute-done((bf16[96,256]{1,0:T(8,128)(2,1)S(1)}, bf16[96,256]{1,0:T(8,128)(2,1)S(1)}, u32[]{:S(2)}, u32[]{:S(2)}) %collective-permute-start.18) | collective-permute-done | bytes 49184 | tf_op jit(solution)/shard_map/ppermute | solution.py:476
  86.8 2.3 %collective-permute-start.24 = (bf16[384,256]{1,0:T(8,128)(2,1)S(1)}, bf16[384,256]{1,0:T(8,128)(2,1)S(1)}, u32[]{:S(2)}, u32[]{:S(2)}) collective-permute-start(bf16[384,256]{1,0:T(8,128)(2,1)S(1)} %line.1.refs_0_.after_ref), channel_id=1, source_target_pairs={{0,5},{1,4},{2,7},{3,6},{4,1},{5,0},{6,3},{7,2},{8,13},{9,12},{10,... | collective-permute-start | bytes 589832 | tf_op jit(solution)/shard_map/ppermute | solution.py:476
  89.1 0.7 collective-permute-start.22
  90.4 1.4 %collective-permute-start.30 = (bf16[256,256]{1,0:T(8,128)(2,1)S(1)}, bf16[256,256]{1,0:T(8,128)(2,1)S(1)}, u32[]{:S(2)}, u32[]{:S(2)}) collective-permute-start(bf16[256,256]{1,0:T(8,128)(2,1)S(1)} %get-tuple-element.104), channel_id=1, source_target_pairs={{0,16},{1,17},{2,18},{3,19},{4,20},{5,21},{6,22},{7,23},{8,24},{9,... | collective-permute-start | bytes 393224 | tf_op jit(solution)/shard_map/ppermute | solution.py:476
  91.7 1.7 %collective-permute-done.24.refs_3_.after_ref = bf16[384,256]{1,0:T(8,128)(2,1)S(1)} collective-permute-done((bf16[384,256]{1,0:T(8,128)(2,1)S(1)}, bf16[384,256]{1,0:T(8,128)(2,1)S(1)}, u32[]{:S(2)}, u32[]{:S(2)}) %collective-permute-start.24) | collective-permute-done | bytes 196640 | tf_op jit(solution)/shard_map/ppermute | solution.py:476
  93.5 2.0 %collective-permute-done.22.refs_2_ = bf16[384,256]{1,0:T(8,128)(2,1)S(1)} collective-permute-done((bf16[384,256]{1,0:T(8,128)(2,1)S(1)}, bf16[384,256]{1,0:T(8,128)(2,1)S(1)}, u32[]{:S(2)}, u32[]{:S(2)}) %collective-permute-start.22) | collective-permute-done | bytes 196640 | tf_op jit(solution)/shard_map/ppermute | solution.py:476
  96.3 1.6 %collective-permute-start.31 = (bf16[256,256]{1,0:T(8,128)(2,1)S(1)}, bf16[256,256]{1,0:T(8,128)(2,1)S(1)}, u32[]{:S(2)}, u32[]{:S(2)}) collective-permute-start(bf16[256,256]{1,0:T(8,128)(2,1)S(1)} %share.1.refs_0_), channel_id=1, source_target_pairs={{0,1},{1,0},{2,3},{3,2},{4,5},{5,4},{6,7},{7,6},{8,9},{9,8},{10,11... | collective-permute-start | bytes 393224 | tf_op jit(solution)/shard_map/ppermute | solution.py:476
  97.9 1.9 %finish0.1.refs_3_ = f32[3072,256]{1,0:T(8,128)} custom-call(s32[6]{0:T(128)S(1)} %stack.28.place_ref, bf16[384,256]{1,0:T(8,128)(2,1)S(1)} %line.1.refs_0_.after_ref, bf16[384,256]{1,0:T(8,128)(2,1)S(1)} %collective-permute-done.20.refs_1_, bf16[384,256]{1,0:T(8,128)(2,1)S(1)} %collective-permute-done.22.refs_2_, ...), custom_call_target="tpu_custom_call" | custom-call | tf_op jit(solution)/shard_map/finish0/pallas_call | solution.py:668
  99.8 1.6 %finish1.1 = (f32[3072,256]{1,0:T(8,128)}, f32[8,128]{1,0:T(8,128)S(1)}) custom-call(s32[6]{0:T(128)S(1)} %stack.28.place_ref, bf16[384,256]{1,0:T(8,128)(2,1)S(1)} %collective-permute-done.21.refs_0_, bf16[384,256]{1,0:T(8,128)(2,1)S(1)} %collective-permute-done.23.refs_1_, ...), custom_call_target="tpu_custom_call", output_to_operand_aliasing={{0}: (4, {})} | custom-call | tf_op jit(solution)/shard_map/finish1/pallas_call | solution.py:668
  101.5 1.4 %table.1 = f32[512,256]{1,0:T(8,128)} custom-call(s32[6]{0:T(128)S(1)} %stack.28.place_ref, f32[8,128]{1,0:T(8,128)S(1)} %get-tuple-element.96.after_ref, bf16[256,256]{1,0:T(8,128)(2,1)S(1)} %share.1.refs_0_, bf16[256,256]{1,0:T(8,128)(2,1)S(1)} %collective-permute-done.31.refs_1_), custom_call_target="tpu_custom_call" | custom-call | tf_op jit(solution)/shard_map/table/pallas_call | solution.py:682
  (40 shorter events, 3.9 us)
Async XLA Ops:
  0.6 16.3 %collective-permute-start = (bf16[512,256]{1,0:T(8,128)(2,1)}, bf16[512,256]{1,0:T(8,128)(2,1)S(1)}, u32[]{:S(2)}, u32[]{:S(2)}) collective-permute-start(bf16[512,256]{1,0:T(8,128)(2,1)} %table_hbm.1), channel_id=1, source_target_pairs={{0,16},{1,17},{2,18},{3,19},{4,20},{5,21},{6,22},{7,23},{8,24},{9,... | collective-permute-start | bytes 786440 | tf_op jit(solution)/shard_map/ppermute | solution.py:476
  17.6 7.4 %collective-permute-start.1 = (bf16[256,256]{1,0:T(8,128)(2,1)S(1)}, bf16[256,256]{1,0:T(8,128)(2,1)S(1)}, u32[]{:S(2)}, u32[]{:S(2)}) collective-permute-start(bf16[256,256]{1,0:T(8,128)(2,1)S(1)} %get-tuple-element.69), channel_id=1, source_target_pairs={{0,12},{1,13},{2,14},{3,15},{4,8},{5,9},{6,10},{7,11},{8,4},{9,5},... | collective-permute-start | bytes 393224 | tf_op jit(solution)/shard_map/ppermute | solution.py:476
  19.3 7.2 %collective-permute-start.2 = (bf16[256,256]{1,0:T(8,128)(2,1)S(1)}, bf16[256,256]{1,0:T(8,128)(2,1)S(1)}, u32[]{:S(2)}, u32[]{:S(2)}) collective-permute-start(bf16[256,256]{1,0:T(8,128)(2,1)S(1)} %get-tuple-element.70), channel_id=1, source_target_pairs={{0,8},{1,9},{2,10},{3,11},{4,12},{5,13},{6,14},{7,15},{8,0},{9,1},... | collective-permute-start | bytes 393224 | tf_op jit(solution)/shard_map/ppermute | solution.py:476
  20.7 8.2 %collective-permute-start.3 = (bf16[256,256]{1,0:T(8,128)(2,1)S(1)}, bf16[256,256]{1,0:T(8,128)(2,1)S(1)}, u32[]{:S(2)}, u32[]{:S(2)}) collective-permute-start(bf16[256,256]{1,0:T(8,128)(2,1)S(1)} %get-tuple-element.71), channel_id=1, source_target_pairs={{0,4},{1,5},{2,6},{3,7},{4,0},{5,1},{6,2},{7,3},{8,12},{9,13},{10,... | collective-permute-start | bytes 393224 | tf_op jit(solution)/shard_map/ppermute | solution.py:476
  21.1 7.8 %collective-permute-start.4 = (bf16[256,256]{1,0:T(8,128)(2,1)S(1)}, bf16[256,256]{1,0:T(8,128)(2,1)S(1)}, u32[]{:S(2)}, u32[]{:S(2)}) collective-permute-start(bf16[256,256]{1,0:T(8,128)(2,1)S(1)} %get-tuple-element.72), channel_id=1, source_target_pairs={{0,14},{1,15},{2,12},{3,13},{4,10},{5,11},{6,8},{7,9},{8,6},{9,7},... | collective-permute-start | bytes 393224 | tf_op jit(solution)/shard_map/ppermute | solution.py:476
  21.6 9.2 %collective-permute-start.5 = (bf16[256,256]{1,0:T(8,128)(2,1)S(1)}, bf16[256,256]{1,0:T(8,128)(2,1)S(1)}, u32[]{:S(2)}, u32[]{:S(2)}) collective-permute-start(bf16[256,256]{1,0:T(8,128)(2,1)S(1)} %get-tuple-element.73), channel_id=1, source_target_pairs={{0,10},{1,11},{2,8},{3,9},{4,14},{5,15},{6,12},{7,13},{8,2},{9,3},... | collective-permute-start | bytes 393224 | tf_op jit(solution)/shard_map/ppermute | solution.py:476
  24.9 7.1 %collective-permute-start.6 = (bf16[256,256]{1,0:T(8,128)(2,1)S(1)}, bf16[256,256]{1,0:T(8,128)(2,1)S(1)}, u32[]{:S(2)}, u32[]{:S(2)}) collective-permute-start(bf16[256,256]{1,0:T(8,128)(2,1)S(1)} %get-tuple-element.74), channel_id=1, source_target_pairs={{0,6},{1,7},{2,4},{3,5},{4,2},{5,3},{6,0},{7,1},{8,14},{9,15},{10,... | collective-permute-start | bytes 393224 | tf_op jit(solution)/shard_map/ppermute | solution.py:476
  26.5 5.5 %collective-permute-start.7 = (bf16[256,256]{1,0:T(8,128)(2,1)S(1)}, bf16[256,256]{1,0:T(8,128)(2,1)S(1)}, u32[]{:S(2)}, u32[]{:S(2)}) collective-permute-start(bf16[256,256]{1,0:T(8,128)(2,1)S(1)} %get-tuple-element.75), channel_id=1, source_target_pairs={{0,2},{1,3},{2,0},{3,1},{4,6},{5,7},{6,4},{7,5},{8,10},{9,11},{10,... | collective-permute-start | bytes 393224 | tf_op jit(solution)/shard_map/ppermute | solution.py:476
  43.0 2.4 %collective-permute-start.8 = (bf16[1552,256]{1,0:T(8,128)(2,1)S(1)}, bf16[1552,256]{1,0:T(8,128)(2,1)S(1)}, u32[]{:S(2)}, u32[]{:S(2)}) collective-permute-start(bf16[1552,256]{1,0:T(8,128)(2,1)S(1)} %get-tuple-element.78), channel_id=1, source_target_pairs={{0,2},{1,3},{2,0},{3,1},{4,6},{5,7},{6,4},{7,5},{8,10},{9,11},{10,... | collective-permute-start | bytes 2383880 | tf_op jit(solution)/shard_map/ppermute | solution.py:476
  44.1 3.6 %collective-permute-start.12 = (bf16[4,256,256]{2,1,0:T(8,128)(2,1)S(1)}, bf16[4,256,256]{2,1,0:T(8,128)(2,1)S(1)}, u32[]{:S(2)}, u32[]{:S(2)}) collective-permute-start(bf16[4,256,256]{2,1,0:T(8,128)(2,1)S(1)} %get-tuple-element.86), channel_id=1, source_target_pairs={{0,2},{1,3},{2,0},{3,1},{4,6},{5,7},{6,4},{7,5},{8,10},{9,11},{10,... | collective-permute-start | bytes 1572872 | tf_op jit(solution)/shard_map/ppermute | solution.py:476
  46.1 8.0 %collective-permute-start.9 = (bf16[400,256]{1,0:T(8,128)(2,1)S(1)}, bf16[400,256]{1,0:T(8,128)(2,1)S(1)}, u32[]{:S(2)}, u32[]{:S(2)}) collective-permute-start(bf16[400,256]{1,0:T(8,128)(2,1)S(1)} %get-tuple-element.81), channel_id=1, source_target_pairs={{0,1},{1,0},{2,3},{3,2},{4,5},{5,4},{6,7},{7,6},{8,9},{9,8},{10,11... | collective-permute-start | bytes 614408 | tf_op jit(solution)/shard_map/ppermute | solution.py:476
  47.8 19.1 %collective-permute-start.13 = (bf16[2,256,256]{2,1,0:T(8,128)(2,1)S(1)}, bf16[2,256,256]{2,1,0:T(8,128)(2,1)S(1)}, u32[]{:S(2)}, u32[]{:S(2)}) collective-permute-start(bf16[2,256,256]{2,1,0:T(8,128)(2,1)S(1)} %get-tuple-element.87), channel_id=1, source_target_pairs={{0,8},{1,9},{2,10},{3,11},{4,12},{5,13},{6,14},{7,15},{8,0},{9,1},... | collective-permute-start | bytes 786440 | tf_op jit(solution)/shard_map/ppermute | solution.py:476
  48.9 18.0 %collective-permute-start.10 = (bf16[400,256]{1,0:T(8,128)(2,1)S(1)}, bf16[400,256]{1,0:T(8,128)(2,1)S(1)}, u32[]{:S(2)}, u32[]{:S(2)}) collective-permute-start(bf16[400,256]{1,0:T(8,128)(2,1)S(1)} %get-tuple-element.82), channel_id=1, source_target_pairs={{0,4},{1,5},{2,6},{3,7},{4,0},{5,1},{6,2},{7,3},{8,12},{9,13},{10,... | collective-permute-start | bytes 614408 | tf_op jit(solution)/shard_map/ppermute | solution.py:476
  50.4 16.5 %collective-permute-start.11 = (bf16[400,256]{1,0:T(8,128)(2,1)S(1)}, bf16[400,256]{1,0:T(8,128)(2,1)S(1)}, u32[]{:S(2)}, u32[]{:S(2)}) collective-permute-start(bf16[400,256]{1,0:T(8,128)(2,1)S(1)} %get-tuple-element.83), channel_id=1, source_target_pairs={{0,5},{1,4},{2,7},{3,6},{4,1},{5,0},{6,3},{7,2},{8,13},{9,12},{10,... | collective-permute-start | bytes 614408 | tf_op jit(solution)/shard_map/ppermute | solution.py:476
  50.9 26.9 %collective-permute-start.27 = (bf16[2,256,256]{2,1,0:T(8,128)(2,1)S(1)}, bf16[2,256,256]{2,1,0:T(8,128)(2,1)S(1)}, u32[]{:S(2)}, u32[]{:S(2)}) collective-permute-start(bf16[2,256,256]{2,1,0:T(8,128)(2,1)S(1)} %get-tuple-element.98), channel_id=1, source_target_pairs={{0,4},{1,5},{2,6},{3,7},{4,0},{5,1},{6,2},{7,3},{8,12},{9,13},{10,... | collective-permute-start | bytes 786440 | tf_op jit(solution)/shard_map/ppermute | solution.py:476
  54.1 23.7 %collective-permute-start.28 = (bf16[2,256,256]{2,1,0:T(8,128)(2,1)S(1)}, bf16[2,256,256]{2,1,0:T(8,128)(2,1)S(1)}, u32[]{:S(2)}, u32[]{:S(2)}) collective-permute-start(bf16[2,256,256]{2,1,0:T(8,128)(2,1)S(1)} %get-tuple-element.99), channel_id=1, source_target_pairs={{0,12},{1,13},{2,14},{3,15},{4,8},{5,9},{6,10},{7,11},{8,4},{9,5},... | collective-permute-start | bytes 786440 | tf_op jit(solution)/shard_map/ppermute | solution.py:476
  67.6 4.8 %collective-permute-start.14 = (bf16[112,256]{1,0:T(8,128)(2,1)S(1)}, bf16[112,256]{1,0:T(8,128)(2,1)S(1)}, u32[]{:S(2)}, u32[]{:S(2)}) collective-permute-start(bf16[112,256]{1,0:T(8,128)(2,1)S(1)} %get-tuple-element.90), channel_id=1, source_target_pairs={{0,8},{1,9},{2,10},{3,11},{4,12},{5,13},{6,14},{7,15},{8,0},{9,1},... | collective-permute-start | bytes 172040 | tf_op jit(solution)/shard_map/ppermute | solution.py:476
  68.6 5.1 %collective-permute-start.15 = (bf16[112,256]{1,0:T(8,128)(2,1)S(1)}, bf16[112,256]{1,0:T(8,128)(2,1)S(1)}, u32[]{:S(2)}, u32[]{:S(2)}) collective-permute-start(bf16[112,256]{1,0:T(8,128)(2,1)S(1)} %get-tuple-element.91), channel_id=1, source_target_pairs={{0,16},{1,17},{2,18},{3,19},{4,20},{5,21},{6,22},{7,23},{8,24},{9,... | collective-permute-start | bytes 172040 | tf_op jit(solution)/shard_map/ppermute | solution.py:476
  71.2 6.0 %collective-permute-start.16 = (bf16[112,256]{1,0:T(8,128)(2,1)S(1)}, bf16[112,256]{1,0:T(8,128)(2,1)S(1)}, u32[]{:S(2)}, u32[]{:S(2)}) collective-permute-start(bf16[112,256]{1,0:T(8,128)(2,1)S(1)} %get-tuple-element.92), channel_id=1, source_target_pairs={{0,24},{1,25},{2,26},{3,27},{4,28},{5,29},{6,30},{7,31},{8,16},{9,... | collective-permute-start | bytes 172040 | tf_op jit(solution)/shard_map/ppermute | solution.py:476
  79.2 11.1 %collective-permute-start.29 = (bf16[512,256]{1,0:T(8,128)(2,1)S(1)}, bf16[512,256]{1,0:T(8,128)(2,1)S(1)}, u32[]{:S(2)}, u32[]{:S(2)}) collective-permute-start(bf16[512,256]{1,0:T(8,128)(2,1)S(1)} %get-tuple-element.102), channel_id=1, source_target_pairs={{0,1},{1,0},{2,3},{3,2},{4,5},{5,4},{6,7},{7,6},{8,9},{9,8},{10,11... | collective-permute-start | bytes 786440 | tf_op jit(solution)/shard_map/ppermute | solution.py:476
  79.8 5.9 %collective-permute-start.19 = (bf16[96,256]{1,0:T(8,128)(2,1)S(1)}, bf16[96,256]{1,0:T(8,128)(2,1)S(1)}, u32[]{:S(2)}, u32[]{:S(2)}) collective-permute-start(bf16[96,256]{1,0:T(8,128)(2,1)S(1)} %get-tuple-element.93.refs_0_.after_ref), channel_id=1, source_target_pairs={{0,24},{1,25},{2,26},{3,27},{4,28},{5,29},{6,30},{7,31},{8,16},{9,... | collective-permute-start | bytes 147464 | tf_op jit(solution)/shard_map/ppermute | solution.py:476
  81.0 5.7 %collective-permute-start.18 = (bf16[96,256]{1,0:T(8,128)(2,1)S(1)}, bf16[96,256]{1,0:T(8,128)(2,1)S(1)}, u32[]{:S(2)}, u32[]{:S(2)}) collective-permute-start(bf16[96,256]{1,0:T(8,128)(2,1)S(1)} %get-tuple-element.93.refs_0_.after_ref), channel_id=1, source_target_pairs={{0,16},{1,17},{2,18},{3,19},{4,20},{5,21},{6,22},{7,23},{8,24},{9,... | collective-permute-start | bytes 147464 | tf_op jit(solution)/shard_map/ppermute | solution.py:476
  81.1 5.6 %collective-permute-start.17 = (bf16[96,256]{1,0:T(8,128)(2,1)S(1)}, bf16[96,256]{1,0:T(8,128)(2,1)S(1)}, u32[]{:S(2)}, u32[]{:S(2)}) collective-permute-start(bf16[96,256]{1,0:T(8,128)(2,1)S(1)} %get-tuple-element.93.refs_0_.after_ref), channel_id=1, source_target_pairs={{0,8},{1,9},{2,10},{3,11},{4,12},{5,13},{6,14},{7,15},{8,0},{9,1},... | collective-permute-start | bytes 147464 | tf_op jit(solution)/shard_map/ppermute | solution.py:476
  86.8 6.7 %collective-permute-start.24 = (bf16[384,256]{1,0:T(8,128)(2,1)S(1)}, bf16[384,256]{1,0:T(8,128)(2,1)S(1)}, u32[]{:S(2)}, u32[]{:S(2)}) collective-permute-start(bf16[384,256]{1,0:T(8,128)(2,1)S(1)} %line.1.refs_0_.after_ref), channel_id=1, source_target_pairs={{0,5},{1,4},{2,7},{3,6},{4,1},{5,0},{6,3},{7,2},{8,13},{9,12},{10,... | collective-permute-start | bytes 589832 | tf_op jit(solution)/shard_map/ppermute | solution.py:476
  89.1 6.4 %collective-permute-start.22 = (bf16[384,256]{1,0:T(8,128)(2,1)S(1)}, bf16[384,256]{1,0:T(8,128)(2,1)S(1)}, u32[]{:S(2)}, u32[]{:S(2)}) collective-permute-start(bf16[384,256]{1,0:T(8,128)(2,1)S(1)} %line.1.refs_0_.after_ref), channel_id=1, source_target_pairs={{0,4},{1,5},{2,6},{3,7},{4,0},{5,1},{6,2},{7,3},{8,12},{9,13},{10,... | collective-permute-start | bytes 589832 | tf_op jit(solution)/shard_map/ppermute | solution.py:476
  89.8 5.7 %collective-permute-start.20 = (bf16[384,256]{1,0:T(8,128)(2,1)S(1)}, bf16[384,256]{1,0:T(8,128)(2,1)S(1)}, u32[]{:S(2)}, u32[]{:S(2)}) collective-permute-start(bf16[384,256]{1,0:T(8,128)(2,1)S(1)} %line.1.refs_0_.after_ref), channel_id=1, source_target_pairs={{0,1},{1,0},{2,3},{3,2},{4,5},{5,4},{6,7},{7,6},{8,9},{9,8},{10,11... | collective-permute-start | bytes 589832 | tf_op jit(solution)/shard_map/ppermute | solution.py:476
  90.4 5.9 %collective-permute-start.30 = (bf16[256,256]{1,0:T(8,128)(2,1)S(1)}, bf16[256,256]{1,0:T(8,128)(2,1)S(1)}, u32[]{:S(2)}, u32[]{:S(2)}) collective-permute-start(bf16[256,256]{1,0:T(8,128)(2,1)S(1)} %get-tuple-element.104), channel_id=1, source_target_pairs={{0,16},{1,17},{2,18},{3,19},{4,20},{5,21},{6,22},{7,23},{8,24},{9,... | collective-permute-start | bytes 393224 | tf_op jit(solution)/shard_map/ppermute | solution.py:476
  91.7 6.2 %collective-permute-start.26 = (bf16[384,256]{1,0:T(8,128)(2,1)S(1)}, bf16[384,256]{1,0:T(8,128)(2,1)S(1)}, u32[]{:S(2)}, u32[]{:S(2)}) collective-permute-start(bf16[384,256]{1,0:T(8,128)(2,1)S(1)} %line.1.refs_0_.after_ref), channel_id=1, source_target_pairs={{0,2},{1,3},{2,0},{3,1},{4,6},{5,7},{6,4},{7,5},{8,10},{9,11},{10,... | collective-permute-start | bytes 589832 | tf_op jit(solution)/shard_map/ppermute | solution.py:476
  93.5 6.3 %collective-permute-start.25 = (bf16[384,256]{1,0:T(8,128)(2,1)S(1)}, bf16[384,256]{1,0:T(8,128)(2,1)S(1)}, u32[]{:S(2)}, u32[]{:S(2)}) collective-permute-start(bf16[384,256]{1,0:T(8,128)(2,1)S(1)} %collective-permute-done.24.refs_3_.after_ref), channel_id=1, source_target_pairs={{0,2},{1,3},{2,0},{3,1},{4,6},{5,7},{6,4},{7,5},{8,10},{9,11},{10,... | collective-permute-start | bytes 589832 | tf_op jit(solution)/shard_map/ppermute | solution.py:476
  95.5 4.3 %collective-permute-start.23 = (bf16[384,256]{1,0:T(8,128)(2,1)S(1)}, bf16[384,256]{1,0:T(8,128)(2,1)S(1)}, u32[]{:S(2)}, u32[]{:S(2)}) collective-permute-start(bf16[384,256]{1,0:T(8,128)(2,1)S(1)} %collective-permute-done.22.refs_2_), channel_id=1, source_target_pairs={{0,2},{1,3},{2,0},{3,1},{4,6},{5,7},{6,4},{7,5},{8,10},{9,11},{10,... | collective-permute-start | bytes 589832 | tf_op jit(solution)/shard_map/ppermute | solution.py:476
  95.5 4.3 %collective-permute-start.21 = (bf16[384,256]{1,0:T(8,128)(2,1)S(1)}, bf16[384,256]{1,0:T(8,128)(2,1)S(1)}, u32[]{:S(2)}, u32[]{:S(2)}) collective-permute-start(bf16[384,256]{1,0:T(8,128)(2,1)S(1)} %collective-permute-done.20.refs_1_), channel_id=1, source_target_pairs={{0,2},{1,3},{2,0},{3,1},{4,6},{5,7},{6,4},{7,5},{8,10},{9,11},{10,... | collective-permute-start | bytes 589832 | tf_op jit(solution)/shard_map/ppermute | solution.py:476
  96.3 5.2 %collective-permute-start.31 = (bf16[256,256]{1,0:T(8,128)(2,1)S(1)}, bf16[256,256]{1,0:T(8,128)(2,1)S(1)}, u32[]{:S(2)}, u32[]{:S(2)}) collective-permute-start(bf16[256,256]{1,0:T(8,128)(2,1)S(1)} %share.1.refs_0_), channel_id=1, source_target_pairs={{0,1},{1,0},{2,3},{3,2},{4,5},{5,4},{6,7},{7,6},{8,9},{9,8},{10,11... | collective-permute-start | bytes 393224 | tf_op jit(solution)/shard_map/ppermute | solution.py:476
